TPU v7x, 32 devices: a whole 2x2x4 slice. The times are simulated.
32 devices in a mesh: dp: 16 (over z, x, core), mp: 2 (over y).
Axes of the slice: x: 2, y: 2, z: 4, core: 2. Of those that a mesh axis runs over, the one named last changes fastest.
Arguments:
- normed_input_rows: bfloat16 [6144, 8192], P('dp', 'mp'), may hold values from -6 to 6
- frozen_queries: bfloat16 [6144, 8192], P('dp', 'mp'), may hold values from -6 to 6
- frozen_keys: bfloat16 [6144, 1024], P('dp', 'mp'), may hold values from -6 to 6
- frozen_values: bfloat16 [6144, 1024], P('dp', 'mp'), may hold values from -6 to 6
- attention_output_gradient: bfloat16 [6144, 8192], P('dp', 'mp'), may hold values from -1.1953125 to 1.1953125
- adapter_down_weight: float32 [64, 8192, 192], P(None, ('mp', 'dp')), may hold values from -0.0625 to 0.0625
- adapter_up_query: float32 [64, 64, 8192], P(None, 'dp', 'mp'), may hold values from -0.75 to 0.75
- adapter_up_key_value: float32 [64, 64, 8, 256], P(None, 'dp', 'mp'), may hold values from -0.75 to 0.75
- document_numbers: int32 [6144], P('dp'), may hold values from 0 to 383, as said below
- block_tenant_slot: int32 [48], P('dp'), may hold values from 0 to 1, as said below
- shard_tenant_table: int32 [16, 2], replicated, may hold values from 0 to 63, as said below
Outputs:
- grad_down: float32 [64, 8192, 192], P(None, ('mp', 'dp'))
- grad_upq: float32 [64, 64, 8192], P(None, 'dp', 'mp')
- grad_upkv: float32 [64, 64, 8, 256], P(None, 'dp', 'mp')
Inputs may be any that keep to these rules, and one draw needn't show every extreme that they name: `document_numbers`: document numbers never fall along the rows; a document starts only at a multiple of 16 rows, always at the first row of each index of dp, at the last 16 rows of all, and wherever the slot of a block changes; a document's number is its first row divided by 16. `block_tenant_slot`: the 3 blocks of each index of dp name slots in an order that never falls, and every one of the 2 slots is named. `shard_tenant_table`: each row holds 2 distinct tenants.
All inputs are finite; a program needn't handle non-finite values.
Results may differ from a plain program's by a relative error of at most 0.012.
The roundings to bfloat16 on the way count: a program that leaves them out, or rounds other values in their place, can miss the bound.
Values sent between devices are 32-bit elements; how exact they have to be, the bound alone decides.
No kernel may reach another device: no remote copies, remote signals or barrier semaphores. Data moves between devices by JAX's collectives and lax.ppermute only.
A program may use at most 192 MiB of HBM per device.

v0:
```python
import jax
import jax.numpy as jnp
from jax import lax
from jax.sharding import PartitionSpec as P

ADAPTER_SCALE = 0.5
MASKED = -1e30
PRECISION_HIGH = lax.Precision.HIGHEST


def attention_grads(query_row_block, key_row_block, value_row_block, upstream, doc_row):
    row_total = query_row_block.shape[0]
    kv_heads = key_row_block.shape[1]
    groups = query_row_block.shape[1] // kv_heads
    head_size = query_row_block.shape[2]
    query_g = query_row_block.reshape(row_total, kv_heads, groups, head_size)
    upstream_g = upstream.reshape(row_total, kv_heads, groups, head_size)
    inverse = 1.0 / head_size**0.5
    scores = (
        jnp.einsum("qkgd,jkd->kgqj", query_g, key_row_block, preferred_element_type=jnp.float32)
        * inverse
    )
    position = jnp.arange(row_total, dtype=jnp.int32)
    allowed = (doc_row[:, None] == doc_row[None, :]) & (position[:, None] >= position[None, :])
    scores = jnp.where(allowed, scores, MASKED)
    row_top = jnp.max(scores, axis=-1, keepdims=True)
    weights = jnp.exp(scores - row_top)
    attn_probs = weights / jnp.sum(weights, axis=-1, keepdims=True)
    probs_low = attn_probs.astype(jnp.bfloat16)
    grad_probs = jnp.einsum(
        "qkgd,jkd->kgqj", upstream_g, value_row_block, preferred_element_type=jnp.float32
    )
    row_inner = jnp.sum(attn_probs * grad_probs, axis=-1, keepdims=True)
    grad_scores = (attn_probs * (grad_probs - row_inner) * inverse).astype(jnp.bfloat16)
    grad_query = jnp.einsum(
        "kgqj,jkd->qkgd", grad_scores, key_row_block, preferred_element_type=jnp.float32
    ).reshape(row_total, -1)
    key_gradient = jnp.einsum(
        "kgqj,qkgd->jkd", grad_scores, query_g, preferred_element_type=jnp.float32
    ).reshape(row_total, -1)
    value_gradient = jnp.einsum(
        "kgqj,qkgd->jkd", probs_low, upstream_g, preferred_element_type=jnp.float32
    ).reshape(row_total, -1)
    return (grad_query, key_gradient, value_gradient)


def adapted(frozen_rows, low_part, panel_cols):
    extra_term = jnp.einsum("brk,bkc->brc", low_part, panel_cols, precision=PRECISION_HIGH)
    extra_term = extra_term.reshape(frozen_rows.shape[0], -1)
    return (frozen_rows.astype(jnp.float32) + ADAPTER_SCALE * extra_term).astype(jnp.bfloat16)


def on_device(
    normed_input_rows,
    frozen_queries,
    frozen_keys,
    frozen_values,
    attention_output_gradient,
    adapter_down_weight,
    adapter_up_query,
    adapter_up_key_value,
    document_numbers,
    block_tenant_slot,
    shard_tenant_table,
):
    row_count = normed_input_rows.shape[0]
    block_count = block_tenant_slot.shape[0]
    block_rows = row_count // block_count
    dp_count = lax.axis_size("dp")
    count_of_tenants = adapter_down_weight.shape[0]
    desired_result = shard_tenant_table.reshape(-1)
    down_panels, upq_panels, upkv_panels = (
        lax.all_to_all(
            adapter_down_weight[desired_result], "dp", split_axis=0, concat_axis=1, tiled=True
        ),
        lax.all_to_all(
            adapter_up_query[desired_result], "dp", split_axis=0, concat_axis=1, tiled=True
        ),
        lax.all_to_all(
            adapter_up_key_value[desired_result], "dp", split_axis=0, concat_axis=1, tiled=True
        ),
    )
    adapter_rank = down_panels.shape[2] // 3
    row_blocks = normed_input_rows.reshape(block_count, block_rows, -1).astype(jnp.float32)
    partial_down = jnp.einsum(
        "bri,bij->brj", row_blocks, down_panels[block_tenant_slot], precision=PRECISION_HIGH
    )
    lowrank = lax.psum(partial_down.reshape(row_count, 3 * adapter_rank), "mp")
    head_size = upkv_panels.shape[3] // 2
    kv_heads = upkv_panels.shape[2]
    query_heads = frozen_queries.shape[1] // head_size
    low_blocks = lowrank.reshape(block_count, block_rows, 3, adapter_rank)
    upq_blocks = upq_panels[block_tenant_slot]
    upkv_blocks = upkv_panels[block_tenant_slot]
    upk_blocks = upkv_blocks[..., :head_size].reshape(
        block_count, adapter_rank, kv_heads * head_size
    )
    upv_blocks = upkv_blocks[..., head_size:].reshape(
        block_count, adapter_rank, kv_heads * head_size
    )
    query_row_block = adapted(frozen_queries, low_blocks[:, :, 0], upq_blocks)
    key_row_block = adapted(frozen_keys, low_blocks[:, :, 1], upk_blocks)
    value_row_block = adapted(frozen_values, low_blocks[:, :, 2], upv_blocks)
    grad_query, key_gradient, value_gradient = attention_grads(
        query_row_block.reshape(row_count, query_heads, head_size),
        key_row_block.reshape(row_count, kv_heads, head_size),
        value_row_block.reshape(row_count, kv_heads, head_size),
        attention_output_gradient.reshape(row_count, query_heads, head_size),
        document_numbers,
    )
    gq_blocks = grad_query.reshape(block_count, block_rows, -1)
    gk_blocks = key_gradient.reshape(block_count, block_rows, -1)
    gv_blocks = value_gradient.reshape(block_count, block_rows, -1)
    gradient_portion = ADAPTER_SCALE * jnp.concatenate(
        [
            jnp.einsum("brc,bkc->brk", gq_blocks, upq_blocks, precision=PRECISION_HIGH),
            jnp.einsum("brc,bkc->brk", gk_blocks, upk_blocks, precision=PRECISION_HIGH),
            jnp.einsum("brc,bkc->brk", gv_blocks, upv_blocks, precision=PRECISION_HIGH),
        ],
        axis=-1,
    )
    lowrank_grad = lax.psum(gradient_portion.reshape(row_count, 3 * adapter_rank), "mp")
    lowrank_gradient = lowrank_grad.reshape(block_count, block_rows, 3 * adapter_rank)
    down_terms = jnp.einsum("bri,brj->bij", row_blocks, lowrank_gradient, precision=PRECISION_HIGH)
    query_up_terms = ADAPTER_SCALE * jnp.einsum(
        "brk,brc->bkc", low_blocks[:, :, 0], gq_blocks, precision=PRECISION_HIGH
    )
    key_up_terms = ADAPTER_SCALE * jnp.einsum(
        "brk,brc->bkc", low_blocks[:, :, 1], gk_blocks, precision=PRECISION_HIGH
    )
    value_up_terms = ADAPTER_SCALE * jnp.einsum(
        "brk,brc->bkc", low_blocks[:, :, 2], gv_blocks, precision=PRECISION_HIGH
    )
    upkv_terms = jnp.concatenate(
        [
            key_up_terms.reshape(block_count, adapter_rank, kv_heads, head_size),
            value_up_terms.reshape(block_count, adapter_rank, kv_heads, head_size),
        ],
        axis=-1,
    )
    all_slots = lax.all_gather(block_tenant_slot, "dp", axis=0, tiled=True)
    senders = jnp.arange(dp_count * block_count, dtype=jnp.int32) // block_count
    owners = shard_tenant_table[senders, all_slots]
    down_in, upq_in, upkv_in = (
        lax.all_to_all(down_terms, "dp", split_axis=1, concat_axis=0, tiled=True),
        lax.all_to_all(query_up_terms, "dp", split_axis=1, concat_axis=0, tiled=True),
        lax.all_to_all(upkv_terms, "dp", split_axis=1, concat_axis=0, tiled=True),
    )
    owner_hot = (jnp.arange(count_of_tenants, dtype=jnp.int32)[:, None] == owners[None, :]).astype(
        jnp.float32
    )
    grad_down = jnp.einsum("tj,jrc->trc", owner_hot, down_in, precision=PRECISION_HIGH)
    grad_upq = jnp.einsum("tj,jrc->trc", owner_hot, upq_in, precision=PRECISION_HIGH)
    grad_upkv = jnp.einsum("tj,jrkc->trkc", owner_hot, upkv_in, precision=PRECISION_HIGH)
    return (grad_down, grad_upq, grad_upkv)


def solution(mesh):
    placed = (
        P("dp", "mp"),
        P("dp", "mp"),
        P("dp", "mp"),
        P("dp", "mp"),
        P("dp", "mp"),
        P(None, ("mp", "dp"), None),
        P(None, "dp", "mp"),
        P(None, "dp", "mp", None),
        P("dp"),
        P("dp"),
        P(),
    )
    return jax.shard_map(
        on_device,
        mesh=mesh,
        in_specs=placed,
        out_specs=(P(None, ("mp", "dp"), None), P(None, "dp", "mp"), P(None, "dp", "mp", None)),
        check_vma=False,
    )
```

profile of v0, /device:TPU:1, one launch (start us, length us, event | category | flops | bytes accessed | tf_op | source)
XLA Modules:
  0.0 968.5 jit_solution(3892837181411767936)
XLA Ops:
  8.2 2.8 gather_fusion.3
  11.0 7.3 all-to-all-start.1
  18.4 8.2 gather_fusion.1
  26.6 6.0 all-to-all-done.1
  32.5 4.9 all-to-all-start
  37.4 5.2 gather_fusion.5
  42.7 109.4 %all-to-all-done = f32[32,256,192]{1,2,0:T(8,128)} async-done(((f32[32,256,192]{1,2,0:T(8,128)}), f32[32,256,192]{1,2,0:T(8,128)}, u32[]{:S(2)}, u32[]{:S(2)}) %all-to-all-start) | async-done | bytes 6291488 | tf_op jit(solution)/shard_map/all_to_all | solution.py:73
  152.1 27.7 %all-to-all-start.2 = ((f32[32,4,4096]{2,1,0:T(4,128)}), f32[32,4,4096]{2,1,0:T(4,128)}, u32[]{:S(2)}, u32[]{:S(2)}) async-start(f32[32,4,4096]{2,1,0:T(4,128)} %gather_fusion.5), calls=%async_computation.2 | async-start | bytes 4194304 | tf_op jit(solution)/shard_map/all_to_all | solution.py:76
  179.8 9.1 copy.209
  189.0 7.2 all_to_all.81
  196.2 7.7 gather_fusion.2
  203.8 7.5 fusion.54
  212.9 4.4 copy.187
  219.2 2.9 gather_fusion.4
  227.2 3.2 copy.134
  230.5 2.5 copy.135
  233.0 4.0 gather_fusion.6
  244.4 7.2 convolution_multiply_fusion
  255.3 9.9 %fusion.17 = f32[4,384,384,8]{2,1,3,0:T(8,128)} fusion(bf16[384,4,128,1]{0,2,3,1:T(8,128)(2,1)S(1)} %copy-done.6, bf16[384,4,8,128]{3,2,1,0:T(8,128)(2,1)S(1)} %bitcast.166), kind=kOutput, calls=%fused_computation.34 | convolution fusion | flops 1207959552 | bytes 22413312 | tf_op jit(solution)/shard_map/qkgd,jkd->kgqj/dot_general | solution.py:20
  265.2 24.1 %fusion.53 = (f32[4,8,384]{2,1,0:T(8,128)}, f32[4,8,384,384]{2,3,1,0:T(8,128)}) fusion(f32[4,384,384,8]{2,1,3,0:T(8,128)} %fusion.17, pred[384,384]{0,1:T(8,128)(4,1)} %fusion.31), kind=kOutput, calls=%fused_computation.95 | output fusion | flops 28311936 | bytes 37945344 | tf_op jit(solution)/shard_map/sub | solution.py:27
  289.3 11.0 %fusion.22 = f32[384,4,128]{2,0,1:T(8,128)} fusion(bf16[384,4,8,128]{3,2,1,0:T(8,128)(2,1)} %bitcast.171, f32[4,8,384,384]{2,3,1,0:T(8,128)} %get-tuple-element.21, f32[4,8,384]{2,1,0:T(8,128)} %get-tuple-element.20), kind=kOutput, calls=%fused_computation.43 | convolution fusion | flops 1217396736 | bytes 22855680 | tf_op jit(solution)/shard_map/kgqj,qkgd->jkd/dot_general | solution.py:41
  300.2 2.5 copy.148
  310.7 11.4 %fusion.20 = f32[4,384,384,8]{2,1,3,0:T(8,128)} fusion(bf16[384,4,8,128]{3,2,1,0:T(8,128)(2,1)} %bitcast.172, bf16[384,4,128,1]{2,1,0,3:T(4,128)(2,1)} %bitcast.178), kind=kOutput, calls=%fused_computation.37 | convolution fusion | flops 1207959552 | bytes 22413312 | tf_op jit(solution)/shard_map/qkgd,jkd->kgqj/dot_general | solution.py:30
  322.1 29.9 %fusion.4 = bf16[4,8,384,384]{2,3,1,0:T(8,128)(2,1)} fusion(f32[4,384,384,8]{2,1,3,0:T(8,128)} %fusion.20, f32[4,8,384,384]{2,3,1,0:T(8,128)} %get-tuple-element.21, f32[4,8,384]{2,1,0:T(8,128)S(1)} %copy-done.12), kind=kOutput, calls=%fused_computation.13 | output fusion | flops 33042816 | bytes 47235072 | tf_op jit(solution)/shard_map/sub | solution.py:34
  352.0 13.1 %copy.144 = bf16[4,8,384,384]{3,1,0,2:T(8,128)(2,1)} copy(bf16[4,8,384,384]{2,3,1,0:T(8,128)(2,1)} %fusion.4) | data formatting | bytes 18874368 | tf_op jit(solution)/shard_map/convert_element_type | solution.py:34
  365.2 7.4 convolution_bitcast_fusion.2
  377.2 2.5 convolution_multiply_fusion.4
  381.6 2.5 convolution_multiply_fusion.5
  388.2 6.0 all-to-all-start.5
  394.2 8.3 convolution_bitcast_fusion.1
  402.5 6.6 copy.142
  409.1 7.2 reshape_reshape.17
  416.3 5.6 convolution_multiply_fusion.1
  421.9 4.2 copy.155
  426.0 6.0 all-to-all-start.4
  432.1 9.9 %convolution_bitcast_fusion.5 = f32[3,8,8,128]{3,2,1,0:T(8,128)S(1)} fusion(f32[3,128,4096]{2,1,0:T(8,128)} %reshape_reshape.17, f32[3,64,4096]{2,1,0:T(8,128)} %gather_fusion.6), kind=kOutput, calls=%fused_computation.48 | convolution fusion | flops 1207959552 | bytes 9535488 | tf_op jit(solution)/shard_map/brc,bkc->brk/dot_general | solution.py:116
  444.8 24.4 %all-reduce.6.cloned.1.call-done = f32[3,128,192]{1,2,0:T(8,128)} async-done(((f32[3,128,192]{1,2,0:T(8,128)}), f32[3,128,192]{1,2,0:T(8,128)}) %all-reduce.6.cloned.1.call-update) | async-done | bytes 294928 | tf_op jit(solution)/shard_map/psum | solution.py:122
  469.2 7.1 convolution_bitcast_fusion
  476.4 15.8 %copy.151 = f32[3,4096,192]{2,0,1:T(4,128)} copy(f32[3,4096,192]{1,2,0:T(8,128)} %convolution_bitcast_fusion) | data formatting | bytes 18874368 | tf_op jit(solution)/shard_map/bri,brj->bij/dot_general | solution.py:124
  492.2 17.9 %all-to-all-done.4 = f32[3,64,4096]{2,0,1:T(4,128)} async-done(((f32[3,64,4096]{2,0,1:T(4,128)}), f32[3,64,4096]{2,0,1:T(4,128)}, u32[]{:S(2)}, u32[]{:S(2)}) %all-to-all-start.4) | async-done | bytes 3145760 | tf_op jit(solution)/shard_map/all_to_all | solution.py:146
  510.1 19.3 %all-to-all-start.3 = ((f32[3,4096,192]{2,0,1:T(4,128)}), f32[3,4096,192]{2,0,1:T(4,128)}, u32[]{:S(2)}, u32[]{:S(2)}) async-start(f32[3,4096,192]{2,0,1:T(4,128)} %copy.151), calls=%async_computation.3 | async-start | bytes 33554432 | tf_op jit(solution)/shard_map/all_to_all | solution.py:145
  530.9 361.1 %all-reduce = s32[48]{0:T(128)S(1)} all-reduce(s32[48]{0:T(128)S(1)} %dynamic-update-slice), channel_id=1, replica_groups=mesh['dp'=16,'mp'=2] {'dp'}, use_global_device_ids=true, to_apply=%add | all-reduce | flops 48 | bytes 384
  897.3 4.3 copy.156
  901.5 4.1 fusion.15
  905.7 4.7 copy.164
  910.4 16.5 %copy.179 = f32[3,16,256,192]{2,3,0,1:T(8,128)} copy(f32[3,16,256,192]{3,0,2,1:T(4,128)} %bitcast.34) | data formatting | bytes 18874368 | tf_op jit(solution)/shard_map/all_to_all | solution.py:145
  926.9 17.9 %fusion.6 = f32[64,256,192]{1,0,2:T(8,128)} fusion(f32[48,256,192]{1,2,0:T(8,128)} %bitcast.165, s32[48]{0:T(128)S(1)} %gather_fusion), kind=kOutput, calls=%fused_computation.17 | convolution fusion | flops 1811942400 | bytes 22020288 | tf_op jit(solution)/shard_map/tj,jrc->trc/dot_general | solution.py:152
  944.8 16.6 %copy.163 = f32[64,256,192]{1,2,0:T(8,128)} copy(f32[64,256,192]{1,0,2:T(8,128)} %fusion.6) | data formatting | bytes 25165824
  (75 shorter events, 48.1 us)
Async XLA Ops:
  7.2 196.7 %copy-start = (bf16[384,4096]{1,0:T(8,128)(2,1)S(1)}, bf16[384,4096]{1,0:T(8,128)(2,1)}, u32[]{:S(2)}) copy-start(bf16[384,4096]{1,0:T(8,128)(2,1)} %param.11) | copy-start | bytes 9437188
  11.0 21.5 %all-to-all-start.1 = ((f32[32,4,4,256]{3,2,1,0:T(4,128)}), f32[32,4,4,256]{3,2,1,0:T(4,128)}, u32[]{:S(2)}, u32[]{:S(2)}) async-start(f32[32,4,4,256]{3,2,1,0:T(4,128)} %gather_fusion.3), calls=%async_computation.1 | async-start | bytes 1048576 | tf_op jit(solution)/shard_map/all_to_all | solution.py:79
  32.5 119.5 %all-to-all-start = ((f32[32,256,192]{1,2,0:T(8,128)}), f32[32,256,192]{1,2,0:T(8,128)}, u32[]{:S(2)}, u32[]{:S(2)}) async-start(f32[32,256,192]{1,2,0:T(8,128)} %gather_fusion.1), calls=%async_computation | async-start | bytes 12582912 | tf_op jit(solution)/shard_map/all_to_all | solution.py:73
  37.4 142.4 %copy-start.9 = (s32[3]{0:T(128)S(1)}, s32[3]{0:T(128)}, u32[]{:S(2)}) copy-start(s32[3]{0:T(128)} %param.20) | copy-start | bytes 40
  152.1 75.1 %all-to-all-start.2 = ((f32[32,4,4096]{2,1,0:T(4,128)}), f32[32,4,4096]{2,1,0:T(4,128)}, u32[]{:S(2)}, u32[]{:S(2)}) async-start(f32[32,4,4096]{2,1,0:T(4,128)} %gather_fusion.5), calls=%async_computation.2 | async-start | bytes 4194304 | tf_op jit(solution)/shard_map/all_to_all | solution.py:76
  179.8 57.2 %all-reduce.4.cloned.1.call-start = ((), (), s32[]{:S(2)}) async-start(), calls=%async_computation.6 | async-start | bytes 589824 | tf_op jit(solution)/shard_map/psum | solution.py:88
  203.8 8.3 copy-start.8
  244.4 7.2 copy-start.7
  252.7 2.5 copy-start.6
  253.6 1.7 copy-start.2
  310.7 11.4 %copy-start.12 = (f32[4,8,384]{2,1,0:T(8,128)S(1)}, f32[4,8,384]{2,1,0:T(8,128)}, u32[]{:S(2)}) copy-start(f32[4,8,384]{2,1,0:T(8,128)} %get-tuple-element.20) | copy-start | bytes 147460
  388.2 37.8 %all-to-all-start.5 = ((f32[3,64,4,256]{3,2,0,1:T(4,128)}), f32[3,64,4,256]{3,2,0,1:T(4,128)}, u32[]{:S(2)}, u32[]{:S(2)}) async-start(f32[3,64,4,256]{3,2,0,1:T(4,128)} %copy.180), calls=%async_computation.5 | async-start | bytes 1572864 | tf_op jit(solution)/shard_map/all_to_all | solution.py:147
  426.0 84.1 %all-to-all-start.4 = ((f32[3,64,4096]{2,0,1:T(4,128)}), f32[3,64,4096]{2,0,1:T(4,128)}, u32[]{:S(2)}, u32[]{:S(2)}) async-start(f32[3,64,4096]{2,0,1:T(4,128)} %copy.155), calls=%async_computation.4 | async-start | bytes 8388608 | tf_op jit(solution)/shard_map/all_to_all | solution.py:146
  432.0 37.2 %all-reduce.6.cloned.1.call-start = ((), (), s32[]{:S(2)}) async-start(), calls=%async_computation.7 | async-start | bytes 589824 | tf_op jit(solution)/shard_map/psum | solution.py:122
  432.1 10.0 %copy-start.3 = (f32[3,128,512]{2,1,0:T(8,128)S(1)}, f32[3,128,512]{2,1,0:T(8,128)}, u32[]{:S(2)}) copy-start(f32[3,128,512]{2,1,0:T(8,128)} %reshape_reshape.19) | copy-start | bytes 2359300
  432.1 10.0 %copy-start.5 = (f32[3,64,512]{2,1,0:T(8,128)S(1)}, f32[3,64,512]{2,1,0:T(8,128)}, u32[]{:S(2)}) copy-start(f32[3,64,512]{2,1,0:T(8,128)} %reshape.135) | copy-start | bytes 1179652
  432.1 11.0 %copy-start.4 = (f32[3,128,512]{2,1,0:T(8,128)S(1)}, f32[3,128,512]{2,1,0:T(8,128)}, u32[]{:S(2)}) copy-start(f32[3,128,512]{2,1,0:T(8,128)} %reshape_reshape.18) | copy-start | bytes 2359300
  492.2 37.2 %copy-start.11 = (u32[32]{0:T(128)S(1)}, u32[32]{0:T(128)}, u32[]{:S(2)}) copy-start(u32[32]{0:T(128)} %constant.53) | copy-start | bytes 388
  492.2 38.5 %copy-start.10 = (s32[3]{0:T(128)S(1)}, s32[3]{0:T(128)}, u32[]{:S(2)}) copy-start(s32[3]{0:T(128)} %param.20) | copy-start | bytes 40
  492.2 399.9 %copy-start.1 = (s32[16,2]{0,1:T(2,128)S(1)}, s32[16,2]{0,1:T(2,128)}, u32[]{:S(2)}) copy-start(s32[16,2]{0,1:T(2,128)} %param.21) | copy-start | bytes 388
  510.1 400.3 %all-to-all-start.3 = ((f32[3,4096,192]{2,0,1:T(4,128)}), f32[3,4096,192]{2,0,1:T(4,128)}, u32[]{:S(2)}, u32[]{:S(2)}) async-start(f32[3,4096,192]{2,0,1:T(4,128)} %copy.151), calls=%async_computation.3 | async-start | bytes 33554432 | tf_op jit(solution)/shard_map/all_to_all | solution.py:145
Sparse Core Ops, SparseCore 0:
  212.2 23.9 all-reduce.3
  444.9 24.2 all-reduce.5
where the time goes:
time: 980 us; the launch traced here: 969 us
  blocking collectives  361 us (37%)
  local copies, waits for them, and re-layouts  182 us (19%)
  waiting for transfers between devices  158 us (16%)
  matrix products  119 us (12%)
  starting transfers between devices  71.3 us (7%)
  other arithmetic  61.7 us (6%)
  between operations  15.3 us (2%)
    unnamed x1, blocking collectives  361 us
    all_to_all x1, waiting for transfers between devices, on_device(): lax.all_to_all(adapter_down_weight[desired_result], 'dp', split_axis=0, c...  109 us
    unnamed x34, local copies, waits for them, and re-layouts  31.7 us
    sub x1, other arithmetic, attention_grads(): grad_probs - row_inner  29.9 us
    all_to_all x1, starting transfers between devices, on_device(): lax.all_to_all(adapter_up_query[desired_result], 'dp', split_axis=0, conc...  27.7 us
    psum x1, waiting for transfers between devices, on_device(): lax.psum(gradient_portion.reshape(row_count, 3 * adapter_rank), 'mp')  24.4 us
    sub x1, other arithmetic, attention_grads(): weights = jnp.exp(scores - row_top)  24.1 us
  transfers between devices with their start and end apart: 8, of which 4 were waited for; matrix products, arithmetic and copies ran while one was open for 15% of the time, Pallas kernels for 0%

commit v1 on v0

v1 whole, which is shorter than its diff:
```python
import functools

import jax
import jax.numpy as jnp
from jax import lax
from jax.experimental import pallas as pl
from jax.experimental.pallas import tpu as pltpu
from jax.sharding import PartitionSpec as P

ADAPTER_SCALE = 0.5
MASKED = -1e30
BF16, F32 = jnp.bfloat16, jnp.float32
VMEM_LIMIT = 56 * 1024 * 1024
NN = (((1,), (0,)), ((), ()))
NT = (((1,), (1,)), ((), ()))
TN = (((0,), (0,)), ((), ()))
HEADS_PER_CALL = 4


def split2(a):
    high = a.astype(BF16)
    return high, (a - high.astype(F32)).astype(BF16)


def mm(a, b, dims=NN):
    return lax.dot_general(a, b, dims, preferred_element_type=F32)


def mm3(a, b, dims=NN):
    (ah, al), (bh, bl) = a, b
    return mm(ah, bh, dims) + mm(ah, bl, dims) + mm(al, bh, dims)


def bit_reverse(value, bits):
    out = jnp.zeros_like(value)
    for k in range(bits):
        out = out | (((value >> k) & 1) << (bits - 1 - k))
    return out


def swap(a, axis, size, bit):
    return lax.ppermute(a, axis, [(i, i ^ bit) for i in range(size)])


def sum_over(a, axis, size):
    bit = 1
    while bit < size:
        a = a + swap(a, axis, size, bit)
        bit *= 2
    return a


def scatter_sum(part, axis, size):
    bit = 1
    while bit < size:
        half = part.shape[0] // 2
        part = part[:half] + swap(part[half:], axis, size, bit)
        bit *= 2
    return part[0]


def gather_halves(a, axis, size):
    a = a[None]
    bit = size // 2
    while bit > 1:
        a = jnp.concatenate([a, swap(a, axis, size, bit)], axis=0)
        bit //= 2
    return a, swap(a, axis, size, 1)


def by_tenant(owners, tenants):
    count = owners.shape[0]
    index = jnp.arange(count, dtype=jnp.int32)
    ahead = (owners[None, :] < owners[:, None]) | (
        (owners[None, :] == owners[:, None]) & (index[None, :] < index[:, None])
    )
    place = jnp.sum(ahead.astype(jnp.int32), axis=1)
    order = jnp.sum(
        jnp.where(place[None, :] == index[:, None], index[None, :], 0), axis=1
    )
    edge = jnp.arange(tenants + 1, dtype=jnp.int32)
    first = jnp.sum((owners[None, :] < edge[:, None]).astype(jnp.int32), axis=1)
    return order.astype(jnp.int32), first.astype(jnp.int32)


def down_kernel(source_ref, tenant_ref, x_ref, w_ref, out_ref):
    x = x_ref[0].astype(BF16)
    high, low = split2(w_ref[0])
    out_ref[0] = mm(high, x, NT) + mm(low, x, NT)


def down_partial(x, weights, source, tenant):
    n, rows, width = x.shape
    rank = weights.shape[1]
    return pl.pallas_call(
        down_kernel,
        grid_spec=pltpu.PrefetchScalarGridSpec(
            num_scalar_prefetch=2,
            grid=(n,),
            in_specs=[
                pl.BlockSpec((1, rows, width), lambda p, s, t: (s[p], 0, 0)),
                pl.BlockSpec((1, rank, width), lambda p, s, t: (t[p], 0, 0)),
            ],
            out_specs=pl.BlockSpec((1, rank, rows), lambda p, s, t: (p, 0, 0)),
        ),
        out_shape=jax.ShapeDtypeStruct((n, rank, rows), F32),
        compiler_params=pltpu.CompilerParams(vmem_limit_bytes=VMEM_LIMIT),
        name="down_partial",
    )(source, tenant, x, weights)


def attention_kernel(
    groups,
    blocks,
    slots,
    fq_ref,
    fk_ref,
    fv_ref,
    up_ref,
    *rest,
):
    low_refs = rest[:blocks]
    (
        panel_ref,
        slot_ref,
        doc_row_ref,
        doc_col_ref,
        du_ref,
        g_ref,
        bias,
        low_t,
        lct_h,
        lct_l,
        lc_h,
        lc_l,
        panel,
        du,
        q_s,
        dq_s,
        dk_t,
        dv_t,
    ) = rest[blocks:]
    step = pl.program_id(0)
    rows, head = fk_ref.shape
    block = rows // blocks
    owners, _, piece, _ = panel_ref.shape
    rank = owners * piece
    wide = groups * head
    inverse = 1.0 / head**0.5
    slot = slot_ref[...]

    @pl.when(step == 0)
    def _():
        row = lax.broadcasted_iota(jnp.int32, (rows, rows), 0)
        col = lax.broadcasted_iota(jnp.int32, (rows, rows), 1)
        joined = (doc_row_ref[...] == doc_col_ref[...]) & (row >= col)
        bias[...] = jnp.where(joined, 0.0, MASKED)
        for b in range(blocks):
            low_t[:, b * block : (b + 1) * block] = low_refs[b][...]
        for part in range(3):
            low = low_t[part * rank : (part + 1) * rank, :] * ADAPTER_SCALE
            for s in range(slots):
                mine = jnp.where(slot == s, low, 0.0)
                span = slice(s * rank, (s + 1) * rank)
                high, rest_ = split2(mine)
                lct_h[part, span, :] = high
                lct_l[part, span, :] = rest_
            both = jnp.concatenate(
                [jnp.where(slot == s, low, 0.0) for s in range(slots)], axis=0
            ).T
            high, rest_ = split2(both)
            lc_h[part] = high
            lc_l[part] = rest_
        g_ref[...] = jnp.zeros_like(g_ref)

    for w in range(owners):
        for s in range(slots):
            start = s * rank + w * piece
            panel[start : start + piece, :] = panel_ref[w, s]
    u_q = split2(panel[:, :wide])
    u_k = split2(panel[:, wide : wide + head])
    u_v = split2(panel[:, wide + head :])
    k = (fk_ref[...].astype(F32) + mm3((lc_h[1], lc_l[1]), u_k)).astype(BF16)
    v = (fv_ref[...].astype(F32) + mm3((lc_h[2], lc_l[2]), u_v)).astype(BF16)
    q_s[...] = (fq_ref[...].astype(F32) + mm3((lc_h[0], lc_l[0]), u_q)).astype(BF16)
    dk_t[...] = jnp.zeros_like(dk_t)
    dv_t[...] = jnp.zeros_like(dv_t)

    for b in range(blocks):
        here = slice(b * block, (b + 1) * block)
        reach = (b + 1) * block
        kk, vv = k[:reach], v[:reach]
        mask = bias[here, :reach]
        for h in range(groups):
            lanes = slice(h * head, (h + 1) * head)
            q = q_s[here, lanes]
            up = up_ref[here, lanes]
            scores = mm(q, kk, NT) * inverse + mask
            top = jnp.max(scores, axis=-1, keepdims=True)
            weights = jnp.exp(scores - top)
            total = jnp.sum(weights, axis=-1, keepdims=True)
            probs = weights * (1.0 / total)
            grad_probs = mm(up, vv, NT)
            inner = jnp.sum(probs * grad_probs, axis=-1, keepdims=True)
            grad_scores = (probs * (grad_probs - inner) * inverse).astype(BF16)
            dq_s[here, lanes] = mm(grad_scores, kk)
            dk_t[:, :reach] += mm(q, grad_scores, TN)
            dv_t[:, :reach] += mm(up, probs.astype(BF16), TN)

    dq = split2(dq_s[...])
    dk = split2(dk_t[...])
    dv = split2(dv_t[...])
    du[:, :wide] = mm3((lct_h[0], lct_l[0]), dq)
    du[:, wide : wide + head] = mm3((lct_h[1], lct_l[1]), dk, NT)
    du[:, wide + head :] = mm3((lct_h[2], lct_l[2]), dv, NT)
    for w in range(owners):
        for s in range(slots):
            start = s * rank + w * piece
            du_ref[w, s] = du[start : start + piece, :]
    for part, both in enumerate((mm3(u_q, dq, NT), mm3(u_k, dk), mm3(u_v, dv))):
        mine = jnp.zeros((rank, rows), F32)
        for s in range(slots):
            mine += jnp.where(slot == s, both[s * rank : (s + 1) * rank], 0.0)
        mine *= ADAPTER_SCALE
        for b in range(blocks):
            g_ref[b, part * rank : (part + 1) * rank, :] += mine[
                :, b * block : (b + 1) * block
            ]


def attention(fq, fk, fv, up, lows, panels, slot_rows, docs, head, first, heads):
    rows = fq.shape[0]
    blocks = len(lows)
    block = rows // blocks
    n, slots, piece, cols = panels.shape
    kv_heads = fk.shape[1] // head
    groups = fq.shape[1] // fk.shape[1]
    wide = groups * head
    per = wide + 2 * head
    rank = n * piece
    whole = lambda shape: pl.BlockSpec(shape, lambda g: (0,) * len(shape))
    spans = slots * rank
    return pl.pallas_call(
        functools.partial(attention_kernel, groups, blocks, slots),
        grid=(heads,),
        in_specs=[
            pl.BlockSpec((rows, wide), lambda g: (0, first + g)),
            pl.BlockSpec((rows, head), lambda g: (0, first + g)),
            pl.BlockSpec((rows, head), lambda g: (0, first + g)),
            pl.BlockSpec((rows, wide), lambda g: (0, first + g)),
        ]
        + [whole((3 * rank, block))] * blocks
        + [
            pl.BlockSpec((n, slots, piece, per), lambda g: (0, 0, 0, g)),
            whole((1, rows)),
            whole((1, rows)),
            whole((rows, 1)),
        ],
        out_specs=[
            pl.BlockSpec((n, slots, piece, per), lambda g: (0, 0, 0, g)),
            whole((blocks, 3 * rank, block)),
        ],
        out_shape=[
            jax.ShapeDtypeStruct((n, slots, piece, heads * per), F32),
            jax.ShapeDtypeStruct((blocks, 3 * rank, block), F32),
        ],
        scratch_shapes=[
            pltpu.VMEM((rows, rows), F32),
            pltpu.VMEM((3 * rank, rows), F32),
            pltpu.VMEM((3, spans, rows), BF16),
            pltpu.VMEM((3, spans, rows), BF16),
            pltpu.VMEM((3, rows, spans), BF16),
            pltpu.VMEM((3, rows, spans), BF16),
            pltpu.VMEM((spans, per), F32),
            pltpu.VMEM((spans, per), F32),
            pltpu.VMEM((rows, wide), BF16),
            pltpu.VMEM((rows, wide), F32),
            pltpu.VMEM((head, rows), F32),
            pltpu.VMEM((head, rows), F32),
        ],
        compiler_params=pltpu.CompilerParams(vmem_limit_bytes=VMEM_LIMIT),
        name="attention_grads",
    )(fq, fk, fv, up, *lows, panels, slot_rows, docs[None, :], docs[:, None])


def down_grad_kernel(blocks, per_step, order_ref, first_ref, source_ref, *refs):
    x_refs, (g0_ref, g1_ref, out_ref, x_all, g_ref, sems) = refs[:blocks], refs[blocks:]
    half = g0_ref.shape[0]
    step = pl.program_id(0)

    @pl.when(step == 0)
    def _():
        copies = [
            pltpu.make_async_copy(x_refs[b], x_all.at[b], sems.at[b]) for b in range(blocks)
        ] + [
            pltpu.make_async_copy(
                ref, g_ref.at[pl.ds(side * half, half)], sems.at[blocks + side]
            )
            for side, ref in enumerate((g0_ref, g1_ref))
        ]
        for copy in copies:
            copy.start()
        for copy in copies:
            copy.wait()

    for t in range(per_step):
        tenant = step * per_step + t
        out_ref[t] = jnp.zeros(out_ref.shape[1:], F32)

        def add(e, carry):
            item = order_ref[e]
            place = item // blocks
            b = item - place * blocks
            x = x_all[b, source_ref[place]].astype(BF16)
            high, low = split2(g_ref[place, b])
            out_ref[t] += mm(high, x) + mm(low, x)
            return carry

        lax.fori_loop(first_ref[tenant], first_ref[tenant + 1], add, 0)


def down_grad(xs, g, order, first, source, tenants):
    blocks = len(xs)
    n, rows, width = xs[0].shape
    rank = g[0].shape[2]
    per_step = 8
    return pl.pallas_call(
        functools.partial(down_grad_kernel, blocks, per_step),
        grid_spec=pltpu.PrefetchScalarGridSpec(
            num_scalar_prefetch=3,
            grid=(tenants // per_step,),
            in_specs=[pl.BlockSpec(memory_space=pl.ANY)] * (blocks + 2),
            out_specs=pl.BlockSpec((per_step, rank, width), lambda i, *_: (i, 0, 0)),
            scratch_shapes=[
                pltpu.VMEM((blocks, n, rows, width), F32),
                pltpu.VMEM((n,) + g[0].shape[1:], F32),
                pltpu.SemaphoreType.DMA((blocks + 2,)),
            ],
        ),
        out_shape=jax.ShapeDtypeStruct((tenants, rank, width), F32),
        compiler_params=pltpu.CompilerParams(vmem_limit_bytes=VMEM_LIMIT),
        name="down_grad",
    )(order, first, source, *xs, *g)


def up_grad_kernel(calls, per_step, kv_heads, head, order_ref, first_ref, *refs):
    in_refs, (q_ref, kv_ref) = refs[:calls], refs[calls:]
    step = pl.program_id(0)
    wide = q_ref.shape[2] // kv_heads
    per = wide + 2 * head
    heads = kv_heads // calls
    for t in range(per_step):
        tenant = step * per_step + t
        q_ref[t] = jnp.zeros(q_ref.shape[1:], F32)
        kv_ref[t] = jnp.zeros(kv_ref.shape[1:], F32)

        def add(e, carry):
            item = order_ref[e]
            for c in range(calls):
                for h in range(heads):
                    at = c * heads + h
                    q_ref[t, :, at * wide : (at + 1) * wide] += in_refs[c][
                        item, :, h * per : h * per + wide
                    ]
                    kv_ref[t, at] += in_refs[c][item, :, h * per + wide : (h + 1) * per]
            return carry

        lax.fori_loop(first_ref[tenant], first_ref[tenant + 1], add, 0)


def up_grad(dus, order, first, tenants, kv_heads, head):
    calls = len(dus)
    items, piece, cols = dus[0].shape
    per_step = 8
    wide = cols * calls // kv_heads - 2 * head
    return pl.pallas_call(
        functools.partial(up_grad_kernel, calls, per_step, kv_heads, head),
        grid_spec=pltpu.PrefetchScalarGridSpec(
            num_scalar_prefetch=2,
            grid=(tenants // per_step,),
            in_specs=[pl.BlockSpec((items, piece, cols), lambda i, *_: (0, 0, 0))] * calls,
            out_specs=[
                pl.BlockSpec((per_step, piece, kv_heads * wide), lambda i, *_: (i, 0, 0)),
                pl.BlockSpec((per_step, kv_heads, piece, 2 * head), lambda i, *_: (i, 0, 0, 0)),
            ],
        ),
        out_shape=[
            jax.ShapeDtypeStruct((tenants, piece, kv_heads * wide), F32),
            jax.ShapeDtypeStruct((tenants, kv_heads, piece, 2 * head), F32),
        ],
        compiler_params=pltpu.CompilerParams(vmem_limit_bytes=VMEM_LIMIT),
        name="up_grad",
    )(order, first, *dus)


def exchange(a):
    return lax.all_to_all(a, "dp", split_axis=0, concat_axis=0, tiled=True)


def on_device(
    dp_count,
    mp_count,
    normed_input_rows,
    frozen_queries,
    frozen_keys,
    frozen_values,
    attention_output_gradient,
    adapter_down_weight,
    adapter_up_query,
    adapter_up_key_value,
    document_numbers,
    block_tenant_slot,
    shard_tenant_table,
):
    rows = normed_input_rows.shape[0]
    blocks = block_tenant_slot.shape[0]
    block = rows // blocks
    tenants, width, ranks = adapter_down_weight.shape
    slots = shard_tenant_table.shape[1]
    piece = adapter_up_query.shape[1]
    kv_heads = adapter_up_key_value.shape[2]
    head = adapter_up_key_value.shape[3] // 2
    wide = adapter_up_query.shape[2] // kv_heads
    me = lax.axis_index("dp").astype(jnp.int32)

    xs = [
        exchange(
            normed_input_rows[b * block : (b + 1) * block]
            .reshape(block, dp_count, width)
            .transpose(1, 0, 2)
            .astype(F32)
        )
        for b in range(blocks)
    ]

    source = me ^ bit_reverse(
        jnp.arange(dp_count, dtype=jnp.int32), dp_count.bit_length() - 1
    )
    slots_all = jnp.concatenate(gather_halves(block_tenant_slot, "dp", dp_count), axis=0)
    owners = shard_tenant_table[source[:, None], slots_all]

    wanted = shard_tenant_table.reshape(-1)
    up_query = adapter_up_query[wanted].reshape(-1, piece, kv_heads, wide)
    up_key_value = adapter_up_key_value[wanted]
    wire = jnp.concatenate([up_query, up_key_value], axis=-1)
    heads = min(HEADS_PER_CALL, kv_heads)
    calls = kv_heads // heads
    per = wide + 2 * head
    panels = [
        exchange(
            wire[:, :, c * heads : (c + 1) * heads].reshape(-1, piece, heads * per)
        ).reshape(dp_count, slots, piece, heads * per)
        for c in range(calls)
    ]

    weights = jnp.swapaxes(adapter_down_weight, 1, 2)
    lows = []
    for b in range(blocks):
        part = down_partial(xs[b], weights, source, owners[:, b])
        lows.append(sum_over(scatter_sum(part, "dp", dp_count), "mp", mp_count))

    slot_rows = jnp.repeat(block_tenant_slot, block)[None, :]
    dus, g = [], None
    for c in range(calls):
        du, g_part = attention(
            frozen_queries,
            frozen_keys,
            frozen_values,
            attention_output_gradient,
            lows,
            panels[c],
            slot_rows,
            document_numbers,
            head,
            c * heads,
            heads,
        )
        dus.append(exchange(du.reshape(dp_count * slots, piece, heads * per)))
        g = g_part if g is None else g + g_part

    g_halves = gather_halves(sum_over(g, "mp", mp_count), "dp", dp_count)
    order, first = by_tenant(owners.reshape(-1), tenants)
    grad_down = down_grad(xs, g_halves, order, first, source, tenants)
    order, first = by_tenant(wanted, tenants)
    grad_upq, grad_upkv = up_grad(dus, order, first, tenants, kv_heads, head)
    return (
        jnp.swapaxes(grad_down, 1, 2),
        grad_upq,
        jnp.swapaxes(grad_upkv, 1, 2),
    )


def solution(mesh):
    placed = (
        P("dp", "mp"),
        P("dp", "mp"),
        P("dp", "mp"),
        P("dp", "mp"),
        P("dp", "mp"),
        P(None, ("mp", "dp"), None),
        P(None, "dp", "mp"),
        P(None, "dp", "mp", None),
        P("dp"),
        P("dp"),
        P(),
    )
    return jax.shard_map(
        functools.partial(on_device, mesh.shape["dp"], mesh.shape["mp"]),
        mesh=mesh,
        in_specs=placed,
        out_specs=(P(None, ("mp", "dp"), None), P(None, "dp", "mp"), P(None, "dp", "mp", None)),
        check_vma=False,
    )
```

time: 980 us -> 529 us (0.54)
  blocking collectives: 361 us -> 0 us
  local copies, waits for them, and re-layouts: 182 us -> 43.6 us
  waiting for transfers between devices: 158 us -> 278 us
  matrix products: 119 us -> 0 us
  Pallas kernels: 0 us -> 117 us
  other arithmetic: 61.7 us -> 10.2 us
  between operations: 15.3 us -> 0.97 us
    unnamed x1 -> x0, blocking collectives: 361 us -> none
    ppermute x0 -> x24, waiting for transfers between devices: none -> 185 us  [swap(): return lax.ppermute(a, axis, [(i, i ^ bit) for i in range(size)])]
    dot_general x19 -> x0, matrix products: 119 us -> none  [the longest x1 17.9 us: on_device(): jnp.einsum('tj,jrc->trc', owner_hot, down_in, precision=PRECISION_HIGH)]
    pallas_call x0 -> x6, Pallas kernels: none -> 117 us  [the longest x1 56.2 us: attention(): pl.pallas_call(functools.partial(attention_kernel, groups, blocks, slots)...]
    sub x2 -> x0, other arithmetic: 54 us -> none  [the longest x1 29.9 us: attention_grads(): grad_probs - row_inner]
    all_to_all x8 -> x0, local copies, waits for them, and re-layouts: 46.1 us -> none  [the longest x1 16.5 us: on_device(): lax.all_to_all(down_terms, 'dp', split_axis=1, concat_axis=0, tiled=True)]
    all_to_all x6 -> x5, waiting for transfers between devices: 133 us -> 93 us  [exchange(): return lax.all_to_all(a, 'dp', split_axis=0, concat_axis=0, tiled=True)]
    ppermute x0 -> x24, starting transfers between devices: none -> 30.7 us  [swap(): return lax.ppermute(a, axis, [(i, i ^ bit) for i in range(size)])]
  transfers between devices with their start and end apart: 8 -> 29, of which waited for: 4 -> 16; matrix products, arithmetic and copies ran while one was open for 15% -> 8% of each run, Pallas kernels for 0% -> 10%
where the time goes in v1:
time: 529 us; the launch traced here: 527 us
  waiting for transfers between devices  278 us (53%)
  Pallas kernels  117 us (22%)
  starting transfers between devices  76.9 us (15%)
  local copies, waits for them, and re-layouts  43.6 us (8%)
  other arithmetic  10.2 us (2%)
    ppermute x24, waiting for transfers between devices, swap(): return lax.ppermute(a, axis, [(i, i ^ bit) for i in range(size)])  185 us
    all_to_all x5, waiting for transfers between devices, exchange(): return lax.all_to_all(a, 'dp', split_axis=0, concat_axis=0, tiled=True)  93 us
    pallas_call x1, Pallas kernels, attention(): pl.pallas_call(functools.partial(attention_kernel, groups, blocks, slots)...  56.2 us
    all_to_all x5, starting transfers between devices, exchange(): return lax.all_to_all(a, 'dp', split_axis=0, concat_axis=0, tiled=True)  46.2 us
    pallas_call x3, Pallas kernels, down_partial(): pl.pallas_call(down_kernel, grid_spec=pltpu.PrefetchScalarGridSpec(num_sc...  36.7 us
    ppermute x24, starting transfers between devices, swap(): return lax.ppermute(a, axis, [(i, i ^ bit) for i in range(size)])  30.7 us
    pallas_call x1, Pallas kernels, down_grad(): pl.pallas_call(functools.partial(down_grad_kernel, blocks, per_step), gri...  18.1 us
  transfers between devices with their start and end apart: 29, of which 16 were waited for; matrix products, arithmetic and copies ran while one was open for 8% of the time, Pallas kernels for 10%

profile of v1, /device:TPU:1, one launch (start us, length us, event | category | flops | bytes accessed | tf_op | source)
XLA Modules:
  0.0 526.8 jit_solution(12382898808608536221)
XLA Ops:
  0.6 3.6 fusion.25
  4.9 1.6 copy.50
  6.5 7.3 %all-to-all-start.2 = ((f32[16,128,256]{2,1,0:T(8,128)}), f32[16,128,256]{2,1,0:T(8,128)S(1)}, u32[]{:S(2)}, u32[]{:S(2)}) async-start(f32[16,128,256]{2,1,0:T(8,128)} %bitcast.44), calls=%async_computation.2 | async-start | bytes 4194304 | tf_op jit(solution)/shard_map/all_to_all | solution.py:397
  13.8 2.3 copy.56
  16.1 2.6 copy.48
  18.7 36.6 %all-to-all-done.2.x_ref.refs_2_ = f32[16,128,256]{2,1,0:T(8,128)S(1)} async-done(((f32[16,128,256]{2,1,0:T(8,128)}), f32[16,128,256]{2,1,0:T(8,128)S(1)}, u32[]{:S(2)}, u32[]{:S(2)}) %all-to-all-start.2) | async-done | bytes 2097184 | tf_op jit(solution)/shard_map/all_to_all | solution.py:397
  55.3 10.9 %all-to-all-start.1 = ((f32[16,128,256]{2,1,0:T(8,128)}), f32[16,128,256]{2,1,0:T(8,128)}, u32[]{:S(2)}, u32[]{:S(2)}) async-start(f32[16,128,256]{2,1,0:T(8,128)} %bitcast.43), calls=%async_computation.1 | async-start | bytes 4194304 | tf_op jit(solution)/shard_map/all_to_all | solution.py:397
  66.2 2.3 copy.55
  68.4 2.6 copy.46
  71.0 36.7 %all-to-all-done.1.x_ref.refs_1_ = f32[16,128,256]{2,1,0:T(8,128)} async-done(((f32[16,128,256]{2,1,0:T(8,128)}), f32[16,128,256]{2,1,0:T(8,128)}, u32[]{:S(2)}, u32[]{:S(2)}) %all-to-all-start.1) | async-done | bytes 2097184 | tf_op jit(solution)/shard_map/all_to_all | solution.py:397
  107.7 10.9 %all-to-all-start = ((f32[16,128,256]{2,1,0:T(8,128)}), f32[16,128,256]{2,1,0:T(8,128)S(1)}, u32[]{:S(2)}, u32[]{:S(2)}) async-start(f32[16,128,256]{2,1,0:T(8,128)} %bitcast.42), calls=%async_computation | async-start | bytes 4194304 | tf_op jit(solution)/shard_map/all_to_all | solution.py:397
  118.6 2.4 collective-permute-start
  121.3 1.6 gather_fusion.2
  122.9 5.2 gather_fusion.1
  128.0 4.0 reshape.291
  132.1 3.8 pad_maximum_fusion
  135.9 4.5 reshape.292
  140.4 19.7 %all-to-all-done.x_ref.refs_0_ = f32[16,128,256]{2,1,0:T(8,128)S(1)} async-done(((f32[16,128,256]{2,1,0:T(8,128)}), f32[16,128,256]{2,1,0:T(8,128)S(1)}, u32[]{:S(2)}, u32[]{:S(2)}) %all-to-all-start) | async-done | bytes 2097184 | tf_op jit(solution)/shard_map/all_to_all | solution.py:397
  160.1 1.4 copy-done.4
  161.5 10.9 %all-to-all-start.3 = ((f32[32,4,5120]{2,1,0:T(4,128)}), f32[32,4,5120]{2,1,0:T(4,128)}, u32[]{:S(2)}, u32[]{:S(2)}) async-start(f32[32,4,5120]{2,1,0:T(4,128)} %reshape.292), calls=%async_computation.3 | async-start | bytes 5242880 | tf_op jit(solution)/shard_map/all_to_all | solution.py:397
  173.1 1.4 collective-permute-start.1
  174.5 40.8 %collective-permute-done.1 = s32[2,3]{1,0:T(2,128)S(1)} collective-permute-done((s32[2,3]{1,0:T(2,128)S(1)}, s32[2,3]{1,0:T(2,128)S(1)}, u32[]{:S(2)}, u32[]{:S(2)}) %collective-permute-start.1) | collective-permute-done | bytes 56 | tf_op jit(solution)/shard_map/ppermute | solution.py:42
  215.4 2.0 collective-permute-start.2
  217.4 1.6 collective-permute-done.2
  223.5 12.2 %down_partial.3 = f32[16,192,128]{2,1,0:T(8,128)} custom-call(s32[16]{0:T(128)} %fusion.19.source_ref, s32[16]{0:T(128)} %get-tuple-element.21.tenant_ref, f32[16,128,256]{2,1,0:T(8,128)} %copy-done.4, f32[64,192,256]{2,1,0:T(8,128)} %bitcast.38), custom_call_target="tpu_custom_call" | custom-call | tf_op jit(solution)/shard_map/down_partial/pallas_call | solution.py:95
  237.3 12.2 %down_partial.4 = f32[16,192,128]{2,1,0:T(8,128)} custom-call(s32[16]{0:T(128)} %fusion.19.source_ref, s32[16]{0:T(128)} %get-tuple-element.22.tenant_ref, f32[16,128,256]{2,1,0:T(8,128)} %all-to-all-done.1.x_ref.refs_1_, f32[64,192,256]{2,1,0:T(8,128)} %bitcast.39), custom_call_target="tpu_custom_call" | custom-call | tf_op jit(solution)/shard_map/down_partial/pallas_call | solution.py:95
  250.9 12.3 %down_partial.5 = f32[16,192,128]{2,1,0:T(8,128)} custom-call(s32[16]{0:T(128)} %fusion.19.source_ref, s32[16]{0:T(128)} %get-tuple-element.20.tenant_ref, f32[16,128,256]{2,1,0:T(8,128)} %copy-done.3, f32[64,192,256]{2,1,0:T(8,128)} %bitcast.40), custom_call_target="tpu_custom_call" | custom-call | tf_op jit(solution)/shard_map/down_partial/pallas_call | solution.py:95
  265.1 1.7 collective-permute-start.5
  267.2 1.6 collective-permute-start.15
  268.7 7.3 %collective-permute-done.5 = f32[4,192,128]{2,1,0:T(8,128)S(1)} collective-permute-done((f32[4,192,128]{2,1,0:T(8,128)S(1)}, f32[4,192,128]{2,1,0:T(8,128)S(1)}, u32[]{:S(2)}, u32[]{:S(2)}) %collective-permute-start.5) | collective-permute-done | bytes 393248 | tf_op jit(solution)/shard_map/ppermute | solution.py:42
  276.1 2.3 collective-permute-start.6
  278.4 6.0 %collective-permute-done.10 = f32[4,192,128]{2,1,0:T(8,128)S(1)} collective-permute-done((f32[4,192,128]{2,1,0:T(8,128)S(1)}, f32[4,192,128]{2,1,0:T(8,128)S(1)}, u32[]{:S(2)}, u32[]{:S(2)}) %collective-permute-start.10) | collective-permute-done | bytes 393248 | tf_op jit(solution)/shard_map/ppermute | solution.py:42
  284.6 2.3 collective-permute-start.11
  286.9 6.0 %collective-permute-done.15 = f32[4,192,128]{2,1,0:T(8,128)S(1)} collective-permute-done((f32[4,192,128]{2,1,0:T(8,128)S(1)}, f32[4,192,128]{2,1,0:T(8,128)S(1)}, u32[]{:S(2)}, u32[]{:S(2)}) %collective-permute-start.15) | collective-permute-done | bytes 393248 | tf_op jit(solution)/shard_map/ppermute | solution.py:42
  293.0 2.3 collective-permute-start.16
  296.4 1.5 collective-permute-start.12
  297.9 5.3 %collective-permute-done.16 = f32[2,192,128]{2,1,0:T(8,128)S(1)} collective-permute-done((f32[2,192,128]{2,1,0:T(8,128)S(1)}, f32[2,192,128]{2,1,0:T(8,128)S(1)}, u32[]{:S(2)}, u32[]{:S(2)}) %collective-permute-start.16) | collective-permute-done | bytes 196640 | tf_op jit(solution)/shard_map/ppermute | solution.py:42
  305.0 6.5 %collective-permute-done.17 = f32[1,192,128]{2,1,0:T(8,128)S(1)} collective-permute-done((f32[1,192,128]{2,1,0:T(8,128)S(1)}, f32[1,192,128]{2,1,0:T(8,128)S(1)}, u32[]{:S(2)}, u32[]{:S(2)}) %collective-permute-start.17) | collective-permute-done | bytes 98336 | tf_op jit(solution)/shard_map/ppermute | solution.py:42
  316.8 56.2 %attention_grads.1 = (f32[16,2,4,5120]{3,2,1,0:T(4,128)}, f32[3,192,128]{2,1,0:T(8,128)}) custom-call(bf16[384,4096]{1,0:T(8,128)(2,1)} %fq_ref.1, bf16[384,512]{1,0:T(8,128)(2,1)} %fk_ref.1, bf16[384,512]{1,0:T(8,128)(2,1)} %fv_ref.1, bf16[384,4096]{1,0:T(8,128)(2,1)} %up_ref.1, f32[192,128]{1,0:T(8,128)} %add.87.rest_0_, f32[192,128]{1,0:T(8,128)} %add.92.rest_1_, ...), custom_call_target="tpu_custom_call" | custom-call | tf_op jit(solution)/shard_map/attention_grads/pallas_call | solution.py:243
  374.0 6.3 %all-to-all-start.4 = ((f32[32,4,5120]{2,1,0:T(4,128)}), f32[32,4,5120]{2,1,0:T(4,128)}, u32[]{:S(2)}, u32[]{:S(2)}) async-start(f32[32,4,5120]{2,1,0:T(4,128)} %bitcast.48), calls=%async_computation.4 | async-start | bytes 5242880 | tf_op jit(solution)/shard_map/all_to_all | solution.py:397
  381.0 1.7 collective-permute-start.20
  382.7 69.8 %collective-permute-done.20 = f32[1,3,192,128]{3,2,1,0:T(8,128)S(1)} collective-permute-done((f32[1,3,192,128]{3,2,1,0:T(8,128)S(1)}, f32[1,3,192,128]{3,2,1,0:T(8,128)S(1)}, u32[]{:S(2)}, u32[]{:S(2)}) %collective-permute-start.20) | collective-permute-done | bytes 294944 | tf_op jit(solution)/shard_map/ppermute | solution.py:42
  452.7 14.0 %collective-permute-done.21 = f32[2,3,192,128]{3,2,1,0:T(8,128)S(1)} collective-permute-done((f32[2,3,192,128]{3,2,1,0:T(8,128)S(1)}, f32[2,3,192,128]{3,2,1,0:T(8,128)S(1)}, u32[]{:S(2)}, u32[]{:S(2)}) %collective-permute-start.21) | collective-permute-done | bytes 589856 | tf_op jit(solution)/shard_map/ppermute | solution.py:42
  468.0 24.5 %collective-permute-done.22 = f32[4,3,192,128]{3,2,1,0:T(8,128)S(1)} collective-permute-done((f32[4,3,192,128]{3,2,1,0:T(8,128)S(1)}, f32[4,3,192,128]{3,2,1,0:T(8,128)S(1)}, u32[]{:S(2)}, u32[]{:S(2)}) %collective-permute-start.22) | collective-permute-done | bytes 1179680 | tf_op jit(solution)/shard_map/ppermute | solution.py:42
  492.7 2.8 collective-permute-start.23
  499.7 18.1 %down_grad.1 = f32[64,192,256]{2,1,0:T(8,128)} custom-call(s32[48]{0:T(128)} %select_reduce_fusion.order_ref, s32[65]{0:T(128)} %convert_reduce_fusion.first_ref, s32[16]{0:T(128)} %fusion.19.source_ref, f32[16,128,256]{2,1,0:T(8,128)} %copy-done.4, f32[16,128,256]{2,1,0:T(8,128)} %all-to-all-done.1.x_ref.refs_1_, f32[16,128,256]{2,1,0:T(8,128)} %copy-done.3, ...), custom_call_target="tpu_custom_call" | custom-call | tf_op jit(solution)/shard_map/down_grad/pallas_call | solution.py:327
  517.9 6.4 %up_grad.1 = (f32[64,4,4096]{2,1,0:T(4,128)}, f32[64,4,4,256]{3,2,1,0:T(4,128)}) custom-call(s32[32]{0:T(128)} %select_reduce_fusion.1.order_ref, s32[65]{0:T(128)} %convert_reduce_fusion.2.first_ref, f32[32,4,5120]{2,1,0:T(4,128)} %all-to-all-done.4.refs_0_), custom_call_target="tpu_custom_call" | custom-call | tf_op jit(solution)/shard_map/up_grad/pallas_call | solution.py:376
  524.3 2.5 copy.54
  (118 shorter events, 27.4 us)
Async XLA Ops:
  0.6 120.6 %copy-start = (f32[64,4,4,256]{3,2,1,0:T(4,128)S(1)}, f32[64,4,4,256]{3,2,1,0:T(4,128)}, u32[]{:S(2)}) copy-start(f32[64,4,4,256]{3,2,1,0:T(4,128)} %param.18) | copy-start | bytes 3145732
  6.5 48.8 %all-to-all-start.2 = ((f32[16,128,256]{2,1,0:T(8,128)}), f32[16,128,256]{2,1,0:T(8,128)S(1)}, u32[]{:S(2)}, u32[]{:S(2)}) async-start(f32[16,128,256]{2,1,0:T(8,128)} %bitcast.44), calls=%async_computation.2 | async-start | bytes 4194304 | tf_op jit(solution)/shard_map/all_to_all | solution.py:397
  55.3 13.1 %copy-start.3 = (f32[16,128,256]{2,1,0:T(8,128)}, f32[16,128,256]{2,1,0:T(8,128)S(1)}, u32[]{:S(2)}) copy-start(f32[16,128,256]{2,1,0:T(8,128)S(1)} %all-to-all-done.2.x_ref.refs_2_) | copy-start | bytes 6291460
  55.3 52.4 %all-to-all-start.1 = ((f32[16,128,256]{2,1,0:T(8,128)}), f32[16,128,256]{2,1,0:T(8,128)}, u32[]{:S(2)}, u32[]{:S(2)}) async-start(f32[16,128,256]{2,1,0:T(8,128)} %bitcast.43), calls=%async_computation.1 | async-start | bytes 4194304 | tf_op jit(solution)/shard_map/all_to_all | solution.py:397
  71.0 47.6 %copy-start.11 = (s32[3]{0:T(128)S(1)}, s32[3]{0:T(128)}, u32[]{:S(2)}) copy-start(s32[3]{0:T(128)} %param.20) | copy-start | bytes 40
  71.0 50.0 %copy-start.2 = (s32[16,2]{0,1:T(2,128)S(1)}, s32[16,2]{0,1:T(2,128)}, u32[]{:S(2)}) copy-start(s32[16,2]{0,1:T(2,128)} %param.21) | copy-start | bytes 388
  107.7 52.3 %all-to-all-start = ((f32[16,128,256]{2,1,0:T(8,128)}), f32[16,128,256]{2,1,0:T(8,128)S(1)}, u32[]{:S(2)}, u32[]{:S(2)}) async-start(f32[16,128,256]{2,1,0:T(8,128)} %bitcast.42), calls=%async_computation | async-start | bytes 4194304 | tf_op jit(solution)/shard_map/all_to_all | solution.py:397
  118.6 54.4 %collective-permute-start = (s32[1,3]{1,0:T(1,128)S(1)}, s32[1,3]{1,0:T(1,128)S(1)}, u32[]{:S(2)}, u32[]{:S(2)}) collective-permute-start(s32[1,3]{1,0:T(1,128)S(1)} %bitcast.50), channel_id=1, source_target_pairs={{0,16},{2,18},{4,20},{6,22},{8,24},{10,26},{12,28},{14,30},{16,0},... | collective-permute-start | bytes 44 | tf_op jit(solution)/shard_map/ppermute | solution.py:42
  128.0 4.0 copy-start.9
  160.1 1.4 copy-start.4
  161.5 155.3 %all-to-all-start.3 = ((f32[32,4,5120]{2,1,0:T(4,128)}), f32[32,4,5120]{2,1,0:T(4,128)}, u32[]{:S(2)}, u32[]{:S(2)}) async-start(f32[32,4,5120]{2,1,0:T(4,128)} %reshape.292), calls=%async_computation.3 | async-start | bytes 5242880 | tf_op jit(solution)/shard_map/all_to_all | solution.py:397
  173.1 42.2 %collective-permute-start.1 = (s32[2,3]{1,0:T(2,128)S(1)}, s32[2,3]{1,0:T(2,128)S(1)}, u32[]{:S(2)}, u32[]{:S(2)}) collective-permute-start(s32[2,3]{1,0:T(2,128)S(1)} %pad_add_fusion.2), channel_id=1, source_target_pairs={{0,8},{2,10},{4,12},{6,14},{8,0},{10,2},{12,4},{14,6},{16,24},{18,... | collective-permute-start | bytes 80 | tf_op jit(solution)/shard_map/ppermute | solution.py:42
  215.4 3.6 collective-permute-start.2
  219.0 2.2 collective-permute-start.3
  236.9 28.1 %collective-permute-start.4 = (f32[8,192,128]{2,1,0:T(8,128)S(1)}, f32[8,192,128]{2,1,0:T(8,128)S(1)}, u32[]{:S(2)}, u32[]{:S(2)}) collective-permute-start(f32[8,192,128]{2,1,0:T(8,128)S(1)} %slice.128), channel_id=1, source_target_pairs={{0,2},{2,0},{4,6},{6,4},{8,10},{10,8},{12,14},{14,12},{16,18},{18,... | collective-permute-start | bytes 2359304 | tf_op jit(solution)/shard_map/ppermute | solution.py:42
  250.7 16.1 %collective-permute-start.9 = (f32[8,192,128]{2,1,0:T(8,128)S(1)}, f32[8,192,128]{2,1,0:T(8,128)S(1)}, u32[]{:S(2)}, u32[]{:S(2)}) collective-permute-start(f32[8,192,128]{2,1,0:T(8,128)S(1)} %slice.137), channel_id=1, source_target_pairs={{0,2},{2,0},{4,6},{6,4},{8,10},{10,8},{12,14},{14,12},{16,18},{18,... | collective-permute-start | bytes 2359304 | tf_op jit(solution)/shard_map/ppermute | solution.py:42
  250.9 14.1 %copy-start.8 = (f32[16,192,128]{2,1,0:T(8,128)S(1)}, f32[16,192,128]{2,1,0:T(8,128)}, u32[]{:S(2)}) copy-start(f32[16,192,128]{2,1,0:T(8,128)} %down_partial.3) | copy-start | bytes 4718596
  263.3 3.5 copy-start.7
  264.6 2.4 collective-permute-start.14
  265.1 1.9 copy-start.6
  265.1 10.9 %collective-permute-start.5 = (f32[4,192,128]{2,1,0:T(8,128)S(1)}, f32[4,192,128]{2,1,0:T(8,128)S(1)}, u32[]{:S(2)}, u32[]{:S(2)}) collective-permute-start(f32[4,192,128]{2,1,0:T(8,128)S(1)} %slice.130), channel_id=1, source_target_pairs={{0,4},{2,6},{4,0},{6,2},{8,12},{10,14},{12,8},{14,10},{16,20},{18,... | collective-permute-start | bytes 1179656 | tf_op jit(solution)/shard_map/ppermute | solution.py:42
  266.9 17.6 %collective-permute-start.10 = (f32[4,192,128]{2,1,0:T(8,128)S(1)}, f32[4,192,128]{2,1,0:T(8,128)S(1)}, u32[]{:S(2)}, u32[]{:S(2)}) collective-permute-start(f32[4,192,128]{2,1,0:T(8,128)S(1)} %slice.139), channel_id=1, source_target_pairs={{0,4},{2,6},{4,0},{6,2},{8,12},{10,14},{12,8},{14,10},{16,20},{18,... | collective-permute-start | bytes 1179656 | tf_op jit(solution)/shard_map/ppermute | solution.py:42
  267.2 25.8 %collective-permute-start.15 = (f32[4,192,128]{2,1,0:T(8,128)S(1)}, f32[4,192,128]{2,1,0:T(8,128)S(1)}, u32[]{:S(2)}, u32[]{:S(2)}) collective-permute-start(f32[4,192,128]{2,1,0:T(8,128)S(1)} %slice.148), channel_id=1, source_target_pairs={{0,4},{2,6},{4,0},{6,2},{8,12},{10,14},{12,8},{14,10},{16,20},{18,... | collective-permute-start | bytes 1179656 | tf_op jit(solution)/shard_map/ppermute | solution.py:42
  276.1 19.2 %collective-permute-start.6 = (f32[2,192,128]{2,1,0:T(8,128)S(1)}, f32[2,192,128]{2,1,0:T(8,128)S(1)}, u32[]{:S(2)}, u32[]{:S(2)}) collective-permute-start(f32[2,192,128]{2,1,0:T(8,128)S(1)} %slice.132), channel_id=1, source_target_pairs={{0,8},{2,10},{4,12},{6,14},{8,0},{10,2},{12,4},{14,6},{16,24},{18,... | collective-permute-start | bytes 589832 | tf_op jit(solution)/shard_map/ppermute | solution.py:42
  284.6 28.3 %copy-start.12 = (s32[384]{0:T(512)S(1)}, s32[384]{0:T(512)}, u32[]{:S(2)}) copy-start(s32[384]{0:T(512)} %param.19) | copy-start | bytes 4612
  284.6 11.8 %collective-permute-start.11 = (f32[2,192,128]{2,1,0:T(8,128)S(1)}, f32[2,192,128]{2,1,0:T(8,128)S(1)}, u32[]{:S(2)}, u32[]{:S(2)}) collective-permute-start(f32[2,192,128]{2,1,0:T(8,128)S(1)} %slice.141), channel_id=1, source_target_pairs={{0,8},{2,10},{4,12},{6,14},{8,0},{10,2},{12,4},{14,6},{16,24},{18,... | collective-permute-start | bytes 589832 | tf_op jit(solution)/shard_map/ppermute | solution.py:42
  293.0 10.2 %collective-permute-start.16 = (f32[2,192,128]{2,1,0:T(8,128)S(1)}, f32[2,192,128]{2,1,0:T(8,128)S(1)}, u32[]{:S(2)}, u32[]{:S(2)}) collective-permute-start(f32[2,192,128]{2,1,0:T(8,128)S(1)} %slice.150), channel_id=1, source_target_pairs={{0,8},{2,10},{4,12},{6,14},{8,0},{10,2},{12,4},{14,6},{16,24},{18,... | collective-permute-start | bytes 589832 | tf_op jit(solution)/shard_map/ppermute | solution.py:42
  295.3 8.0 %collective-permute-start.7 = (f32[1,192,128]{2,1,0:T(8,128)S(1)}, f32[1,192,128]{2,1,0:T(8,128)S(1)}, u32[]{:S(2)}, u32[]{:S(2)}) collective-permute-start(f32[1,192,128]{2,1,0:T(8,128)S(1)} %slice.134), channel_id=1, source_target_pairs={{0,16},{2,18},{4,20},{6,22},{8,24},{10,26},{12,28},{14,30},{16,0},... | collective-permute-start | bytes 294920 | tf_op jit(solution)/shard_map/ppermute | solution.py:42
  296.4 8.2 %collective-permute-start.12 = (f32[1,192,128]{2,1,0:T(8,128)S(1)}, f32[1,192,128]{2,1,0:T(8,128)S(1)}, u32[]{:S(2)}, u32[]{:S(2)}) collective-permute-start(f32[1,192,128]{2,1,0:T(8,128)S(1)} %slice.143), channel_id=1, source_target_pairs={{0,16},{2,18},{4,20},{6,22},{8,24},{10,26},{12,28},{14,30},{16,0},... | collective-permute-start | bytes 294920 | tf_op jit(solution)/shard_map/ppermute | solution.py:42
  303.2 8.2 %collective-permute-start.17 = (f32[1,192,128]{2,1,0:T(8,128)S(1)}, f32[1,192,128]{2,1,0:T(8,128)S(1)}, u32[]{:S(2)}, u32[]{:S(2)}) collective-permute-start(f32[1,192,128]{2,1,0:T(8,128)S(1)} %slice.152), channel_id=1, source_target_pairs={{0,16},{2,18},{4,20},{6,22},{8,24},{10,26},{12,28},{14,30},{16,0},... | collective-permute-start | bytes 294920 | tf_op jit(solution)/shard_map/ppermute | solution.py:42
  303.4 11.5 %collective-permute-start.8 = (f32[192,128]{1,0:T(8,128)S(1)}, f32[192,128]{1,0:T(8,128)S(1)}, u32[]{:S(2)}, u32[]{:S(2)}) collective-permute-start(f32[192,128]{1,0:T(8,128)S(1)} %fusion.2), channel_id=1, source_target_pairs={{0,1},{1,0},{2,3},{3,2},{4,5},{5,4},{6,7},{7,6},{8,9},{9,8},{10,11... | collective-permute-start | bytes 294920 | tf_op jit(solution)/shard_map/ppermute | solution.py:42
  304.7 10.8 %collective-permute-start.13 = (f32[192,128]{1,0:T(8,128)S(1)}, f32[192,128]{1,0:T(8,128)S(1)}, u32[]{:S(2)}, u32[]{:S(2)}) collective-permute-start(f32[192,128]{1,0:T(8,128)S(1)} %fusion.1), channel_id=1, source_target_pairs={{0,1},{1,0},{2,3},{3,2},{4,5},{5,4},{6,7},{7,6},{8,9},{9,8},{10,11... | collective-permute-start | bytes 294920 | tf_op jit(solution)/shard_map/ppermute | solution.py:42
  311.5 4.7 collective-permute-start.18
  373.1 7.9 %collective-permute-start.19 = (f32[3,192,128]{2,1,0:T(8,128)}, f32[3,192,128]{2,1,0:T(8,128)S(1)}, u32[]{:S(2)}, u32[]{:S(2)}) collective-permute-start(f32[3,192,128]{2,1,0:T(8,128)} %get-tuple-element.7), channel_id=1, source_target_pairs={{0,1},{1,0},{2,3},{3,2},{4,5},{5,4},{6,7},{7,6},{8,9},{9,8},{10,11... | collective-permute-start | bytes 884744 | tf_op jit(solution)/shard_map/ppermute | solution.py:42
  374.0 7.0 %copy-start.10 = (f32[3,192,128]{2,1,0:T(8,128)S(1)}, f32[3,192,128]{2,1,0:T(8,128)}, u32[]{:S(2)}) copy-start(f32[3,192,128]{2,1,0:T(8,128)} %get-tuple-element.7) | copy-start | bytes 884740
  374.0 143.8 %all-to-all-start.4 = ((f32[32,4,5120]{2,1,0:T(4,128)}), f32[32,4,5120]{2,1,0:T(4,128)}, u32[]{:S(2)}, u32[]{:S(2)}) async-start(f32[32,4,5120]{2,1,0:T(4,128)} %bitcast.48), calls=%async_computation.4 | async-start | bytes 5242880 | tf_op jit(solution)/shard_map/all_to_all | solution.py:397
  381.0 71.5 %collective-permute-start.20 = (f32[1,3,192,128]{3,2,1,0:T(8,128)S(1)}, f32[1,3,192,128]{3,2,1,0:T(8,128)S(1)}, u32[]{:S(2)}, u32[]{:S(2)}) collective-permute-start(f32[1,3,192,128]{3,2,1,0:T(8,128)S(1)} %add_bitcast_fusion), channel_id=1, source_target_pairs={{0,16},{2,18},{4,20},{6,22},{8,24},{10,26},{12,28},{14,30},{16,0},... | collective-permute-start | bytes 884744 | tf_op jit(solution)/shard_map/ppermute | solution.py:42
  452.6 14.0 %collective-permute-start.21 = (f32[2,3,192,128]{3,2,1,0:T(8,128)S(1)}, f32[2,3,192,128]{3,2,1,0:T(8,128)S(1)}, u32[]{:S(2)}, u32[]{:S(2)}) collective-permute-start(f32[2,3,192,128]{3,2,1,0:T(8,128)S(1)} %pad_maximum_fusion.3), channel_id=1, source_target_pairs={{0,8},{2,10},{4,12},{6,14},{8,0},{10,2},{12,4},{14,6},{16,24},{18,... | collective-permute-start | bytes 1769480 | tf_op jit(solution)/shard_map/ppermute | solution.py:42
  466.7 25.8 %collective-permute-start.22 = (f32[4,3,192,128]{3,2,1,0:T(8,128)S(1)}, f32[4,3,192,128]{3,2,1,0:T(8,128)S(1)}, u32[]{:S(2)}, u32[]{:S(2)}) collective-permute-start(f32[4,3,192,128]{3,2,1,0:T(8,128)S(1)} %pad_maximum_fusion.2), channel_id=1, source_target_pairs={{0,4},{2,6},{4,0},{6,2},{8,12},{10,14},{12,8},{14,10},{16,20},{18,... | collective-permute-start | bytes 3538952 | tf_op jit(solution)/shard_map/ppermute | solution.py:42
  492.7 7.1 %copy-start.5 = (f32[8,3,192,128]{3,2,1,0:T(8,128)}, f32[8,3,192,128]{3,2,1,0:T(8,128)S(1)}, u32[]{:S(2)}) copy-start(f32[8,3,192,128]{3,2,1,0:T(8,128)S(1)} %pad_maximum_fusion.1.refs_3_) | copy-start | bytes 7077892
  492.7 7.1 %collective-permute-start.23 = (f32[8,3,192,128]{3,2,1,0:T(8,128)S(1)}, f32[8,3,192,128]{3,2,1,0:T(8,128)}, u32[]{:S(2)}, u32[]{:S(2)}) collective-permute-start(f32[8,3,192,128]{3,2,1,0:T(8,128)S(1)} %pad_maximum_fusion.1.refs_3_), channel_id=1, source_target_pairs={{0,2},{2,0},{4,6},{6,4},{8,10},{10,8},{12,14},{14,12},{16,18},{18,... | collective-permute-start | bytes 7077896 | tf_op jit(solution)/shard_map/ppermute | solution.py:42
  499.7 27.0 %copy-start.1 = (f32[64,4,4,256]{3,2,1,0:T(4,128)S(1)}, f32[64,4,4,256]{3,2,1,0:T(4,128)}, u32[]{:S(2)}) copy-start(f32[64,4,4,256]{3,2,1,0:T(4,128)} %param.18) | copy-start | bytes 3145732

commit v2 on v1

--- a/solution.py
+++ b/solution.py
@@ -14,7 +14,13 @@
 NN = (((1,), (0,)), ((), ()))
 NT = (((1,), (1,)), ((), ()))
 TN = (((0,), (0,)), ((), ()))
-HEADS_PER_CALL = 4
+HEADS_PER_CALL = 2
+
+
+def cost(micros):
+    return pl.CostEstimate(
+        flops=int(micros * 1e9), bytes_accessed=int(micros * 3.6e6), transcendentals=0
+    )
 
 
 def split2(a):
@@ -59,13 +65,25 @@
     return part[0]
 
 
-def gather_halves(a, axis, size):
+def gather_far(a, axis, size, stop):
     a = a[None]
     bit = size // 2
+    while bit > stop:
+        a = jnp.concatenate([a, swap(a, axis, size, bit)], axis=0)
+        bit //= 2
+    return a
+
+
+def gather_near(a, axis, size, start):
+    bit = start
     while bit > 1:
         a = jnp.concatenate([a, swap(a, axis, size, bit)], axis=0)
         bit //= 2
     return a, swap(a, axis, size, 1)
+
+
+def after(a, *others):
+    return lax.optimization_barrier((a,) + others)[0]
 
 
 def by_tenant(owners, tenants):
@@ -83,30 +101,38 @@
     return order.astype(jnp.int32), first.astype(jnp.int32)
 
 
-def down_kernel(source_ref, tenant_ref, x_ref, w_ref, out_ref):
-    x = x_ref[0].astype(BF16)
-    high, low = split2(w_ref[0])
-    out_ref[0] = mm(high, x, NT) + mm(low, x, NT)
-
-
-def down_partial(x, weights, source, tenant):
-    n, rows, width = x.shape
+def down_kernel(count, source_ref, tenant_ref, *refs):
+    x_refs, w_refs, out_ref = refs[:count], refs[count : 2 * count], refs[2 * count]
+    for c in range(count):
+        x = x_refs[c][0].astype(BF16)
+        high, low = split2(w_refs[c][0])
+        out_ref[c] = mm(high, x, NT) + mm(low, x, NT)
+
+
+def down_partial(x, weights, source, tenant, rows):
+    n, _, width = x.shape
     rank = weights.shape[1]
+    count = 4
+
+    def x_spec(c):
+        return pl.BlockSpec((1, rows, width), lambda p, s, t: (s[p * count + c], 0, 0))
+
+    def w_spec(c):
+        return pl.BlockSpec((1, rank, width), lambda p, s, t: (t[p * count + c], 0, 0))
+
     return pl.pallas_call(
-        down_kernel,
+        functools.partial(down_kernel, count),
         grid_spec=pltpu.PrefetchScalarGridSpec(
             num_scalar_prefetch=2,
-            grid=(n,),
-            in_specs=[
-                pl.BlockSpec((1, rows, width), lambda p, s, t: (s[p], 0, 0)),
-                pl.BlockSpec((1, rank, width), lambda p, s, t: (t[p], 0, 0)),
-            ],
-            out_specs=pl.BlockSpec((1, rank, rows), lambda p, s, t: (p, 0, 0)),
+            grid=(n // count,),
+            in_specs=[x_spec(c) for c in range(count)] + [w_spec(c) for c in range(count)],
+            out_specs=pl.BlockSpec((count, rank, rows), lambda p, s, t: (p, 0, 0)),
         ),
         out_shape=jax.ShapeDtypeStruct((n, rank, rows), F32),
         compiler_params=pltpu.CompilerParams(vmem_limit_bytes=VMEM_LIMIT),
+        cost_estimate=cost(6),
         name="down_partial",
-    )(source, tenant, x, weights)
+    )(source, tenant, *[x] * count, *[weights] * count)
 
 
 def attention_kernel(
@@ -279,6 +305,7 @@
             pltpu.VMEM((head, rows), F32),
         ],
         compiler_params=pltpu.CompilerParams(vmem_limit_bytes=VMEM_LIMIT),
+        cost_estimate=cost(15 * heads),
         name="attention_grads",
     )(fq, fk, fv, up, *lows, panels, slot_rows, docs[None, :], docs[:, None])
 
@@ -291,7 +318,10 @@
     @pl.when(step == 0)
     def _():
         copies = [
-            pltpu.make_async_copy(x_refs[b], x_all.at[b], sems.at[b]) for b in range(blocks)
+            pltpu.make_async_copy(
+                x_refs[b].at[:, pl.ds(0, x_all.shape[2])], x_all.at[b], sems.at[b]
+            )
+            for b in range(blocks)
         ] + [
             pltpu.make_async_copy(
                 ref, g_ref.at[pl.ds(side * half, half)], sems.at[blocks + side]
@@ -321,7 +351,7 @@
 
 def down_grad(xs, g, order, first, source, tenants):
     blocks = len(xs)
-    n, rows, width = xs[0].shape
+    n, rows, width = xs[1].shape
     rank = g[0].shape[2]
     per_step = 8
     return pl.pallas_call(
@@ -339,6 +369,7 @@
         ),
         out_shape=jax.ShapeDtypeStruct((tenants, rank, width), F32),
         compiler_params=pltpu.CompilerParams(vmem_limit_bytes=VMEM_LIMIT),
+        cost_estimate=cost(15),
         name="down_grad",
     )(order, first, source, *xs, *g)
 
@@ -389,6 +420,7 @@
             jax.ShapeDtypeStruct((tenants, kv_heads, piece, 2 * head), F32),
         ],
         compiler_params=pltpu.CompilerParams(vmem_limit_bytes=VMEM_LIMIT),
+        cost_estimate=cost(6),
         name="up_grad",
     )(order, first, *dus)
 
@@ -423,21 +455,32 @@
     wide = adapter_up_query.shape[2] // kv_heads
     me = lax.axis_index("dp").astype(jnp.int32)
 
-    xs = [
-        exchange(
-            normed_input_rows[b * block : (b + 1) * block]
-            .reshape(block, dp_count, width)
-            .transpose(1, 0, 2)
-            .astype(F32)
-        )
+    wires = [
+        normed_input_rows[b * block : (b + 1) * block]
+        .reshape(block, dp_count, width)
+        .transpose(1, 0, 2)
+        .astype(F32)
         for b in range(blocks)
     ]
+    slot_tile = jnp.zeros((8, width), F32).at[0, :blocks].set(block_tenant_slot.astype(F32))
+    wires[0] = jnp.concatenate(
+        [wires[0], jnp.broadcast_to(slot_tile[None], (dp_count, 8, width))], axis=1
+    )
+    xs = [exchange(wires[0])]
+    for b in range(1, blocks):
+        xs.append(exchange(after(wires[b], xs[-1])))
 
     source = me ^ bit_reverse(
         jnp.arange(dp_count, dtype=jnp.int32), dp_count.bit_length() - 1
     )
-    slots_all = jnp.concatenate(gather_halves(block_tenant_slot, "dp", dp_count), axis=0)
+    slots_all = xs[0][:, block, :blocks].astype(jnp.int32)[source]
     owners = shard_tenant_table[source[:, None], slots_all]
+
+    weights = jnp.swapaxes(adapter_down_weight, 1, 2)
+    lows = []
+    for b in range(blocks):
+        part = down_partial(xs[b], weights, source, owners[:, b], block)
+        lows.append(sum_over(scatter_sum(part, "dp", dp_count), "mp", mp_count))
 
     wanted = shard_tenant_table.reshape(-1)
     up_query = adapter_up_query[wanted].reshape(-1, piece, kv_heads, wide)
@@ -446,18 +489,11 @@
     heads = min(HEADS_PER_CALL, kv_heads)
     calls = kv_heads // heads
     per = wide + 2 * head
-    panels = [
-        exchange(
-            wire[:, :, c * heads : (c + 1) * heads].reshape(-1, piece, heads * per)
-        ).reshape(dp_count, slots, piece, heads * per)
-        for c in range(calls)
-    ]
-
-    weights = jnp.swapaxes(adapter_down_weight, 1, 2)
-    lows = []
-    for b in range(blocks):
-        part = down_partial(xs[b], weights, source, owners[:, b])
-        lows.append(sum_over(scatter_sum(part, "dp", dp_count), "mp", mp_count))
+    panels = []
+    for c in range(calls):
+        own = wire[:, :, c * heads : (c + 1) * heads].reshape(-1, piece, heads * per)
+        own = after(own, xs[-1]) if c == 0 else after(own, panels[-1], lows[-1])
+        panels.append(exchange(own).reshape(dp_count, slots, piece, heads * per))
 
     slot_rows = jnp.repeat(block_tenant_slot, block)[None, :]
     dus, g = [], None
@@ -475,10 +511,13 @@
             c * heads,
             heads,
         )
-        dus.append(exchange(du.reshape(dp_count * slots, piece, heads * per)))
         g = g_part if g is None else g + g_part
-
-    g_halves = gather_halves(sum_over(g, "mp", mp_count), "dp", dp_count)
+        dus.append(du.reshape(dp_count * slots, piece, heads * per))
+    for c in range(calls - 1):
+        dus[c] = exchange(dus[c])
+    far = gather_far(sum_over(after(g, *dus[:-1]), "mp", mp_count), "dp", dp_count, 2)
+    dus[-1] = exchange(after(dus[-1], far))
+    g_halves = gather_near(far, "dp", dp_count, 2)
     order, first = by_tenant(owners.reshape(-1), tenants)
     grad_down = down_grad(xs, g_halves, order, first, source, tenants)
     order, first = by_tenant(wanted, tenants)

time: 529 us -> 438 us (0.83)
  waiting for transfers between devices: 278 us -> 171 us
  Pallas kernels: 117 us -> 101 us
  starting transfers between devices: 76.9 us -> 91.2 us
  local copies, waits for them, and re-layouts: 43.6 us -> 54.2 us
  other arithmetic: 10.2 us -> 18 us
    ppermute x24 -> x20, waiting for transfers between devices: 185 us -> 95.2 us  [swap(): return lax.ppermute(a, axis, [(i, i ^ bit) for i in range(size)])]
    pallas_call x3, Pallas kernels: 36.7 us -> 17.3 us  [down_partial(): pl.pallas_call(functools.partial(down_kernel, count), grid_spec=pltpu.Pre...]
    all_to_all x5 -> x7, waiting for transfers between devices: 93 us -> 75.6 us  [exchange(): return lax.all_to_all(a, 'dp', split_axis=0, concat_axis=0, tiled=True)]
    all_to_all x5 -> x7, starting transfers between devices: 46.2 us -> 56.7 us  [exchange(): return lax.all_to_all(a, 'dp', split_axis=0, concat_axis=0, tiled=True)]
    unnamed x33 -> x42, local copies, waits for them, and re-layouts: 9.87 us -> 15.4 us
    ppermute x24 -> x20, starting transfers between devices: 30.7 us -> 34.6 us  [swap(): return lax.ppermute(a, axis, [(i, i ^ bit) for i in range(size)])]
    pallas_call x1 -> x2, Pallas kernels: 56.2 us -> 59.3 us  [attention(): pl.pallas_call(functools.partial(attention_kernel, groups, blocks, slots)...]
  transfers between devices with their start and end apart: 29 -> 27, of which waited for: 16 -> 12; matrix products, arithmetic and copies ran while one was open for 8% -> 14% of each run, Pallas kernels for 10% -> 19%
where the time goes in v2:
time: 438 us; the launch traced here: 437 us
  waiting for transfers between devices  171 us (39%)
  Pallas kernels  101 us (23%)
  starting transfers between devices  91.2 us (21%)
  local copies, waits for them, and re-layouts  54.2 us (12%)
  other arithmetic  18 us (4%)
    ppermute x20, waiting for transfers between devices, swap(): return lax.ppermute(a, axis, [(i, i ^ bit) for i in range(size)])  95.2 us
    all_to_all x7, waiting for transfers between devices, exchange(): return lax.all_to_all(a, 'dp', split_axis=0, concat_axis=0, tiled=True)  75.6 us
    pallas_call x2, Pallas kernels, attention(): pl.pallas_call(functools.partial(attention_kernel, groups, blocks, slots)...  59.3 us
    all_to_all x7, starting transfers between devices, exchange(): return lax.all_to_all(a, 'dp', split_axis=0, concat_axis=0, tiled=True)  56.7 us
    ppermute x20, starting transfers between devices, swap(): return lax.ppermute(a, axis, [(i, i ^ bit) for i in range(size)])  34.6 us
    pallas_call x1, Pallas kernels, down_grad(): pl.pallas_call(functools.partial(down_grad_kernel, blocks, per_step), gri...  18.2 us
    pallas_call x3, Pallas kernels, down_partial(): pl.pallas_call(functools.partial(down_kernel, count), grid_spec=pltpu.Pre...  17.3 us
    unnamed x42, local copies, waits for them, and re-layouts  15.4 us
  transfers between devices with their start and end apart: 27, of which 12 were waited for; matrix products, arithmetic and copies ran while one was open for 14% of the time, Pallas kernels for 19%

profile of v2, /device:TPU:1, one launch (start us, length us, event | category | flops | bytes accessed | tf_op | source)
XLA Modules:
  0.0 436.7 jit_solution(12871230375809791204)
XLA Ops:
  1.4 3.5 fusion.38
  7.7 1.6 pad_maximum_fusion.1
  9.3 7.3 %all-to-all-start = ((f32[16,136,256]{2,1,0:T(8,128)}), f32[16,136,256]{2,1,0:T(8,128)S(1)}, u32[]{:S(2)}, u32[]{:S(2)}) async-start(f32[16,136,256]{2,1,0:T(8,128)} %pad_maximum_fusion.1), calls=%async_computation | async-start | bytes 4456448 | tf_op jit(solution)/shard_map/all_to_all | solution.py:429
  16.6 2.3 copy.68
  18.9 2.6 copy.58
  21.4 38.9 %all-to-all-done.refs_0_.refs_1_.refs_2_.refs_3_ = f32[16,136,256]{2,1,0:T(8,128)S(1)} async-done(((f32[16,136,256]{2,1,0:T(8,128)}), f32[16,136,256]{2,1,0:T(8,128)S(1)}, u32[]{:S(2)}, u32[]{:S(2)}) %all-to-all-start) | async-done | bytes 2228256 | tf_op jit(solution)/shard_map/all_to_all | solution.py:429
  60.3 11.4 %all-to-all-start.1 = ((f32[16,128,256]{2,1,0:T(8,128)}), f32[16,128,256]{2,1,0:T(8,128)}, u32[]{:S(2)}, u32[]{:S(2)}) async-start(f32[16,128,256]{2,1,0:T(8,128)} %bitcast.54), calls=%async_computation.1 | async-start | bytes 4194304 | tf_op jit(solution)/shard_map/all_to_all | solution.py:429
  71.7 2.3 copy.69
  74.0 2.6 copy.60
  76.6 36.7 %all-to-all-done.1.refs_0_.refs_1_.refs_2_.refs_3_ = f32[16,128,256]{2,1,0:T(8,128)} async-done(((f32[16,128,256]{2,1,0:T(8,128)}), f32[16,128,256]{2,1,0:T(8,128)}, u32[]{:S(2)}, u32[]{:S(2)}) %all-to-all-start.1) | async-done | bytes 2097184 | tf_op jit(solution)/shard_map/all_to_all | solution.py:429
  113.3 11.0 %all-to-all-start.2 = ((f32[16,128,256]{2,1,0:T(8,128)}), f32[16,128,256]{2,1,0:T(8,128)}, u32[]{:S(2)}, u32[]{:S(2)}) async-start(f32[16,128,256]{2,1,0:T(8,128)} %bitcast.53), calls=%async_computation.2 | async-start | bytes 4194304 | tf_op jit(solution)/shard_map/all_to_all | solution.py:429
  127.7 5.8 %down_partial.3 = f32[16,192,128]{2,1,0:T(8,128)} custom-call(s32[16]{0:T(128)} %fusion.19.source_ref, s32[16]{0:T(128)} %get-tuple-element.52.tenant_ref, f32[16,136,256]{2,1,0:T(8,128)} %copy-done.3, f32[16,136,256]{2,1,0:T(8,128)} %copy-done.3, f32[16,136,256]{2,1,0:T(8,128)} %copy-done.3, f32[16,136,256]{2,1,0:T(8,128)} %copy-done.3, ...), custom_call_target="tpu_custom_call" | custom-call | flops 6000000000 | bytes 21600000 | tf_op jit(solution)/shard_map/down_partial/pallas_call | solution.py:123
  133.5 2.2 slice.159
  136.0 2.3 collective-permute-done
  141.9 1.6 gather_fusion.3
  143.5 4.0 gather_fusion.2
  147.5 2.8 reshape.200
  150.3 3.3 constant_dynamic-update-slice_fusion.1
  154.5 3.5 collective-permute-done.1
  160.5 5.8 %down_partial.4 = f32[16,192,128]{2,1,0:T(8,128)} custom-call(s32[16]{0:T(128)} %fusion.19.source_ref, s32[16]{0:T(128)} %get-tuple-element.53.tenant_ref, f32[16,128,256]{2,1,0:T(8,128)} %all-to-all-done.1.refs_0_.refs_1_.refs_2_.refs_3_, f32[16,128,256]{2,1,0:T(8,128)} %all-to-all-done.1.refs_0_.refs_1_.refs_2_.refs_3_, ...), custom_call_target="tpu_custom_call" | custom-call | flops 6000000000 | bytes 21600000 | tf_op jit(solution)/shard_map/down_partial/pallas_call | solution.py:123
  168.3 5.8 %down_partial.5 = f32[16,192,128]{2,1,0:T(8,128)} custom-call(s32[16]{0:T(128)} %fusion.19.source_ref, s32[16]{0:T(128)} %get-tuple-element.51.tenant_ref, f32[16,128,256]{2,1,0:T(8,128)} %all-to-all-done.2.refs_0_.refs_1_.refs_2_.refs_3_, f32[16,128,256]{2,1,0:T(8,128)} %all-to-all-done.2.refs_0_.refs_1_.refs_2_.refs_3_, ...), custom_call_target="tpu_custom_call" | custom-call | flops 6000000000 | bytes 21600000 | tf_op jit(solution)/shard_map/down_partial/pallas_call | solution.py:123
  174.1 2.1 slice.177
  176.2 4.9 %fusion.39 = (f32[32,4,2,1280]{3,2,1,0:T(2,128)}, f32[32,4,2,1280]{3,2,1,0:T(2,128)S(1)}) fusion(f32[32,4,4,1280]{3,2,1,0:T(4,128)} %constant_dynamic-update-slice_fusion), kind=kLoop, calls=%fused_computation.95 | loop fusion | bytes 5242880 | tf_op jit(solution)/shard_map/slice | solution.py:494
  181.1 2.3 reshape.201
  183.5 6.5 %collective-permute-start.3 = (f32[1,192,128]{2,1,0:T(8,128)S(1)}, f32[1,192,128]{2,1,0:T(8,128)S(1)}, u32[]{:S(2)}, u32[]{:S(2)}) collective-permute-start(f32[1,192,128]{2,1,0:T(8,128)S(1)} %slice.165), channel_id=1, source_target_pairs={{0,16},{2,18},{4,20},{6,22},{8,24},{10,26},{12,28},{14,30},{16,0},... | collective-permute-start | bytes 294920 | tf_op jit(solution)/shard_map/ppermute | solution.py:48
  190.0 4.5 %all-to-all-start.3 = ((f32[32,4,2560]{2,1,0:T(4,128)}), f32[32,4,2560]{2,1,0:T(4,128)}, u32[]{:S(2)}, u32[]{:S(2)}) async-start(f32[32,4,2560]{2,1,0:T(4,128)} %reshape.201), calls=%async_computation.3 | async-start | bytes 2621440 | tf_op jit(solution)/shard_map/all_to_all | solution.py:429
  200.1 15.6 %collective-permute-done.6 = f32[4,192,128]{2,1,0:T(8,128)S(1)} collective-permute-done((f32[4,192,128]{2,1,0:T(8,128)S(1)}, f32[4,192,128]{2,1,0:T(8,128)S(1)}, u32[]{:S(2)}, u32[]{:S(2)}) %collective-permute-start.6) | collective-permute-done | bytes 393248 | tf_op jit(solution)/shard_map/ppermute | solution.py:48
  216.7 10.9 %collective-permute-done.11 = f32[4,192,128]{2,1,0:T(8,128)S(1)} collective-permute-done((f32[4,192,128]{2,1,0:T(8,128)S(1)}, f32[4,192,128]{2,1,0:T(8,128)S(1)}, u32[]{:S(2)}, u32[]{:S(2)}) %collective-permute-start.11) | collective-permute-done | bytes 393248 | tf_op jit(solution)/shard_map/ppermute | solution.py:48
  229.0 2.2 collective-permute-start.8
  231.2 3.1 collective-permute-done.12
  234.4 1.7 collective-permute-start.13
  237.5 1.9 collective-permute-done.13
  242.8 2.3 reshape.203
  247.1 8.4 %all-to-all-start.4 = ((f32[32,4,2560]{2,1,0:T(4,128)}), f32[32,4,2560]{2,1,0:T(4,128)S(1)}, u32[]{:S(2)}, u32[]{:S(2)}) async-start(f32[32,4,2560]{2,1,0:T(4,128)} %reshape.203), calls=%async_computation.4 | async-start | bytes 2621440 | tf_op jit(solution)/shard_map/all_to_all | solution.py:429
  255.4 29.7 %attention_grads.2 = (f32[16,2,4,2560]{3,2,1,0:T(4,128)}, f32[3,192,128]{2,1,0:T(8,128)}) custom-call(bf16[384,4096]{1,0:T(8,128)(2,1)} %fq_ref.3, bf16[384,512]{1,0:T(8,128)(2,1)} %fk_ref.3, bf16[384,512]{1,0:T(8,128)(2,1)} %fv_ref.3, bf16[384,4096]{1,0:T(8,128)(2,1)} %up_ref.3, f32[192,128]{1,0:T(8,128)} %add.103.rest_0_, f32[192,128]{1,0:T(8,128)} %add.108.rest_1_, ...), custom_call_target="tpu_custom_call" | custom-call | flops 30000001024 | bytes 108000000 | tf_op jit(solution)/shard_map/attention_grads/pallas_call | solution.py:269
  286.2 6.0 %all-to-all-start.5 = ((f32[32,4,2560]{2,1,0:T(4,128)}), f32[32,4,2560]{2,1,0:T(4,128)S(1)}, u32[]{:S(2)}, u32[]{:S(2)}) async-start(f32[32,4,2560]{2,1,0:T(4,128)} %bitcast.61), calls=%async_computation.5 | async-start | bytes 2621440 | tf_op jit(solution)/shard_map/all_to_all | solution.py:429
  292.2 29.7 %attention_grads.3 = (f32[16,2,4,2560]{3,2,1,0:T(4,128)}, f32[3,192,128]{2,1,0:T(8,128)}) custom-call(bf16[384,4096]{1,0:T(8,128)(2,1)} %fq_ref.3, bf16[384,512]{1,0:T(8,128)(2,1)} %fk_ref.3, bf16[384,512]{1,0:T(8,128)(2,1)} %fv_ref.3, bf16[384,4096]{1,0:T(8,128)(2,1)} %up_ref.3, f32[192,128]{1,0:T(8,128)} %add.103.rest_0_, f32[192,128]{1,0:T(8,128)} %add.108.rest_1_, ...), custom_call_target="tpu_custom_call" | custom-call | flops 30000001024 | bytes 108000000 | tf_op jit(solution)/shard_map/attention_grads/pallas_call | solution.py:269
  323.2 8.3 %collective-permute-done.15 = f32[3,192,128]{2,1,0:T(8,128)S(1)} collective-permute-done((f32[3,192,128]{2,1,0:T(8,128)S(1)}, f32[3,192,128]{2,1,0:T(8,128)S(1)}, u32[]{:S(2)}, u32[]{:S(2)}) %collective-permute-start.15) | collective-permute-done | bytes 294944 | tf_op jit(solution)/shard_map/ppermute | solution.py:48
  331.5 2.1 collective-permute-start.16
  333.6 13.2 %collective-permute-done.16 = f32[1,3,192,128]{3,2,1,0:T(8,128)S(1)} collective-permute-done((f32[1,3,192,128]{3,2,1,0:T(8,128)S(1)}, f32[1,3,192,128]{3,2,1,0:T(8,128)S(1)}, u32[]{:S(2)}, u32[]{:S(2)}) %collective-permute-start.16) | collective-permute-done | bytes 294944 | tf_op jit(solution)/shard_map/ppermute | solution.py:48
  347.9 12.4 %collective-permute-done.17 = f32[2,3,192,128]{3,2,1,0:T(8,128)S(1)} collective-permute-done((f32[2,3,192,128]{3,2,1,0:T(8,128)S(1)}, f32[2,3,192,128]{3,2,1,0:T(8,128)S(1)}, u32[]{:S(2)}, u32[]{:S(2)}) %collective-permute-start.17) | collective-permute-done | bytes 589856 | tf_op jit(solution)/shard_map/ppermute | solution.py:48
  362.5 8.1 %all-to-all-start.6 = ((f32[32,4,2560]{2,1,0:T(4,128)}), f32[32,4,2560]{2,1,0:T(4,128)S(1)}, u32[]{:S(2)}, u32[]{:S(2)}) async-start(f32[32,4,2560]{2,1,0:T(4,128)} %bitcast.59), calls=%async_computation.6 | async-start | bytes 2621440 | tf_op jit(solution)/shard_map/all_to_all | solution.py:429
  370.6 23.8 %collective-permute-done.18 = f32[4,3,192,128]{3,2,1,0:T(8,128)} collective-permute-done((f32[4,3,192,128]{3,2,1,0:T(8,128)}, f32[4,3,192,128]{3,2,1,0:T(8,128)}, u32[]{:S(2)}, u32[]{:S(2)}) %collective-permute-start.18) | collective-permute-done | bytes 1179680 | tf_op jit(solution)/shard_map/ppermute | solution.py:48
  394.4 2.9 pad_maximum_fusion.refs_3_
  397.3 8.0 %collective-permute-start.19 = (f32[8,3,192,128]{3,2,1,0:T(8,128)}, f32[8,3,192,128]{3,2,1,0:T(8,128)}, u32[]{:S(2)}, u32[]{:S(2)}) collective-permute-start(f32[8,3,192,128]{3,2,1,0:T(8,128)} %pad_maximum_fusion.refs_3_), channel_id=1, source_target_pairs={{0,2},{2,0},{4,6},{6,4},{8,10},{10,8},{12,14},{14,12},{16,18},{18,... | collective-permute-start | bytes 7077896 | tf_op jit(solution)/shard_map/ppermute | solution.py:48
  409.4 6.4 %up_grad.1 = (f32[64,4,4096]{2,1,0:T(4,128)}, f32[64,4,4,256]{3,2,1,0:T(4,128)}) custom-call(s32[32]{0:T(128)} %select_reduce_fusion.1.order_ref, s32[65]{0:T(128)} %convert_reduce_fusion.2.first_ref, f32[32,4,2560]{2,1,0:T(4,128)} %copy-done.11, f32[32,4,2560]{2,1,0:T(4,128)} %copy-done.12), custom_call_target="tpu_custom_call" | custom-call | flops 6000000000 | bytes 21600000 | tf_op jit(solution)/shard_map/up_grad/pallas_call | solution.py:407
  415.8 2.5 copy.65
  418.3 18.2 %down_grad.1 = f32[64,192,256]{2,1,0:T(8,128)} custom-call(s32[48]{0:T(128)} %select_reduce_fusion.order_ref, s32[65]{0:T(128)} %convert_reduce_fusion.first_ref, s32[16]{0:T(128)} %fusion.19.source_ref, f32[16,136,256]{2,1,0:T(8,128)} %copy-done.3, f32[16,128,256]{2,1,0:T(8,128)} %all-to-all-done.1.refs_0_.refs_1_.refs_2_.refs_3_, ...), custom_call_target="tpu_custom_call" | custom-call | flops 15000000512 | bytes 54000000 | tf_op jit(solution)/shard_map/down_grad/pallas_call | solution.py:357
  (127 shorter events, 40.6 us)
Async XLA Ops:
  0.6 141.3 %copy-start = (f32[64,4,4,256]{3,2,1,0:T(4,128)S(1)}, f32[64,4,4,256]{3,2,1,0:T(4,128)}, u32[]{:S(2)}) copy-start(f32[64,4,4,256]{3,2,1,0:T(4,128)} %param.20) | copy-start | bytes 3145732
  9.3 51.1 %all-to-all-start = ((f32[16,136,256]{2,1,0:T(8,128)}), f32[16,136,256]{2,1,0:T(8,128)S(1)}, u32[]{:S(2)}, u32[]{:S(2)}) async-start(f32[16,136,256]{2,1,0:T(8,128)} %pad_maximum_fusion.1), calls=%async_computation | async-start | bytes 4456448 | tf_op jit(solution)/shard_map/all_to_all | solution.py:429
  60.3 64.6 %copy-start.3 = (f32[16,136,256]{2,1,0:T(8,128)}, f32[16,136,256]{2,1,0:T(8,128)S(1)}, u32[]{:S(2)}) copy-start(f32[16,136,256]{2,1,0:T(8,128)S(1)} %all-to-all-done.refs_0_.refs_1_.refs_2_.refs_3_) | copy-start | bytes 6684676
  60.3 53.0 %all-to-all-start.1 = ((f32[16,128,256]{2,1,0:T(8,128)}), f32[16,128,256]{2,1,0:T(8,128)}, u32[]{:S(2)}, u32[]{:S(2)}) async-start(f32[16,128,256]{2,1,0:T(8,128)} %bitcast.54), calls=%async_computation.1 | async-start | bytes 4194304 | tf_op jit(solution)/shard_map/all_to_all | solution.py:429
  113.3 12.5 %copy-start.2 = (s32[16,2]{0,1:T(2,128)S(1)}, s32[16,2]{0,1:T(2,128)}, u32[]{:S(2)}) copy-start(s32[16,2]{0,1:T(2,128)} %param.23) | copy-start | bytes 388
  113.3 55.0 %all-to-all-start.2 = ((f32[16,128,256]{2,1,0:T(8,128)}), f32[16,128,256]{2,1,0:T(8,128)}, u32[]{:S(2)}, u32[]{:S(2)}) async-start(f32[16,128,256]{2,1,0:T(8,128)} %bitcast.53), calls=%async_computation.2 | async-start | bytes 4194304 | tf_op jit(solution)/shard_map/all_to_all | solution.py:429
  133.5 4.8 %copy-start.6 = (f32[16,192,128]{2,1,0:T(8,128)S(1)}, f32[16,192,128]{2,1,0:T(8,128)}, u32[]{:S(2)}) copy-start(f32[16,192,128]{2,1,0:T(8,128)} %down_partial.3) | copy-start | bytes 4718596
  135.7 2.6 collective-permute-start
  139.5 0.9 copy-start.8
  140.4 17.5 %collective-permute-start.1 = (f32[4,192,128]{2,1,0:T(8,128)S(1)}, f32[4,192,128]{2,1,0:T(8,128)}, u32[]{:S(2)}, u32[]{:S(2)}) collective-permute-start(f32[4,192,128]{2,1,0:T(8,128)S(1)} %slice.161), channel_id=1, source_target_pairs={{0,4},{2,6},{4,0},{6,2},{8,12},{10,14},{12,8},{14,10},{16,20},{18,... | collective-permute-start | bytes 1179656 | tf_op jit(solution)/shard_map/ppermute | solution.py:48
  150.3 3.3 copy-start.10
  150.3 7.6 %copy-start.9 = (f32[8,192,128]{2,1,0:T(8,128)S(1)}, f32[8,192,128]{2,1,0:T(8,128)}, u32[]{:S(2)}) copy-start(f32[8,192,128]{2,1,0:T(8,128)} %copy-done.8) | copy-start | bytes 2359300
  159.0 24.4 %collective-permute-start.2 = (f32[2,192,128]{2,1,0:T(8,128)S(1)}, f32[2,192,128]{2,1,0:T(8,128)S(1)}, u32[]{:S(2)}, u32[]{:S(2)}) collective-permute-start(f32[2,192,128]{2,1,0:T(8,128)S(1)} %slice.163), channel_id=1, source_target_pairs={{0,8},{2,10},{4,12},{6,14},{8,0},{10,2},{12,4},{14,6},{16,24},{18,... | collective-permute-start | bytes 589832 | tf_op jit(solution)/shard_map/ppermute | solution.py:48
  167.4 27.0 %collective-permute-start.5 = (f32[8,192,128]{2,1,0:T(8,128)S(1)}, f32[8,192,128]{2,1,0:T(8,128)}, u32[]{:S(2)}, u32[]{:S(2)}) collective-permute-start(f32[8,192,128]{2,1,0:T(8,128)S(1)} %slice.168), channel_id=1, source_target_pairs={{0,2},{2,0},{4,6},{6,4},{8,10},{10,8},{12,14},{14,12},{16,18},{18,... | collective-permute-start | bytes 2359304 | tf_op jit(solution)/shard_map/ppermute | solution.py:48
  176.1 21.1 %collective-permute-start.10 = (f32[8,192,128]{2,1,0:T(8,128)}, f32[8,192,128]{2,1,0:T(8,128)}, u32[]{:S(2)}, u32[]{:S(2)}) collective-permute-start(f32[8,192,128]{2,1,0:T(8,128)} %slice.177), channel_id=1, source_target_pairs={{0,2},{2,0},{4,6},{6,4},{8,10},{10,8},{12,14},{14,12},{16,18},{18,... | collective-permute-start | bytes 2359304 | tf_op jit(solution)/shard_map/ppermute | solution.py:48
  183.4 11.1 %copy-start.4 = (f32[16,192,128]{2,1,0:T(8,128)S(1)}, f32[16,192,128]{2,1,0:T(8,128)}, u32[]{:S(2)}) copy-start(f32[16,192,128]{2,1,0:T(8,128)} %down_partial.4) | copy-start | bytes 4718596
  183.5 15.3 %collective-permute-start.3 = (f32[1,192,128]{2,1,0:T(8,128)S(1)}, f32[1,192,128]{2,1,0:T(8,128)S(1)}, u32[]{:S(2)}, u32[]{:S(2)}) collective-permute-start(f32[1,192,128]{2,1,0:T(8,128)S(1)} %slice.165), channel_id=1, source_target_pairs={{0,16},{2,18},{4,20},{6,22},{8,24},{10,26},{12,28},{14,30},{16,0},... | collective-permute-start | bytes 294920 | tf_op jit(solution)/shard_map/ppermute | solution.py:48
  190.0 57.1 %all-to-all-start.3 = ((f32[32,4,2560]{2,1,0:T(4,128)}), f32[32,4,2560]{2,1,0:T(4,128)}, u32[]{:S(2)}, u32[]{:S(2)}) async-start(f32[32,4,2560]{2,1,0:T(4,128)} %reshape.201), calls=%async_computation.3 | async-start | bytes 2621440 | tf_op jit(solution)/shard_map/all_to_all | solution.py:429
  194.4 2.8 copy-start.5
  195.8 19.9 %collective-permute-start.6 = (f32[4,192,128]{2,1,0:T(8,128)S(1)}, f32[4,192,128]{2,1,0:T(8,128)S(1)}, u32[]{:S(2)}, u32[]{:S(2)}) collective-permute-start(f32[4,192,128]{2,1,0:T(8,128)S(1)} %slice.170), channel_id=1, source_target_pairs={{0,4},{2,6},{4,0},{6,2},{8,12},{10,14},{12,8},{14,10},{16,20},{18,... | collective-permute-start | bytes 1179656 | tf_op jit(solution)/shard_map/ppermute | solution.py:48
  198.5 29.1 %collective-permute-start.11 = (f32[4,192,128]{2,1,0:T(8,128)S(1)}, f32[4,192,128]{2,1,0:T(8,128)S(1)}, u32[]{:S(2)}, u32[]{:S(2)}) collective-permute-start(f32[4,192,128]{2,1,0:T(8,128)S(1)} %slice.179), channel_id=1, source_target_pairs={{0,4},{2,6},{4,0},{6,2},{8,12},{10,14},{12,8},{14,10},{16,20},{18,... | collective-permute-start | bytes 1179656 | tf_op jit(solution)/shard_map/ppermute | solution.py:48
  198.7 46.4 %collective-permute-start.4 = (f32[192,128]{1,0:T(8,128)S(1)}, f32[192,128]{1,0:T(8,128)S(1)}, u32[]{:S(2)}, u32[]{:S(2)}) collective-permute-start(f32[192,128]{1,0:T(8,128)S(1)} %fusion.2), channel_id=1, source_target_pairs={{0,1},{1,0},{2,3},{3,2},{4,5},{5,4},{6,7},{7,6},{8,9},{9,8},{10,11... | collective-permute-start | bytes 294920 | tf_op jit(solution)/shard_map/ppermute | solution.py:48
  215.7 25.0 %copy-start.16 = (s32[3]{0:T(128)S(1)}, s32[3]{0:T(128)}, u32[]{:S(2)}) copy-start(s32[3]{0:T(128)} %param.22) | copy-start | bytes 40
  215.8 25.1 %copy-start.15 = (s32[384]{0:T(512)S(1)}, s32[384]{0:T(512)}, u32[]{:S(2)}) copy-start(s32[384]{0:T(512)} %param.21) | copy-start | bytes 4612
  215.8 27.0 %copy-start.7 = (f32[32,4,2,1280]{3,2,1,0:T(2,128)S(1)}, f32[32,4,2,1280]{3,2,1,0:T(2,128)}, u32[]{:S(2)}) copy-start(f32[32,4,2,1280]{3,2,1,0:T(2,128)} %get-tuple-element.57) | copy-start | bytes 3932164
  215.8 13.2 %collective-permute-start.7 = (f32[2,192,128]{2,1,0:T(8,128)S(1)}, f32[2,192,128]{2,1,0:T(8,128)S(1)}, u32[]{:S(2)}, u32[]{:S(2)}) collective-permute-start(f32[2,192,128]{2,1,0:T(8,128)S(1)} %slice.172), channel_id=1, source_target_pairs={{0,8},{2,10},{4,12},{6,14},{8,0},{10,2},{12,4},{14,6},{16,24},{18,... | collective-permute-start | bytes 589832 | tf_op jit(solution)/shard_map/ppermute | solution.py:48
  227.7 6.7 %collective-permute-start.12 = (f32[2,192,128]{2,1,0:T(8,128)S(1)}, f32[2,192,128]{2,1,0:T(8,128)S(1)}, u32[]{:S(2)}, u32[]{:S(2)}) collective-permute-start(f32[2,192,128]{2,1,0:T(8,128)S(1)} %slice.181), channel_id=1, source_target_pairs={{0,8},{2,10},{4,12},{6,14},{8,0},{10,2},{12,4},{14,6},{16,24},{18,... | collective-permute-start | bytes 589832 | tf_op jit(solution)/shard_map/ppermute | solution.py:48
  229.0 7.1 %collective-permute-start.8 = (f32[1,192,128]{2,1,0:T(8,128)S(1)}, f32[1,192,128]{2,1,0:T(8,128)S(1)}, u32[]{:S(2)}, u32[]{:S(2)}) collective-permute-start(f32[1,192,128]{2,1,0:T(8,128)S(1)} %slice.174), channel_id=1, source_target_pairs={{0,16},{2,18},{4,20},{6,22},{8,24},{10,26},{12,28},{14,30},{16,0},... | collective-permute-start | bytes 294920 | tf_op jit(solution)/shard_map/ppermute | solution.py:48
  234.4 5.0 %collective-permute-start.13 = (f32[1,192,128]{2,1,0:T(8,128)S(1)}, f32[1,192,128]{2,1,0:T(8,128)S(1)}, u32[]{:S(2)}, u32[]{:S(2)}) collective-permute-start(f32[1,192,128]{2,1,0:T(8,128)S(1)} %slice.183), channel_id=1, source_target_pairs={{0,16},{2,18},{4,20},{6,22},{8,24},{10,26},{12,28},{14,30},{16,0},... | collective-permute-start | bytes 294920 | tf_op jit(solution)/shard_map/ppermute | solution.py:48
  236.2 9.6 %collective-permute-start.9 = (f32[192,128]{1,0:T(8,128)S(1)}, f32[192,128]{1,0:T(8,128)S(1)}, u32[]{:S(2)}, u32[]{:S(2)}) collective-permute-start(f32[192,128]{1,0:T(8,128)S(1)} %fusion.1), channel_id=1, source_target_pairs={{0,1},{1,0},{2,3},{3,2},{4,5},{5,4},{6,7},{7,6},{8,9},{9,8},{10,11... | collective-permute-start | bytes 294920 | tf_op jit(solution)/shard_map/ppermute | solution.py:48
  239.4 7.0 %collective-permute-start.14 = (f32[192,128]{1,0:T(8,128)S(1)}, f32[192,128]{1,0:T(8,128)S(1)}, u32[]{:S(2)}, u32[]{:S(2)}) collective-permute-start(f32[192,128]{1,0:T(8,128)S(1)} %fusion), channel_id=1, source_target_pairs={{0,1},{1,0},{2,3},{3,2},{4,5},{5,4},{6,7},{7,6},{8,9},{9,8},{10,11... | collective-permute-start | bytes 294920 | tf_op jit(solution)/shard_map/ppermute | solution.py:48
  247.1 38.0 %all-to-all-start.4 = ((f32[32,4,2560]{2,1,0:T(4,128)}), f32[32,4,2560]{2,1,0:T(4,128)S(1)}, u32[]{:S(2)}, u32[]{:S(2)}) async-start(f32[32,4,2560]{2,1,0:T(4,128)} %reshape.203), calls=%async_computation.4 | async-start | bytes 2621440 | tf_op jit(solution)/shard_map/all_to_all | solution.py:429
  285.1 1.1 copy-start.13
  286.2 36.7 %all-to-all-start.5 = ((f32[32,4,2560]{2,1,0:T(4,128)}), f32[32,4,2560]{2,1,0:T(4,128)S(1)}, u32[]{:S(2)}, u32[]{:S(2)}) async-start(f32[32,4,2560]{2,1,0:T(4,128)} %bitcast.61), calls=%async_computation.5 | async-start | bytes 2621440 | tf_op jit(solution)/shard_map/all_to_all | solution.py:429
  292.2 29.7 %copy-start.14 = (f32[3,192,128]{2,1,0:T(8,128)S(1)}, f32[3,192,128]{2,1,0:T(8,128)}, u32[]{:S(2)}) copy-start(f32[3,192,128]{2,1,0:T(8,128)} %get-tuple-element.30) | copy-start | bytes 884740
  322.9 38.5 %copy-start.11 = (f32[32,4,2560]{2,1,0:T(4,128)}, f32[32,4,2560]{2,1,0:T(4,128)S(1)}, u32[]{:S(2)}) copy-start(f32[32,4,2560]{2,1,0:T(4,128)S(1)} %all-to-all-done.5.refs_0_) | copy-start | bytes 3932164
  322.9 8.5 %collective-permute-start.15 = (f32[3,192,128]{2,1,0:T(8,128)S(1)}, f32[3,192,128]{2,1,0:T(8,128)S(1)}, u32[]{:S(2)}, u32[]{:S(2)}) collective-permute-start(f32[3,192,128]{2,1,0:T(8,128)S(1)} %add.115), channel_id=1, source_target_pairs={{0,1},{1,0},{2,3},{3,2},{4,5},{5,4},{6,7},{7,6},{8,9},{9,8},{10,11... | collective-permute-start | bytes 884744 | tf_op jit(solution)/shard_map/ppermute | solution.py:48
  331.5 15.3 %collective-permute-start.16 = (f32[1,3,192,128]{3,2,1,0:T(8,128)S(1)}, f32[1,3,192,128]{3,2,1,0:T(8,128)S(1)}, u32[]{:S(2)}, u32[]{:S(2)}) collective-permute-start(f32[1,3,192,128]{3,2,1,0:T(8,128)S(1)} %add_bitcast_fusion), channel_id=1, source_target_pairs={{0,16},{2,18},{4,20},{6,22},{8,24},{10,26},{12,28},{14,30},{16,0},... | collective-permute-start | bytes 884744 | tf_op jit(solution)/shard_map/ppermute | solution.py:48
  346.8 13.5 %collective-permute-start.17 = (f32[2,3,192,128]{3,2,1,0:T(8,128)S(1)}, f32[2,3,192,128]{3,2,1,0:T(8,128)S(1)}, u32[]{:S(2)}, u32[]{:S(2)}) collective-permute-start(f32[2,3,192,128]{3,2,1,0:T(8,128)S(1)} %pad_maximum_fusion.3), channel_id=1, source_target_pairs={{0,8},{2,10},{4,12},{6,14},{8,0},{10,2},{12,4},{14,6},{16,24},{18,... | collective-permute-start | bytes 1769480 | tf_op jit(solution)/shard_map/ppermute | solution.py:48
  361.4 33.0 %collective-permute-start.18 = (f32[4,3,192,128]{3,2,1,0:T(8,128)}, f32[4,3,192,128]{3,2,1,0:T(8,128)}, u32[]{:S(2)}, u32[]{:S(2)}) collective-permute-start(f32[4,3,192,128]{3,2,1,0:T(8,128)} %pad_maximum_fusion.2), channel_id=1, source_target_pairs={{0,4},{2,6},{4,0},{6,2},{8,12},{10,14},{12,8},{14,10},{16,20},{18,... | collective-permute-start | bytes 3538952 | tf_op jit(solution)/shard_map/ppermute | solution.py:48
  362.5 45.9 %all-to-all-start.6 = ((f32[32,4,2560]{2,1,0:T(4,128)}), f32[32,4,2560]{2,1,0:T(4,128)S(1)}, u32[]{:S(2)}, u32[]{:S(2)}) async-start(f32[32,4,2560]{2,1,0:T(4,128)} %bitcast.59), calls=%async_computation.6 | async-start | bytes 2621440 | tf_op jit(solution)/shard_map/all_to_all | solution.py:429
  397.3 21.0 %collective-permute-start.19 = (f32[8,3,192,128]{3,2,1,0:T(8,128)}, f32[8,3,192,128]{3,2,1,0:T(8,128)}, u32[]{:S(2)}, u32[]{:S(2)}) collective-permute-start(f32[8,3,192,128]{3,2,1,0:T(8,128)} %pad_maximum_fusion.refs_3_), channel_id=1, source_target_pairs={{0,2},{2,0},{4,6},{6,4},{8,10},{10,8},{12,14},{14,12},{16,18},{18,... | collective-permute-start | bytes 7077896 | tf_op jit(solution)/shard_map/ppermute | solution.py:48
  408.3 1.1 copy-start.12
  418.3 18.2 %copy-start.1 = (f32[64,4,4,256]{3,2,1,0:T(4,128)S(1)}, f32[64,4,4,256]{3,2,1,0:T(4,128)}, u32[]{:S(2)}) copy-start(f32[64,4,4,256]{3,2,1,0:T(4,128)} %param.20) | copy-start | bytes 3145732

commit v3 on v2

v3 whole, which is shorter than its diff:
```python
import functools

import jax
import jax.numpy as jnp
from jax import lax
from jax.experimental import pallas as pl
from jax.experimental.pallas import tpu as pltpu
from jax.sharding import PartitionSpec as P

ADAPTER_SCALE = 0.5
MASKED = -1e30
BF16, F32 = jnp.bfloat16, jnp.float32
VMEM_LIMIT = 56 * 1024 * 1024
NN = (((1,), (0,)), ((), ()))
NT = (((1,), (1,)), ((), ()))
TN = (((0,), (0,)), ((), ()))
HEADS_PER_CALL = 2
ATTENTION_MICROS = 10
DOWN_MICROS = 2


def cost(micros):
    return pl.CostEstimate(
        flops=int(micros * 1e9), bytes_accessed=int(micros * 3.6e6), transcendentals=0
    )


def split2(a):
    high = a.astype(BF16)
    return high, (a - high.astype(F32)).astype(BF16)


def mm(a, b, dims=NN):
    return lax.dot_general(a, b, dims, preferred_element_type=F32)


def mm3(a, b, dims=NN):
    (ah, al), (bh, bl) = a, b
    return mm(ah, bh, dims) + mm(ah, bl, dims) + mm(al, bh, dims)


def bit_reverse(value, bits):
    out = jnp.zeros_like(value)
    for k in range(bits):
        out = out | (((value >> k) & 1) << (bits - 1 - k))
    return out


def swap(a, axis, size, bit):
    return lax.ppermute(a, axis, [(i, i ^ bit) for i in range(size)])


def sum_over(a, axis, size):
    bit = 1
    while bit < size:
        a = a + swap(a, axis, size, bit)
        bit *= 2
    return a


def scatter_sum(part, axis, size):
    bit = 1
    while bit < min(size, 4):
        half = part.shape[0] // 2
        part = part[:half] + swap(part[half:], axis, size, bit)
        bit *= 2
    moved = [
        swap(part[k], axis, size, bit_reversed(k, part.shape[0]) * bit)
        for k in range(1, part.shape[0])
    ]
    return functools.reduce(jnp.add, moved, part[0])


def bit_reversed(k, size):
    out = 0
    for i in range(size.bit_length() - 1):
        out |= (k >> i & 1) << (size.bit_length() - 2 - i)
    return out


def gather_far(a, axis, size):
    far = max(size // 4, 1)
    moved = [a] + [swap(a, axis, size, bit_reversed(k, far) * 4) for k in range(1, far)]
    return jnp.concatenate(moved, axis=0)


def gather_step(a, axis, size, bit):
    return jnp.concatenate([a, swap(a, axis, size, bit)], axis=0)


def after(a, *others):
    return lax.optimization_barrier((a,) + others)[0]


def by_tenant(owners, tenants):
    count = owners.shape[0]
    index = jnp.arange(count, dtype=jnp.int32)
    ahead = (owners[None, :] < owners[:, None]) | (
        (owners[None, :] == owners[:, None]) & (index[None, :] < index[:, None])
    )
    place = jnp.sum(ahead.astype(jnp.int32), axis=1)
    order = jnp.sum(
        jnp.where(place[None, :] == index[:, None], index[None, :], 0), axis=1
    )
    edge = jnp.arange(tenants + 1, dtype=jnp.int32)
    first = jnp.sum((owners[None, :] < edge[:, None]).astype(jnp.int32), axis=1)
    return order.astype(jnp.int32), first.astype(jnp.int32)


def wire_kernel(n, slot_ref, x_ref, out_ref):
    rows = x_ref.shape[0]
    width = x_ref.shape[1] // n
    for r in range(n):
        out_ref[r, :rows] = x_ref[:, r * width : (r + 1) * width].astype(F32)
    if out_ref.shape[1] > rows:
        lane = lax.broadcasted_iota(jnp.int32, (8, width), 1)
        tile = jnp.zeros((8, width), F32)
        for b in range(slot_ref.shape[0]):
            tile = jnp.where(lane == b, slot_ref[b].astype(F32), tile)
        out_ref[:, rows:] = jnp.broadcast_to(tile[None], (n, 8, width))


def rows_wire(x, block_slots, n, b):
    blocks = block_slots.shape[0]
    rows, width = x.shape[0] // blocks, x.shape[1] // n
    per = min(n, max(128 // width, 1) * 4)
    tall = rows + (8 if b == 0 else 0)
    return pl.pallas_call(
        functools.partial(wire_kernel, per),
        grid_spec=pltpu.PrefetchScalarGridSpec(
            num_scalar_prefetch=1,
            grid=(n // per,),
            in_specs=[pl.BlockSpec((rows, per * width), lambda i, s: (b, i))],
            out_specs=pl.BlockSpec((per, tall, width), lambda i, s: (i, 0, 0)),
        ),
        out_shape=jax.ShapeDtypeStruct((n, tall, width), F32),
        cost_estimate=cost(2),
        compiler_params=pltpu.CompilerParams(vmem_limit_bytes=VMEM_LIMIT),
        name="rows_wire",
    )(block_slots, x)


def down_kernel(count, calls, source_ref, tenant_ref, *refs):
    x_refs, w_refs, out_ref = refs[: count * calls], refs[count * calls : -1], refs[-1]
    for c in range(count):
        for b in range(calls):
            x = x_refs[c * calls + b][0].astype(BF16)
            high, low = split2(w_refs[c * calls + b][0])
            out_ref[c, b] = mm(high, x, NT) + mm(low, x, NT)


def down_partial(xs, weights, source, tenant, rows):
    n, _, width = xs[0].shape
    rank = weights.shape[1]
    calls = len(xs)
    count = 4 // calls
    every = [(c, b) for c in range(count) for b in range(calls)]

    def x_spec(c, b):
        return pl.BlockSpec((1, rows, width), lambda p, s, t: (s[p * count + c], 0, 0))

    def w_spec(c, b):
        return pl.BlockSpec(
            (1, rank, width), lambda p, s, t: (t[(p * count + c) * calls + b], 0, 0)
        )

    return pl.pallas_call(
        functools.partial(down_kernel, count, calls),
        grid_spec=pltpu.PrefetchScalarGridSpec(
            num_scalar_prefetch=2,
            grid=(n // count,),
            in_specs=[x_spec(*at) for at in every] + [w_spec(*at) for at in every],
            out_specs=pl.BlockSpec((count, calls, rank, rows), lambda p, s, t: (p, 0, 0, 0)),
        ),
        out_shape=jax.ShapeDtypeStruct((n, calls, rank, rows), F32),
        cost_estimate=cost(DOWN_MICROS * calls),
        compiler_params=pltpu.CompilerParams(vmem_limit_bytes=VMEM_LIMIT),
        name="down_partial",
    )(source, tenant.reshape(-1), *[xs[b] for _, b in every], *[weights] * len(every))


def attention_kernel(groups, slots, blocks, todo, *refs):
    first_call, last_call = todo[0] == blocks - 1, todo[-1] == 0
    used = todo[0] + 1
    fq_ref, fk_ref, fv_ref, up_ref = refs[:4]
    low_refs = refs[4 : 4 + used]
    panel_ref, slot_ref, doc_row_ref, doc_col_ref, g_in_ref = refs[4 + used : 9 + used]
    refs = refs[9 + used :]
    if not first_call:
        carry_in, refs = refs[:3], refs[3:]
    if last_call:
        (du_ref, g_ref), refs = refs[:2], refs[2:]
    else:
        (g_ref, *carry_out), refs = refs[:4], refs[4:]
    bias, lct_h, lct_l, lc_h, lc_l, panel, du, dk, dv, q_s, up_s, sc, gp, ds, pr = refs
    step = pl.program_id(0)
    rows, head = fk_ref.shape
    block = rows // blocks
    owners, _, piece, _ = panel_ref.shape
    rank = owners * piece
    wide = groups * head
    inverse = 1.0 / head**0.5
    slot = slot_ref[...]

    @pl.when(step == 0)
    def _():
        key = lax.broadcasted_iota(jnp.int32, (rows, rows), 0)
        row = lax.broadcasted_iota(jnp.int32, (rows, rows), 1)
        joined = (doc_row_ref[...] == doc_col_ref[...]) & (row >= key)
        bias[...] = jnp.where(joined, 0.0, MASKED)
        for b in range(used):
            span = slice(b * block, (b + 1) * block)
            for part in range(3):
                low = low_refs[b][part * rank : (part + 1) * rank, :] * ADAPTER_SCALE
                both = jnp.concatenate(
                    [jnp.where(slot[:, span] == s, low, 0.0) for s in range(slots)], axis=0
                )
                lct_h[part, b], lct_l[part, b] = split2(both)
                lc_h[part, span, :], lc_l[part, span, :] = split2(both.T)
        for b in todo:
            g_ref[b - todo[-1]] = g_in_ref[b] * (1.0 / ADAPTER_SCALE)

    for w in range(owners):
        for s in range(slots):
            start = s * rank + w * piece
            panel[start : start + piece, :] = panel_ref[w, s]
    u_q = split2(panel[:, :wide])
    u_k = split2(panel[:, wide : wide + head])
    u_v = split2(panel[:, wide + head :])
    seen = used * block
    k = fk_ref[:seen].astype(F32) + mm3((lc_h[1, :seen], lc_l[1, :seen]), u_k)
    v = fv_ref[:seen].astype(F32) + mm3((lc_h[2, :seen], lc_l[2, :seen]), u_v)
    k, v = k.astype(BF16), v.astype(BF16)
    k_t = k.T
    if first_call:
        dk[...] = jnp.zeros_like(dk)
        dv[...] = jnp.zeros_like(dv)
        du[...] = jnp.zeros_like(du)
    else:
        dk[...], dv[...], du[...] = [ref[0] for ref in carry_in]

    for b in todo:
        here = slice(b * block, (b + 1) * block)
        reach = (b + 1) * block
        q = fq_ref[here].astype(F32) + mm3((lc_h[0, here], lc_l[0, here]), u_q)
        q = q.astype(BF16)
        for h in range(groups):
            at, lanes = slice(h * block, (h + 1) * block), slice(h * head, (h + 1) * head)
            q_s[at] = q[:, lanes]
            up_s[at] = up_ref[here, lanes]
        sc[:reach] = mm(k[:reach], q_s[...], NT)
        gp[:reach] = mm(v[:reach], up_s[...], NT)
        mask = bias[:reach, here]
        for h in range(groups):
            at = slice(h * block, (h + 1) * block)
            scores = sc[:reach, at] * inverse + mask
            weights = jnp.exp(scores - jnp.max(scores, axis=0, keepdims=True))
            scale = 1.0 / jnp.sum(weights, axis=0, keepdims=True)
            grad_probs = gp[:reach, at]
            probs = weights * scale
            inner = jnp.sum(probs * grad_probs, axis=0, keepdims=True)
            ds[:reach, at] = (probs * (grad_probs - inner) * inverse).astype(BF16)
            pr[:reach, at] = probs.astype(BF16)
        dk[:reach] += mm(ds[:reach], q_s[...])
        dv[:reach] += mm(pr[:reach], up_s[...])
        dq = split2(mm(k_t[:, :reach], ds[:reach]))
        dk_b, dv_b = split2(dk[here]), split2(dv[here])
        lct = [(lct_h[part, b], lct_l[part, b]) for part in range(3)]
        both = jnp.zeros((slots * rank, block), F32)
        for h in range(groups):
            at, lanes = slice(h * block, (h + 1) * block), slice(h * head, (h + 1) * head)
            dq_h = (dq[0][:, at], dq[1][:, at])
            du[:, lanes] += mm3(lct[0], dq_h, NT)
            both += mm3((u_q[0][:, lanes], u_q[1][:, lanes]), dq_h)
        du[:, wide : wide + head] += mm3(lct[1], dk_b)
        du[:, wide + head :] += mm3(lct[2], dv_b)
        for part, full in enumerate((both, mm3(u_k, dk_b, NT), mm3(u_v, dv_b, NT))):
            mine = jnp.zeros((rank, block), F32)
            for s in range(slots):
                mine += jnp.where(slot[:, here] == s, full[s * rank : (s + 1) * rank], 0.0)
            g_ref[b - todo[-1], part * rank : (part + 1) * rank, :] += mine

    @pl.when(step == pl.num_programs(0) - 1)
    def _():
        g_ref[...] *= ADAPTER_SCALE

    if last_call:
        for w in range(owners):
            for s in range(slots):
                start = s * rank + w * piece
                du_ref[w, s] = du[start : start + piece, :]
    else:
        for ref, value in zip(carry_out, (dk, dv, du)):
            ref[0] = value[...]


def attention(
    fq, fk, fv, up, lows, *, panels, slot_rows, docs, g, head, first, heads, todo, carry
):
    rows = fq.shape[0]
    blocks = len(lows)
    block = rows // blocks
    n, slots, piece, cols = panels.shape
    kv_heads = fk.shape[1] // head
    groups = fq.shape[1] // fk.shape[1]
    wide = groups * head
    per = wide + 2 * head
    rank = n * piece
    spans = slots * rank
    used = todo[0] + 1
    whole = lambda shape: pl.BlockSpec(shape, lambda i: (0,) * len(shape))
    carry_shapes = [(heads, rows, head), (heads, rows, head), (heads, spans, per)]
    carry_specs = [
        pl.BlockSpec((1,) + shape[1:], lambda i: (i, 0, 0)) for shape in carry_shapes
    ]
    g_shape = (len(todo), 3 * rank, block)
    if todo[-1] == 0:
        out_specs = [pl.BlockSpec((n, slots, piece, per), lambda i: (0, 0, 0, i)), whole(g_shape)]
        out_shape = [(n, slots, piece, heads * per), g_shape]
    else:
        out_specs = [whole(g_shape)] + carry_specs
        out_shape = [g_shape] + carry_shapes
    first_call = todo[0] == blocks - 1
    pairs = sum(b + 1 for b in todo) / (blocks * (blocks + 1) / 2)
    return pl.pallas_call(
        functools.partial(attention_kernel, groups, slots, blocks, todo),
        grid=(heads,),
        in_specs=[
            pl.BlockSpec((rows, wide), lambda i: (0, first + i)),
            pl.BlockSpec((rows, head), lambda i: (0, first + i)),
            pl.BlockSpec((rows, head), lambda i: (0, first + i)),
            pl.BlockSpec((rows, wide), lambda i: (0, first + i)),
        ]
        + [whole((3 * rank, block))] * used
        + [
            pl.BlockSpec((n, slots, piece, per), lambda i: (0, 0, 0, i)),
            whole((1, rows)),
            whole((1, rows)),
            whole((rows, 1)),
            whole(g.shape),
        ]
        + ([] if first_call else carry_specs),
        out_specs=out_specs,
        out_shape=[jax.ShapeDtypeStruct(shape, F32) for shape in out_shape],
        scratch_shapes=[
            pltpu.VMEM((rows, rows), F32),
            pltpu.VMEM((3, used, spans, block), BF16),
            pltpu.VMEM((3, used, spans, block), BF16),
            pltpu.VMEM((3, used * block, spans), BF16),
            pltpu.VMEM((3, used * block, spans), BF16),
            pltpu.VMEM((spans, per), F32),
            pltpu.VMEM((spans, per), F32),
            pltpu.VMEM((rows, head), F32),
            pltpu.VMEM((rows, head), F32),
            pltpu.VMEM((groups * block, head), BF16),
            pltpu.VMEM((groups * block, head), BF16),
            pltpu.VMEM((rows, groups * block), F32),
            pltpu.VMEM((rows, groups * block), F32),
            pltpu.VMEM((rows, groups * block), BF16),
            pltpu.VMEM((rows, groups * block), BF16),
        ],
        cost_estimate=cost(ATTENTION_MICROS * heads * pairs),
        compiler_params=pltpu.CompilerParams(vmem_limit_bytes=VMEM_LIMIT),
        name="attention_grads",
    )(
        fq,
        fk,
        fv,
        up,
        *lows[:used],
        panels,
        slot_rows,
        docs[None, :],
        docs[:, None],
        g,
        *(() if first_call else carry),
    )


def down_grad_kernel(blocks, per_step, order_ref, first_ref, source_ref, *refs):
    x_refs, g_refs = refs[:blocks], refs[blocks : 3 * blocks]
    out_ref, x_all, g_ref, sems = refs[3 * blocks :]
    half = g_refs[0].shape[0]
    step = pl.program_id(0)

    @pl.when(step == 0)
    def _():
        copies = [
            pltpu.make_async_copy(
                x_refs[b].at[:, pl.ds(0, x_all.shape[2])], x_all.at[b], sems.at[b]
            )
            for b in range(blocks)
        ] + [
            pltpu.make_async_copy(
                ref, g_ref.at[i // 2, pl.ds(i % 2 * half, half)], sems.at[blocks + i]
            )
            for i, ref in enumerate(g_refs)
        ]
        for copy in copies:
            copy.start()
        for copy in copies:
            copy.wait()

    for t in range(per_step):
        tenant = step * per_step + t
        out_ref[t] = jnp.zeros(out_ref.shape[1:], F32)

        def add(e, carry):
            item = order_ref[e]
            place = item // blocks
            b = item - place * blocks
            x = x_all[b, source_ref[place]].astype(BF16)
            high, low = split2(g_ref[b, place])
            out_ref[t] += mm(high, x) + mm(low, x)
            return carry

        lax.fori_loop(first_ref[tenant], first_ref[tenant + 1], add, 0)


def down_grad(xs, g, order, first, source, tenants):
    blocks = len(xs)
    n, rows, width = xs[1].shape
    rank = g[0].shape[1]
    per_step = 8
    return pl.pallas_call(
        functools.partial(down_grad_kernel, blocks, per_step),
        grid_spec=pltpu.PrefetchScalarGridSpec(
            num_scalar_prefetch=3,
            grid=(tenants // per_step,),
            in_specs=[pl.BlockSpec(memory_space=pl.ANY)] * (3 * blocks),
            out_specs=pl.BlockSpec((per_step, rank, width), lambda i, *_: (i, 0, 0)),
            scratch_shapes=[
                pltpu.VMEM((blocks, n, rows, width), F32),
                pltpu.VMEM((blocks, n) + g[0].shape[1:], F32),
                pltpu.SemaphoreType.DMA((3 * blocks,)),
            ],
        ),
        out_shape=jax.ShapeDtypeStruct((tenants, rank, width), F32),
        compiler_params=pltpu.CompilerParams(vmem_limit_bytes=VMEM_LIMIT),
        cost_estimate=cost(15),
        name="down_grad",
    )(order, first, source, *xs, *g)


def down_grad_last_kernel(owner_ref, leader_ref, source_ref, *refs):
    x_ref, g0_ref, g1_ref, sum_ref, out_ref, x_all, g_all, acc, in_sems, out_sems = refs
    del sum_ref
    n, rows, _ = x_all.shape
    half = n // 2
    loads = [
        pltpu.make_async_copy(x_ref.at[:, pl.ds(0, rows)], x_all, in_sems.at[n]),
        pltpu.make_async_copy(g0_ref, g_all.at[pl.ds(0, half)], in_sems.at[n + 1]),
        pltpu.make_async_copy(g1_ref, g_all.at[pl.ds(half, half)], in_sems.at[n + 2]),
    ]
    for load in loads:
        load.start()

    def tile(p, inward):
        there, here = out_ref.at[owner_ref[p]], acc.at[p]
        if inward:
            return pltpu.make_async_copy(there, here, in_sems.at[p])
        return pltpu.make_async_copy(here, there, out_sems.at[p])

    def leaders(act):
        for p in range(n):
            pl.when(leader_ref[p] == p)(functools.partial(act, p))

    leaders(lambda p: tile(p, True).start())
    for load in loads:
        load.wait()
    leaders(lambda p: tile(p, True).wait())
    for p in range(n):
        x = x_all[source_ref[p]].astype(BF16)
        high, low = split2(g_all[p])
        acc[leader_ref[p]] += mm(high, x) + mm(low, x)
    leaders(lambda p: tile(p, False).start())
    leaders(lambda p: tile(p, False).wait())


def down_grad_last(x, g, total, owner, source):
    n, rank, rows = 2 * g[0].shape[0], g[0].shape[1], g[0].shape[2]
    width = x.shape[2]
    index = jnp.arange(n, dtype=jnp.int32)
    same = owner[None, :] == owner[:, None]
    leader = jnp.min(jnp.where(same, index[None, :], n), axis=1).astype(jnp.int32)
    return pl.pallas_call(
        down_grad_last_kernel,
        grid_spec=pltpu.PrefetchScalarGridSpec(
            num_scalar_prefetch=3,
            grid=(1,),
            in_specs=[pl.BlockSpec(memory_space=pl.ANY)] * 4,
            out_specs=pl.BlockSpec(memory_space=pl.ANY),
            scratch_shapes=[
                pltpu.VMEM((n, rows, width), F32),
                pltpu.VMEM((n, rank, rows), F32),
                pltpu.VMEM((n, rank, width), F32),
                pltpu.SemaphoreType.DMA((n + 3,)),
                pltpu.SemaphoreType.DMA((n,)),
            ],
        ),
        out_shape=jax.ShapeDtypeStruct(total.shape, F32),
        input_output_aliases={6: 0},
        cost_estimate=cost(6),
        compiler_params=pltpu.CompilerParams(vmem_limit_bytes=VMEM_LIMIT),
        name="down_grad_last",
    )(owner, leader, source, x, *g, total)


def up_grad_kernel(calls, per_step, kv_heads, head, order_ref, first_ref, *refs):
    in_refs, (q_ref, kv_ref, kv_sum) = refs[:calls], refs[calls:]
    step = pl.program_id(0)
    wide = q_ref.shape[2] // kv_heads
    per = wide + 2 * head
    heads = kv_heads // calls
    for t in range(per_step):
        tenant = step * per_step + t
        q_ref[t] = jnp.zeros(q_ref.shape[1:], F32)
        kv_sum[...] = jnp.zeros_like(kv_sum)

        def add(e, carry):
            item = order_ref[e]
            for c in range(calls):
                for h in range(heads):
                    at = c * heads + h
                    q_ref[t, :, at * wide : (at + 1) * wide] += in_refs[c][
                        item, :, h * per : h * per + wide
                    ]
                    kv_sum[at] += in_refs[c][item, :, h * per + wide : (h + 1) * per]
            return carry

        lax.fori_loop(first_ref[tenant], first_ref[tenant + 1], add, 0)
        for k in range(kv_ref.shape[1]):
            for h in range(kv_heads):
                kv_ref[t, k, h, :] = kv_sum[h, k, :]


def up_grad(dus, order, first, tenants, kv_heads, head):
    calls = len(dus)
    items, piece, cols = dus[0].shape
    per_step = 8
    wide = cols * calls // kv_heads - 2 * head
    return pl.pallas_call(
        functools.partial(up_grad_kernel, calls, per_step, kv_heads, head),
        grid_spec=pltpu.PrefetchScalarGridSpec(
            num_scalar_prefetch=2,
            grid=(tenants // per_step,),
            in_specs=[pl.BlockSpec((items, piece, cols), lambda i, *_: (0, 0, 0))] * calls,
            out_specs=[
                pl.BlockSpec((per_step, piece, kv_heads * wide), lambda i, *_: (i, 0, 0)),
                pl.BlockSpec((per_step, piece, kv_heads, 2 * head), lambda i, *_: (i, 0, 0, 0)),
            ],
            scratch_shapes=[pltpu.VMEM((kv_heads, piece, 2 * head), F32)],
        ),
        out_shape=[
            jax.ShapeDtypeStruct((tenants, piece, kv_heads * wide), F32),
            jax.ShapeDtypeStruct((tenants, piece, kv_heads, 2 * head), F32),
        ],
        compiler_params=pltpu.CompilerParams(vmem_limit_bytes=VMEM_LIMIT),
        cost_estimate=cost(6),
        name="up_grad",
    )(order, first, *dus)


def exchange(a):
    return lax.all_to_all(a, "dp", split_axis=0, concat_axis=0, tiled=True)


def on_device(
    dp_count,
    mp_count,
    normed_input_rows,
    frozen_queries,
    frozen_keys,
    frozen_values,
    attention_output_gradient,
    adapter_down_weight,
    adapter_up_query,
    adapter_up_key_value,
    document_numbers,
    block_tenant_slot,
    shard_tenant_table,
):
    rows = normed_input_rows.shape[0]
    blocks = block_tenant_slot.shape[0]
    block = rows // blocks
    tenants, width, ranks = adapter_down_weight.shape
    slots = shard_tenant_table.shape[1]
    piece = adapter_up_query.shape[1]
    kv_heads = adapter_up_key_value.shape[2]
    head = adapter_up_key_value.shape[3] // 2
    wide = adapter_up_query.shape[2] // kv_heads
    me = lax.axis_index("dp").astype(jnp.int32)

    wires = [
        rows_wire(normed_input_rows, block_tenant_slot, dp_count, b) for b in range(blocks)
    ]
    wanted = shard_tenant_table.reshape(-1)
    up_query = adapter_up_query[wanted].reshape(-1, piece, kv_heads, wide)
    up_key_value = adapter_up_key_value[wanted]
    wire = jnp.concatenate([up_query, up_key_value], axis=-1)
    heads = min(HEADS_PER_CALL, kv_heads)
    calls = kv_heads // heads
    per = wide + 2 * head
    owns = [
        wire[:, :, c * heads : (c + 1) * heads].reshape(-1, piece, heads * per)
        for c in range(calls)
    ]

    xs = [exchange(wires[0])]
    for b in range(1, blocks):
        xs.append(exchange(after(wires[b], xs[-1], *(owns if b == blocks - 1 else ()))))

    source = me ^ bit_reverse(
        jnp.arange(dp_count, dtype=jnp.int32), dp_count.bit_length() - 1
    )
    slots_all = xs[0][:, block, :blocks].astype(jnp.int32)[source]
    owners = shard_tenant_table[source[:, None], slots_all]

    weights = jnp.swapaxes(adapter_down_weight, 1, 2)
    part = down_partial(xs[:-1], weights, source, owners[:, :-1], block)
    early = sum_over(scatter_sum(part, "dp", dp_count), "mp", mp_count)
    part = down_partial(xs[-1:], weights, source, owners[:, -1:], block)
    late = sum_over(scatter_sum(part, "dp", dp_count), "mp", mp_count)
    lows = [early[b] for b in range(blocks - 1)] + [late[0]]

    panels = []
    for c in range(calls):
        own = after(owns[c], xs[-1], early) if c == 0 else after(owns[c], panels[-1], late)
        panels.append(exchange(own).reshape(dp_count, slots, piece, heads * per))

    attend = functools.partial(
        attention,
        frozen_queries,
        frozen_keys,
        frozen_values,
        attention_output_gradient,
        lows,
        slot_rows=jnp.repeat(block_tenant_slot, block)[None, :],
        docs=document_numbers,
        head=head,
        heads=heads,
    )
    g = jnp.zeros((blocks, 3 * piece * dp_count, block), F32)
    every = tuple(range(blocks))[::-1]
    dus = []
    for c in range(calls - 1):
        du, g = attend(panels=panels[c], g=g, first=c * heads, todo=every, carry=())
        dus.append(exchange(du.reshape(dp_count * slots, piece, heads * per)))
    sums, fars, carry = {}, {}, ()
    for b in every:
        if b == blocks - 3:
            fars[blocks - 1] = gather_far(sums[blocks - 1], "dp", dp_count)
            carry = after(carry, sums[blocks - 1])
        out = attend(panels=panels[-1], g=g, first=kv_heads - heads, todo=(b,), carry=carry)
        du, g_b = out if b == 0 else (None, out[0])
        carry = out[1:]
        if b == 0:
            g_b = after(g_b, *dus, fars[blocks - 1], *(sums[k] for k in every[:-1]))
        sums[b] = sum_over(g_b, "mp", mp_count)
    du = du.reshape(dp_count * slots, piece, heads * per)
    g_halves = [None] * blocks
    for b in every:
        if b not in fars:
            fars[b] = gather_far(sums[b], "dp", dp_count)
        fars[b] = gather_step(fars[b], "dp", dp_count, 2)
        if b > 0:
            g_halves[b] = (fars[b], swap(fars[b], "dp", dp_count, 1))
    dus.append(exchange(du))

    early = [half for pair in g_halves[1:] for half in pair]
    order, first = by_tenant(owners[:, 1:].reshape(-1), tenants)
    grad_down = down_grad(xs[1:], early, order, first, source, tenants)
    fars[0] = after(fars[0], grad_down)
    g_halves[0] = (fars[0], swap(fars[0], "dp", dp_count, 1))
    grad_down = down_grad_last(xs[0], g_halves[0], grad_down, owners[:, 0], source)
    order, first = by_tenant(wanted, tenants)
    grad_upq, grad_upkv = up_grad(dus, order, first, tenants, kv_heads, head)
    return (
        jnp.swapaxes(grad_down, 1, 2),
        grad_upq,
        grad_upkv,
    )


def solution(mesh):
    placed = (
        P("dp", "mp"),
        P("dp", "mp"),
        P("dp", "mp"),
        P("dp", "mp"),
        P("dp", "mp"),
        P(None, ("mp", "dp"), None),
        P(None, "dp", "mp"),
        P(None, "dp", "mp", None),
        P("dp"),
        P("dp"),
        P(),
    )
    return jax.shard_map(
        functools.partial(on_device, mesh.shape["dp"], mesh.shape["mp"]),
        mesh=mesh,
        in_specs=placed,
        out_specs=(P(None, ("mp", "dp"), None), P(None, "dp", "mp"), P(None, "dp", "mp", None)),
        check_vma=False,
    )
```

time: 438 us -> 397 us (0.906)
  waiting for transfers between devices: 171 us -> 148 us
  local copies, waits for them, and re-layouts: 54.2 us -> 40.9 us
  other arithmetic: 18 us -> 7.71 us
    all_to_all x7, waiting for transfers between devices: 75.6 us -> 55.8 us  [exchange(): return lax.all_to_all(a, 'dp', split_axis=0, concat_axis=0, tiled=True)]
    convert_element_type x3 -> x0, local copies, waits for them, and re-layouts: 6.64 us -> none  [on_device(): wires = [normed_input_rows[b * block:(b + 1) * block].reshape(block, dp_c...]
    ppermute x20 -> x30, starting transfers between devices: 34.6 us -> 41.1 us  [swap(): return lax.ppermute(a, axis, [(i, i ^ bit) for i in range(size)])]
    slice x3, local copies, waits for them, and re-layouts: 9.17 us -> 3.29 us  [the longest x1 2.51 us: on_device(): wire[:, :, c * heads:(c + 1) * heads].reshape(-1, piece, heads * per)]
    pallas_call x5 -> x10, Pallas kernels: 76.7 us -> 82.5 us  [the longest x4 48.1 us: attention(): pl.pallas_call(functools.partial(attention_kernel, groups, slots, blocks,...]
    unnamed x42 -> x49, local copies, waits for them, and re-layouts: 15.4 us -> 9.58 us
    concatenate x4 -> x3, other arithmetic: 5.61 us -> 0.08 us  [gather_far(): return jnp.concatenate(moved, axis=0)]
    add x9 -> x4, other arithmetic: 4.98 us -> 0.46 us  [scatter_sum(): part = part[:half] + swap(part[half:], axis, size, bit)]
  transfers between devices with their start and end apart: 27 -> 37, of which waited for: 12 -> 19; matrix products, arithmetic and copies ran while one was open for 14% -> 11% of each run, Pallas kernels for 19% -> 23%
where the time goes in v3:
time: 397 us; the launch traced here: 396 us
  waiting for transfers between devices  148 us (37%)
  Pallas kernels  104 us (26%)
  starting transfers between devices  94.1 us (24%)
  local copies, waits for them, and re-layouts  40.9 us (10%)
  other arithmetic  7.71 us (2%)
    ppermute x30, waiting for transfers between devices, swap(): return lax.ppermute(a, axis, [(i, i ^ bit) for i in range(size)])  92.5 us
    all_to_all x7, waiting for transfers between devices, exchange(): return lax.all_to_all(a, 'dp', split_axis=0, concat_axis=0, tiled=True)  55.8 us
    all_to_all x7, starting transfers between devices, exchange(): return lax.all_to_all(a, 'dp', split_axis=0, concat_axis=0, tiled=True)  53 us
    pallas_call x4, Pallas kernels, attention(): pl.pallas_call(functools.partial(attention_kernel, groups, slots, blocks,...  48.1 us
    ppermute x30, starting transfers between devices, swap(): return lax.ppermute(a, axis, [(i, i ^ bit) for i in range(size)])  41.1 us
    pallas_call x2, Pallas kernels, down_partial(): pl.pallas_call(functools.partial(down_kernel, count, calls), grid_spec=pl...  15.5 us
    pallas_call x1, Pallas kernels, down_grad(): pl.pallas_call(functools.partial(down_grad_kernel, blocks, per_step), gri...  14.4 us
    pallas_call x3, Pallas kernels, rows_wire(): pl.pallas_call(functools.partial(wire_kernel, per), grid_spec=pltpu.Prefe...  12.9 us
  transfers between devices with their start and end apart: 37, of which 19 were waited for; matrix products, arithmetic and copies ran while one was open for 11% of the time, Pallas kernels for 23%

profile of v3, /device:TPU:1, one launch (start us, length us, event | category | flops | bytes accessed | tf_op | source)
XLA Modules:
  0.0 395.8 jit_solution(12676230476569392661)
XLA Ops:
  0.6 4.4 %rows_wire.3 = f32[16,136,256]{2,1,0:T(8,128)} custom-call(s32[3]{0:T(128)} %slot_ref.5, bf16[384,4096]{1,0:T(8,128)(2,1)} %x_ref.5), custom_call_target="tpu_custom_call" | custom-call | flops 2000000000 | bytes 7200000 | tf_op jit(solution)/shard_map/rows_wire/pallas_call | solution.py:128
  5.1 7.3 %all-to-all-start = ((f32[16,136,256]{2,1,0:T(8,128)}), f32[16,136,256]{2,1,0:T(8,128)S(1)}, u32[]{:S(2)}, u32[]{:S(2)}) async-start(f32[16,136,256]{2,1,0:T(8,128)} %rows_wire.3), calls=%async_computation | async-start | bytes 4456448 | tf_op jit(solution)/shard_map/all_to_all | solution.py:565
  12.4 4.2 %rows_wire.4 = f32[16,128,256]{2,1,0:T(8,128)} custom-call(s32[3]{0:T(128)} %slot_ref.5, bf16[384,4096]{1,0:T(8,128)(2,1)} %x_ref.5), custom_call_target="tpu_custom_call" | custom-call | flops 2000000000 | bytes 7200000 | tf_op jit(solution)/shard_map/rows_wire/pallas_call | solution.py:128
  16.6 39.5 %all-to-all-done.refs_0_.refs_2_ = f32[16,136,256]{2,1,0:T(8,128)S(1)} async-done(((f32[16,136,256]{2,1,0:T(8,128)}), f32[16,136,256]{2,1,0:T(8,128)S(1)}, u32[]{:S(2)}, u32[]{:S(2)}) %all-to-all-start) | async-done | bytes 2228256 | tf_op jit(solution)/shard_map/all_to_all | solution.py:565
  56.1 11.4 %all-to-all-start.1 = ((f32[16,128,256]{2,1,0:T(8,128)}), f32[16,128,256]{2,1,0:T(8,128)}, u32[]{:S(2)}, u32[]{:S(2)}) async-start(f32[16,128,256]{2,1,0:T(8,128)} %rows_wire.4), calls=%async_computation.1 | async-start | bytes 4194304 | tf_op jit(solution)/shard_map/all_to_all | solution.py:565
  67.7 5.2 %gather_fusion.2 = f32[32,4,4096]{2,1,0:T(4,128)} fusion(f32[64,4,4096]{2,1,0:T(4,128)} %param.17, s32[1024]{0:T(1024)S(1)} %pad_clamp_fusion), kind=kCustom, calls=%fused_computation.2 | custom fusion | bytes 4194432 | tf_op jit(solution)/shard_map/gather | solution.py:598
  72.9 4.0 %reshape.165 = f32[32,4,4,1024]{3,2,1,0:T(4,128)} reshape(f32[32,4,4096]{2,1,0:T(4,128)} %gather_fusion.2) | data formatting | bytes 4194304 | tf_op jit(solution)/shard_map/reshape | solution.py:598
  80.5 2.5 fusion.41
  83.0 3.4 reshape.166
  86.4 3.4 reshape.167
  90.3 4.2 %rows_wire.5 = f32[16,128,256]{2,1,0:T(8,128)} custom-call(s32[3]{0:T(128)} %slot_ref.5, bf16[384,4096]{1,0:T(8,128)(2,1)} %x_ref.5), custom_call_target="tpu_custom_call" | custom-call | flops 2000000000 | bytes 7200000 | tf_op jit(solution)/shard_map/rows_wire/pallas_call | solution.py:128
  97.2 11.9 %all-to-all-done.1.refs_1_.refs_3_.refs_0_ = f32[16,128,256]{2,1,0:T(8,128)} async-done(((f32[16,128,256]{2,1,0:T(8,128)}), f32[16,128,256]{2,1,0:T(8,128)}, u32[]{:S(2)}, u32[]{:S(2)}) %all-to-all-start.1) | async-done | bytes 2097184 | tf_op jit(solution)/shard_map/all_to_all | solution.py:565
  109.1 10.9 %all-to-all-start.2 = ((f32[16,128,256]{2,1,0:T(8,128)}), f32[16,128,256]{2,1,0:T(8,128)S(1)}, u32[]{:S(2)}, u32[]{:S(2)}) async-start(f32[16,128,256]{2,1,0:T(8,128)} %rows_wire.5), calls=%async_computation.2 | async-start | bytes 4194304 | tf_op jit(solution)/shard_map/all_to_all | solution.py:565
  119.9 9.7 %down_partial.2 = f32[16,2,192,128]{3,2,1,0:T(8,128)} custom-call(s32[16]{0:T(128)} %fusion.22.source_ref, s32[32]{0:T(128)} %reshape.163.tenant_ref, f32[16,136,256]{2,1,0:T(8,128)} %copy-done.4, f32[16,128,256]{2,1,0:T(8,128)} %all-to-all-done.1.refs_1_.refs_3_.refs_0_, f32[16,136,256]{2,1,0:T(8,128)} %copy-done.4, ...), custom_call_target="tpu_custom_call" | custom-call | flops 4000000000 | bytes 14400000 | tf_op jit(solution)/shard_map/down_partial/pallas_call | solution.py:167
  131.5 3.3 collective-permute-done
  136.6 28.0 %collective-permute-done.1 = f32[4,2,192,128]{3,2,1,0:T(8,128)S(1)} collective-permute-done((f32[4,2,192,128]{3,2,1,0:T(8,128)S(1)}, f32[4,2,192,128]{3,2,1,0:T(8,128)S(1)}, u32[]{:S(2)}, u32[]{:S(2)}) %collective-permute-start.1) | collective-permute-done | bytes 786464 | tf_op jit(solution)/shard_map/ppermute | solution.py:50
  164.8 3.0 collective-permute-start.4
  170.3 2.1 collective-permute-done.4
  172.4 5.3 %collective-permute-done.3 = f32[2,192,128]{2,1,0:T(8,128)S(1)} collective-permute-done((f32[2,192,128]{2,1,0:T(8,128)S(1)}, f32[2,192,128]{2,1,0:T(8,128)S(1)}, u32[]{:S(2)}, u32[]{:S(2)}) %collective-permute-start.3) | collective-permute-done | bytes 196640 | tf_op jit(solution)/shard_map/ppermute | solution.py:50
  177.7 8.4 %collective-permute-done.2 = f32[2,192,128]{2,1,0:T(8,128)S(1)} collective-permute-done((f32[2,192,128]{2,1,0:T(8,128)S(1)}, f32[2,192,128]{2,1,0:T(8,128)S(1)}, u32[]{:S(2)}, u32[]{:S(2)}) %collective-permute-start.2) | collective-permute-done | bytes 196640 | tf_op jit(solution)/shard_map/ppermute | solution.py:50
  188.2 4.1 %collective-permute-done.5 = f32[2,192,128]{2,1,0:T(8,128)S(1)} collective-permute-done((f32[2,192,128]{2,1,0:T(8,128)S(1)}, f32[2,192,128]{2,1,0:T(8,128)S(1)}, u32[]{:S(2)}, u32[]{:S(2)}) %collective-permute-start.5) | collective-permute-done | bytes 196640 | tf_op jit(solution)/shard_map/ppermute | solution.py:50
  192.3 5.9 %all-to-all-start.3 = ((f32[32,4,2560]{2,1,0:T(4,128)}), f32[32,4,2560]{2,1,0:T(4,128)}, u32[]{:S(2)}, u32[]{:S(2)}) async-start(f32[32,4,2560]{2,1,0:T(4,128)} %reshape.167), calls=%async_computation.3 | async-start | bytes 2621440 | tf_op jit(solution)/shard_map/all_to_all | solution.py:565
  198.2 5.8 %down_partial.3 = f32[16,1,192,128]{3,2,1,0:T(8,128)} custom-call(s32[16]{0:T(128)} %fusion.22.source_ref, s32[16]{0:T(128)} %get-tuple-element.49.tenant_ref, f32[16,128,256]{2,1,0:T(8,128)} %copy-done.3, f32[16,128,256]{2,1,0:T(8,128)} %copy-done.3, f32[16,128,256]{2,1,0:T(8,128)} %copy-done.3, f32[16,128,256]{2,1,0:T(8,128)} %copy-done.3, ...), custom_call_target="tpu_custom_call" | custom-call | flops 2000000000 | bytes 7200000 | tf_op jit(solution)/shard_map/down_partial/pallas_call | solution.py:167
  205.5 2.1 collective-permute-done.6
  209.2 13.7 %collective-permute-done.7 = f32[4,1,192,128]{3,2,1,0:T(8,128)S(1)} collective-permute-done((f32[4,1,192,128]{3,2,1,0:T(8,128)S(1)}, f32[4,1,192,128]{3,2,1,0:T(8,128)S(1)}, u32[]{:S(2)}, u32[]{:S(2)}) %collective-permute-start.7) | collective-permute-done | bytes 393248 | tf_op jit(solution)/shard_map/ppermute | solution.py:50
  223.0 3.2 collective-permute-start.10
  228.5 3.0 collective-permute-done.9
  231.5 6.6 %collective-permute-done.8 = f32[1,192,128]{2,1,0:T(8,128)S(1)} collective-permute-done((f32[1,192,128]{2,1,0:T(8,128)S(1)}, f32[1,192,128]{2,1,0:T(8,128)S(1)}, u32[]{:S(2)}, u32[]{:S(2)}) %collective-permute-start.8) | collective-permute-done | bytes 98336 | tf_op jit(solution)/shard_map/ppermute | solution.py:50
  239.4 2.2 collective-permute-done.11
  242.3 5.6 %all-to-all-start.4 = ((f32[32,4,2560]{2,1,0:T(4,128)}), f32[32,4,2560]{2,1,0:T(4,128)S(1)}, u32[]{:S(2)}, u32[]{:S(2)}) async-start(f32[32,4,2560]{2,1,0:T(4,128)} %reshape.166), calls=%async_computation.4 | async-start | bytes 2621440 | tf_op jit(solution)/shard_map/all_to_all | solution.py:565
  251.7 19.6 %attention_grads.4 = (f32[16,2,4,2560]{3,2,1,0:T(4,128)}, f32[3,192,128]{2,1,0:T(8,128)}) custom-call(bf16[384,4096]{1,0:T(8,128)(2,1)} %refs_0_.7, bf16[384,512]{1,0:T(8,128)(2,1)} %refs_1_.7, bf16[384,512]{1,0:T(8,128)(2,1)} %refs_2_.7, bf16[384,4096]{1,0:T(8,128)(2,1)} %refs_3_.7, f32[192,128]{1,0:T(8,128)} %get-tuple-element.66.refs_4_, ...), custom_call_target="tpu_custom_call" | custom-call | flops 20000000000 | bytes 72000000 | tf_op jit(solution)/shard_map/attention_grads/pallas_call | solution.py:325
  271.3 4.4 %all-to-all-done.4 = f32[32,4,2560]{2,1,0:T(4,128)S(1)} async-done(((f32[32,4,2560]{2,1,0:T(4,128)}), f32[32,4,2560]{2,1,0:T(4,128)S(1)}, u32[]{:S(2)}, u32[]{:S(2)}) %all-to-all-start.4) | async-done | bytes 1310752 | tf_op jit(solution)/shard_map/all_to_all | solution.py:565
  276.7 7.7 %all-to-all-start.5 = ((f32[32,4,2560]{2,1,0:T(4,128)}), f32[32,4,2560]{2,1,0:T(4,128)S(1)}, u32[]{:S(2)}, u32[]{:S(2)}) async-start(f32[32,4,2560]{2,1,0:T(4,128)} %bitcast.64), calls=%async_computation.5 | async-start | bytes 2621440 | tf_op jit(solution)/shard_map/all_to_all | solution.py:565
  284.4 10.6 %attention_grads.5 = (f32[1,192,128]{2,1,0:T(8,128)}, f32[2,384,128]{2,1,0:T(8,128)}, f32[2,384,128]{2,1,0:T(8,128)}, f32[2,128,1280]{2,1,0:T(8,128)}) custom-call(bf16[384,4096]{1,0:T(8,128)(2,1)} %refs_0_.7, bf16[384,512]{1,0:T(8,128)(2,1)} %refs_1_.7, bf16[384,512]{1,0:T(8,128)(2,1)} %refs_2_.7, bf16[384,4096]{1,0:T(8,128)(2,1)} %refs_3_.7, ...), custom_call_target="tpu_custom_call" | custom-call | flops 10000000000 | bytes 36000000 | tf_op jit(solution)/shard_map/attention_grads/pallas_call | solution.py:325
  296.3 9.6 %attention_grads.6 = (f32[1,192,128]{2,1,0:T(8,128)}, f32[2,384,128]{2,1,0:T(8,128)}, f32[2,384,128]{2,1,0:T(8,128)}, f32[2,128,1280]{2,1,0:T(8,128)}) custom-call(bf16[384,4096]{1,0:T(8,128)(2,1)} %refs_0_.7, bf16[384,512]{1,0:T(8,128)(2,1)} %refs_1_.7, bf16[384,512]{1,0:T(8,128)(2,1)} %refs_2_.7, bf16[384,4096]{1,0:T(8,128)(2,1)} %refs_3_.7, ...), custom_call_target="tpu_custom_call" | custom-call | flops 6666666496 | bytes 24000000 | tf_op jit(solution)/shard_map/attention_grads/pallas_call | solution.py:325
  306.8 3.2 collective-permute-start.15
  311.9 2.0 collective-permute-start.22
  315.4 8.2 %attention_grads.7 = (f32[16,2,4,2560]{3,2,1,0:T(4,128)}, f32[1,192,128]{2,1,0:T(8,128)}) custom-call(bf16[384,4096]{1,0:T(8,128)(2,1)} %refs_0_.7, bf16[384,512]{1,0:T(8,128)(2,1)} %refs_1_.7, bf16[384,512]{1,0:T(8,128)(2,1)} %refs_2_.7, bf16[384,4096]{1,0:T(8,128)(2,1)} %refs_3_.7, f32[192,128]{1,0:T(8,128)} %get-tuple-element.66.refs_4_, ...), custom_call_target="tpu_custom_call" | custom-call | flops 3333333248 | bytes 11999999 | tf_op jit(solution)/shard_map/attention_grads/pallas_call | solution.py:325
  323.7 2.6 collective-permute-done.13
  334.7 3.4 collective-permute-start.18
  340.3 3.9 collective-permute-done.25
  345.0 2.3 collective-permute-start.26
  350.6 4.3 %all-to-all-start.6 = ((f32[32,4,2560]{2,1,0:T(4,128)}), f32[32,4,2560]{2,1,0:T(4,128)S(1)}, u32[]{:S(2)}, u32[]{:S(2)}) async-start(f32[32,4,2560]{2,1,0:T(4,128)} %bitcast.63), calls=%async_computation.6 | async-start | bytes 2621440 | tf_op jit(solution)/shard_map/all_to_all | solution.py:565
  354.9 6.0 %collective-permute-done.21 = f32[4,192,128]{2,1,0:T(8,128)S(1)} collective-permute-done((f32[4,192,128]{2,1,0:T(8,128)S(1)}, f32[4,192,128]{2,1,0:T(8,128)S(1)}, u32[]{:S(2)}, u32[]{:S(2)}) %collective-permute-start.21) | collective-permute-done | bytes 393248 | tf_op jit(solution)/shard_map/ppermute | solution.py:50
  361.1 14.4 %down_grad.1.refs_3_ = f32[64,192,256]{2,1,0:T(8,128)} custom-call(s32[32]{0:T(128)} %select_reduce_fusion.1.order_ref, s32[65]{0:T(128)} %convert_reduce_fusion.2.first_ref, s32[16]{0:T(128)} %fusion.22.source_ref, f32[16,128,256]{2,1,0:T(8,128)} %all-to-all-done.1.refs_1_.refs_3_.refs_0_, f32[16,128,256]{2,1,0:T(8,128)} %copy-done.3, ...), custom_call_target="tpu_custom_call" | custom-call | flops 15000000512 | bytes 54000000 | tf_op jit(solution)/shard_map/down_grad/pallas_call | solution.py:425
  375.5 3.0 collective-permute-start.29
  381.8 6.1 %down_grad_last.1 = f32[64,192,256]{2,1,0:T(8,128)} custom-call(s32[16]{0:T(128)} %copy-done.16, s32[16]{0:T(128)} %select_reduce_fusion.2.leader_ref, s32[16]{0:T(128)} %fusion.22.source_ref, f32[16,136,256]{2,1,0:T(8,128)} %copy-done.4, f32[8,192,128]{2,1,0:T(8,128)} %copy-done.11, f32[8,192,128]{2,1,0:T(8,128)} %copy-done.12, ...), custom_call_target="tpu_custom_call", output_to_operand_aliasing={{}: (6, {})} | custom-call | flops 6000000000 | bytes 21600000 | tf_op jit(solution)/shard_map/down_grad_last/pallas_call | solution.py:486
  389.0 6.8 %up_grad.1 = (f32[64,4,4096]{2,1,0:T(4,128)}, f32[64,4,4,256]{3,2,1,0:T(4,128)}) custom-call(s32[32]{0:T(128)} %select_reduce_fusion.order_ref, s32[65]{0:T(128)} %convert_reduce_fusion.first_ref, f32[32,4,2560]{2,1,0:T(4,128)} %copy-done.8, f32[32,4,2560]{2,1,0:T(4,128)} %copy-done.10), custom_call_target="tpu_custom_call" | custom-call | flops 6000000000 | bytes 21600000 | tf_op jit(solution)/shard_map/up_grad/pallas_call | solution.py:542
  (148 shorter events, 52.2 us)
Async XLA Ops:
  0.6 76.3 %copy-start = (f32[64,4,4,256]{3,2,1,0:T(4,128)S(1)}, f32[64,4,4,256]{3,2,1,0:T(4,128)}, u32[]{:S(2)}) copy-start(f32[64,4,4,256]{3,2,1,0:T(4,128)} %param.18) | copy-start | bytes 3145732
  5.1 51.1 %all-to-all-start = ((f32[16,136,256]{2,1,0:T(8,128)}), f32[16,136,256]{2,1,0:T(8,128)S(1)}, u32[]{:S(2)}, u32[]{:S(2)}) async-start(f32[16,136,256]{2,1,0:T(8,128)} %rows_wire.3), calls=%async_computation | async-start | bytes 4456448 | tf_op jit(solution)/shard_map/all_to_all | solution.py:565
  16.6 50.9 %copy-start.2 = (s32[16,2]{0,1:T(2,128)S(1)}, s32[16,2]{0,1:T(2,128)}, u32[]{:S(2)}) copy-start(s32[16,2]{0,1:T(2,128)} %param.21) | copy-start | bytes 388
  56.1 38.4 %copy-start.4 = (f32[16,136,256]{2,1,0:T(8,128)}, f32[16,136,256]{2,1,0:T(8,128)S(1)}, u32[]{:S(2)}) copy-start(f32[16,136,256]{2,1,0:T(8,128)S(1)} %all-to-all-done.refs_0_.refs_2_) | copy-start | bytes 6684676
  56.1 53.0 %all-to-all-start.1 = ((f32[16,128,256]{2,1,0:T(8,128)}), f32[16,128,256]{2,1,0:T(8,128)}, u32[]{:S(2)}, u32[]{:S(2)}) async-start(f32[16,128,256]{2,1,0:T(8,128)} %rows_wire.4), calls=%async_computation.1 | async-start | bytes 4194304 | tf_op jit(solution)/shard_map/all_to_all | solution.py:565
  109.1 83.2 %all-to-all-start.2 = ((f32[16,128,256]{2,1,0:T(8,128)}), f32[16,128,256]{2,1,0:T(8,128)S(1)}, u32[]{:S(2)}, u32[]{:S(2)}) async-start(f32[16,128,256]{2,1,0:T(8,128)} %rows_wire.5), calls=%async_computation.2 | async-start | bytes 4194304 | tf_op jit(solution)/shard_map/all_to_all | solution.py:565
  131.4 3.5 collective-permute-start
  135.1 29.5 %collective-permute-start.1 = (f32[4,2,192,128]{3,2,1,0:T(8,128)S(1)}, f32[4,2,192,128]{3,2,1,0:T(8,128)S(1)}, u32[]{:S(2)}, u32[]{:S(2)}) collective-permute-start(f32[4,2,192,128]{3,2,1,0:T(8,128)S(1)} %slice.114), channel_id=1, source_target_pairs={{0,4},{2,6},{4,0},{6,2},{8,12},{10,14},{12,8},{14,10},{16,20},{18,... | collective-permute-start | bytes 2359304 | tf_op jit(solution)/shard_map/ppermute | solution.py:50
  164.8 7.6 %collective-permute-start.4 = (f32[2,192,128]{2,1,0:T(8,128)S(1)}, f32[2,192,128]{2,1,0:T(8,128)S(1)}, u32[]{:S(2)}, u32[]{:S(2)}) collective-permute-start(f32[2,192,128]{2,1,0:T(8,128)S(1)} %get-tuple-element.60), channel_id=1, source_target_pairs={{0,24},{2,26},{4,28},{6,30},{8,16},{10,18},{12,20},{14,22},{16,8},... | collective-permute-start | bytes 589832 | tf_op jit(solution)/shard_map/ppermute | solution.py:50
  167.8 9.9 %collective-permute-start.3 = (f32[2,192,128]{2,1,0:T(8,128)S(1)}, f32[2,192,128]{2,1,0:T(8,128)S(1)}, u32[]{:S(2)}, u32[]{:S(2)}) collective-permute-start(f32[2,192,128]{2,1,0:T(8,128)S(1)} %get-tuple-element.61), channel_id=1, source_target_pairs={{0,8},{2,10},{4,12},{6,14},{8,0},{10,2},{12,4},{14,6},{16,24},{18,... | collective-permute-start | bytes 589832 | tf_op jit(solution)/shard_map/ppermute | solution.py:50
  169.2 16.9 %collective-permute-start.2 = (f32[2,192,128]{2,1,0:T(8,128)S(1)}, f32[2,192,128]{2,1,0:T(8,128)S(1)}, u32[]{:S(2)}, u32[]{:S(2)}) collective-permute-start(f32[2,192,128]{2,1,0:T(8,128)S(1)} %get-tuple-element.59), channel_id=1, source_target_pairs={{0,16},{2,18},{4,20},{6,22},{8,24},{10,26},{12,28},{14,30},{16,0},... | collective-permute-start | bytes 589832 | tf_op jit(solution)/shard_map/ppermute | solution.py:50
  186.2 6.1 %collective-permute-start.5 = (f32[2,192,128]{2,1,0:T(8,128)S(1)}, f32[2,192,128]{2,1,0:T(8,128)S(1)}, u32[]{:S(2)}, u32[]{:S(2)}) collective-permute-start(f32[2,192,128]{2,1,0:T(8,128)S(1)} %fusion.2), channel_id=1, source_target_pairs={{0,1},{1,0},{2,3},{3,2},{4,5},{5,4},{6,7},{7,6},{8,9},{9,8},{10,11... | collective-permute-start | bytes 589832 | tf_op jit(solution)/shard_map/ppermute | solution.py:50
  188.2 191.9 %copy-start.16 = (s32[16]{0:T(128)}, s32[16]{0:T(128)S(1)}, u32[]{:S(2)}) copy-start(s32[16]{0:T(128)S(1)} %get-tuple-element.50.owner_ref) | copy-start | bytes 196
  192.3 50.0 %all-to-all-start.3 = ((f32[32,4,2560]{2,1,0:T(4,128)}), f32[32,4,2560]{2,1,0:T(4,128)}, u32[]{:S(2)}, u32[]{:S(2)}) async-start(f32[32,4,2560]{2,1,0:T(4,128)} %reshape.167), calls=%async_computation.3 | async-start | bytes 2621440 | tf_op jit(solution)/shard_map/all_to_all | solution.py:565
  205.3 2.4 collective-permute-start.6
  207.8 15.1 %collective-permute-start.7 = (f32[4,1,192,128]{3,2,1,0:T(8,128)S(1)}, f32[4,1,192,128]{3,2,1,0:T(8,128)S(1)}, u32[]{:S(2)}, u32[]{:S(2)}) collective-permute-start(f32[4,1,192,128]{3,2,1,0:T(8,128)S(1)} %slice.126), channel_id=1, source_target_pairs={{0,4},{2,6},{4,0},{6,2},{8,12},{10,14},{12,8},{14,10},{16,20},{18,... | collective-permute-start | bytes 1179656 | tf_op jit(solution)/shard_map/ppermute | solution.py:50
  223.0 24.9 %copy-start.15 = (s32[384]{0:T(512)S(1)}, s32[384]{0:T(512)}, u32[]{:S(2)}) copy-start(s32[384]{0:T(512)} %param.19) | copy-start | bytes 4612
  223.0 26.3 %copy-start.17 = (s32[3]{0:T(128)S(1)}, s32[3]{0:T(128)}, u32[]{:S(2)}) copy-start(s32[3]{0:T(128)} %slot_ref.5) | copy-start | bytes 40
  223.0 5.4 %collective-permute-start.10 = (f32[1,192,128]{2,1,0:T(8,128)S(1)}, f32[1,192,128]{2,1,0:T(8,128)S(1)}, u32[]{:S(2)}, u32[]{:S(2)}) collective-permute-start(f32[1,192,128]{2,1,0:T(8,128)S(1)} %get-tuple-element.63), channel_id=1, source_target_pairs={{0,24},{2,26},{4,28},{6,30},{8,16},{10,18},{12,20},{14,22},{16,8},... | collective-permute-start | bytes 294920 | tf_op jit(solution)/shard_map/ppermute | solution.py:50
  226.2 5.2 %collective-permute-start.9 = (f32[1,192,128]{2,1,0:T(8,128)S(1)}, f32[1,192,128]{2,1,0:T(8,128)S(1)}, u32[]{:S(2)}, u32[]{:S(2)}) collective-permute-start(f32[1,192,128]{2,1,0:T(8,128)S(1)} %get-tuple-element.64), channel_id=1, source_target_pairs={{0,8},{2,10},{4,12},{6,14},{8,0},{10,2},{12,4},{14,6},{16,24},{18,... | collective-permute-start | bytes 294920 | tf_op jit(solution)/shard_map/ppermute | solution.py:50
  226.9 11.2 %collective-permute-start.8 = (f32[1,192,128]{2,1,0:T(8,128)S(1)}, f32[1,192,128]{2,1,0:T(8,128)S(1)}, u32[]{:S(2)}, u32[]{:S(2)}) collective-permute-start(f32[1,192,128]{2,1,0:T(8,128)S(1)} %get-tuple-element.62), channel_id=1, source_target_pairs={{0,16},{2,18},{4,20},{6,22},{8,24},{10,26},{12,28},{14,30},{16,0},... | collective-permute-start | bytes 294920 | tf_op jit(solution)/shard_map/ppermute | solution.py:50
  238.1 3.5 collective-permute-start.11
  242.3 33.4 %all-to-all-start.4 = ((f32[32,4,2560]{2,1,0:T(4,128)}), f32[32,4,2560]{2,1,0:T(4,128)S(1)}, u32[]{:S(2)}, u32[]{:S(2)}) async-start(f32[32,4,2560]{2,1,0:T(4,128)} %reshape.166), calls=%async_computation.4 | async-start | bytes 2621440 | tf_op jit(solution)/shard_map/all_to_all | solution.py:565
  276.7 51.0 %all-to-all-start.5 = ((f32[32,4,2560]{2,1,0:T(4,128)}), f32[32,4,2560]{2,1,0:T(4,128)S(1)}, u32[]{:S(2)}, u32[]{:S(2)}) async-start(f32[32,4,2560]{2,1,0:T(4,128)} %bitcast.64), calls=%async_computation.5 | async-start | bytes 2621440 | tf_op jit(solution)/shard_map/all_to_all | solution.py:565
  295.0 11.1 %collective-permute-start.12 = (f32[1,192,128]{2,1,0:T(8,128)}, f32[1,192,128]{2,1,0:T(8,128)S(1)}, u32[]{:S(2)}, u32[]{:S(2)}) collective-permute-start(f32[1,192,128]{2,1,0:T(8,128)} %get-tuple-element.37), channel_id=1, source_target_pairs={{0,1},{1,0},{2,3},{3,2},{4,5},{5,4},{6,7},{7,6},{8,9},{9,8},{10,11... | collective-permute-start | bytes 294920 | tf_op jit(solution)/shard_map/ppermute | solution.py:50
  296.3 9.8 %copy-start.14 = (f32[1,192,128]{2,1,0:T(8,128)S(1)}, f32[1,192,128]{2,1,0:T(8,128)}, u32[]{:S(2)}) copy-start(f32[1,192,128]{2,1,0:T(8,128)} %get-tuple-element.37) | copy-start | bytes 294916
  305.9 4.5 %collective-permute-start.16 = (f32[1,192,128]{2,1,0:T(8,128)}, f32[1,192,128]{2,1,0:T(8,128)S(1)}, u32[]{:S(2)}, u32[]{:S(2)}) collective-permute-start(f32[1,192,128]{2,1,0:T(8,128)} %get-tuple-element.43), channel_id=1, source_target_pairs={{0,1},{1,0},{2,3},{3,2},{4,5},{5,4},{6,7},{7,6},{8,9},{9,8},{10,11... | collective-permute-start | bytes 294920 | tf_op jit(solution)/shard_map/ppermute | solution.py:50
  306.8 16.8 %collective-permute-start.15 = (f32[1,192,128]{2,1,0:T(8,128)S(1)}, f32[1,192,128]{2,1,0:T(8,128)S(1)}, u32[]{:S(2)}, u32[]{:S(2)}) collective-permute-start(f32[1,192,128]{2,1,0:T(8,128)S(1)} %get-tuple-element.52), channel_id=1, source_target_pairs={{0,24},{2,26},{4,28},{6,30},{8,16},{10,18},{12,20},{14,22},{16,8},... | collective-permute-start | bytes 294920 | tf_op jit(solution)/shard_map/ppermute | solution.py:50
  310.0 13.8 %collective-permute-start.14 = (f32[1,192,128]{2,1,0:T(8,128)S(1)}, f32[1,192,128]{2,1,0:T(8,128)S(1)}, u32[]{:S(2)}, u32[]{:S(2)}) collective-permute-start(f32[1,192,128]{2,1,0:T(8,128)S(1)} %get-tuple-element.52), channel_id=1, source_target_pairs={{0,8},{2,10},{4,12},{6,14},{8,0},{10,2},{12,4},{14,6},{16,24},{18,... | collective-permute-start | bytes 294920 | tf_op jit(solution)/shard_map/ppermute | solution.py:50
  310.0 16.4 %collective-permute-start.13 = (f32[1,192,128]{2,1,0:T(8,128)S(1)}, f32[1,192,128]{2,1,0:T(8,128)S(1)}, u32[]{:S(2)}, u32[]{:S(2)}) collective-permute-start(f32[1,192,128]{2,1,0:T(8,128)S(1)} %get-tuple-element.52), channel_id=1, source_target_pairs={{0,16},{2,18},{4,20},{6,22},{8,24},{10,26},{12,28},{14,30},{16,0},... | collective-permute-start | bytes 294920 | tf_op jit(solution)/shard_map/ppermute | solution.py:50
  311.9 17.6 %collective-permute-start.22 = (f32[1,192,128]{2,1,0:T(8,128)S(1)}, f32[1,192,128]{2,1,0:T(8,128)S(1)}, u32[]{:S(2)}, u32[]{:S(2)}) collective-permute-start(f32[1,192,128]{2,1,0:T(8,128)S(1)} %get-tuple-element.54), channel_id=1, source_target_pairs={{0,16},{2,18},{4,20},{6,22},{8,24},{10,26},{12,28},{14,30},{16,0},... | collective-permute-start | bytes 294920 | tf_op jit(solution)/shard_map/ppermute | solution.py:50
  313.9 15.6 %collective-permute-start.23 = (f32[1,192,128]{2,1,0:T(8,128)S(1)}, f32[1,192,128]{2,1,0:T(8,128)S(1)}, u32[]{:S(2)}, u32[]{:S(2)}) collective-permute-start(f32[1,192,128]{2,1,0:T(8,128)S(1)} %get-tuple-element.54), channel_id=1, source_target_pairs={{0,8},{2,10},{4,12},{6,14},{8,0},{10,2},{12,4},{14,6},{16,24},{18,... | collective-permute-start | bytes 294920 | tf_op jit(solution)/shard_map/ppermute | solution.py:50
  323.6 11.1 %copy-start.13 = (f32[1,192,128]{2,1,0:T(8,128)S(1)}, f32[1,192,128]{2,1,0:T(8,128)}, u32[]{:S(2)}) copy-start(f32[1,192,128]{2,1,0:T(8,128)} %get-tuple-element.44) | copy-start | bytes 294916
  323.6 5.9 %collective-permute-start.24 = (f32[1,192,128]{2,1,0:T(8,128)S(1)}, f32[1,192,128]{2,1,0:T(8,128)S(1)}, u32[]{:S(2)}, u32[]{:S(2)}) collective-permute-start(f32[1,192,128]{2,1,0:T(8,128)S(1)} %get-tuple-element.54), channel_id=1, source_target_pairs={{0,24},{2,26},{4,28},{6,30},{8,16},{10,18},{12,20},{14,22},{16,8},... | collective-permute-start | bytes 294920 | tf_op jit(solution)/shard_map/ppermute | solution.py:50
  326.4 20.8 %collective-permute-start.27 = (f32[4,192,128]{2,1,0:T(8,128)S(1)}, f32[4,192,128]{2,1,0:T(8,128)S(1)}, u32[]{:S(2)}, u32[]{:S(2)}) collective-permute-start(f32[4,192,128]{2,1,0:T(8,128)S(1)} %pad_maximum_fusion), channel_id=1, source_target_pairs={{0,4},{2,6},{4,0},{6,2},{8,12},{10,14},{12,8},{14,10},{16,20},{18,... | collective-permute-start | bytes 1179656 | tf_op jit(solution)/shard_map/ppermute | solution.py:50
  327.7 21.0 %copy-start.8 = (f32[32,4,2560]{2,1,0:T(4,128)}, f32[32,4,2560]{2,1,0:T(4,128)S(1)}, u32[]{:S(2)}) copy-start(f32[32,4,2560]{2,1,0:T(4,128)S(1)} %all-to-all-done.5.refs_0_) | copy-start | bytes 3932164
  327.7 7.0 %collective-permute-start.17 = (f32[1,192,128]{2,1,0:T(8,128)}, f32[1,192,128]{2,1,0:T(8,128)S(1)}, u32[]{:S(2)}, u32[]{:S(2)}) collective-permute-start(f32[1,192,128]{2,1,0:T(8,128)} %get-tuple-element.44), channel_id=1, source_target_pairs={{0,1},{1,0},{2,3},{3,2},{4,5},{5,4},{6,7},{7,6},{8,9},{9,8},{10,11... | collective-permute-start | bytes 294920 | tf_op jit(solution)/shard_map/ppermute | solution.py:50
  329.6 14.6 %collective-permute-start.25 = (f32[4,192,128]{2,1,0:T(8,128)S(1)}, f32[4,192,128]{2,1,0:T(8,128)S(1)}, u32[]{:S(2)}, u32[]{:S(2)}) collective-permute-start(f32[4,192,128]{2,1,0:T(8,128)S(1)} %pad_maximum_fusion.2), channel_id=1, source_target_pairs={{0,4},{2,6},{4,0},{6,2},{8,12},{10,14},{12,8},{14,10},{16,20},{18,... | collective-permute-start | bytes 1179656 | tf_op jit(solution)/shard_map/ppermute | solution.py:50
  334.7 13.9 %collective-permute-start.18 = (f32[1,192,128]{2,1,0:T(8,128)S(1)}, f32[1,192,128]{2,1,0:T(8,128)S(1)}, u32[]{:S(2)}, u32[]{:S(2)}) collective-permute-start(f32[1,192,128]{2,1,0:T(8,128)S(1)} %get-tuple-element.56), channel_id=1, source_target_pairs={{0,16},{2,18},{4,20},{6,22},{8,24},{10,26},{12,28},{14,30},{16,0},... | collective-permute-start | bytes 294920 | tf_op jit(solution)/shard_map/ppermute | solution.py:50
  338.2 10.5 %collective-permute-start.19 = (f32[1,192,128]{2,1,0:T(8,128)S(1)}, f32[1,192,128]{2,1,0:T(8,128)S(1)}, u32[]{:S(2)}, u32[]{:S(2)}) collective-permute-start(f32[1,192,128]{2,1,0:T(8,128)S(1)} %get-tuple-element.56), channel_id=1, source_target_pairs={{0,8},{2,10},{4,12},{6,14},{8,0},{10,2},{12,4},{14,6},{16,24},{18,... | collective-permute-start | bytes 294920 | tf_op jit(solution)/shard_map/ppermute | solution.py:50
  338.3 10.4 %collective-permute-start.20 = (f32[1,192,128]{2,1,0:T(8,128)S(1)}, f32[1,192,128]{2,1,0:T(8,128)S(1)}, u32[]{:S(2)}, u32[]{:S(2)}) collective-permute-start(f32[1,192,128]{2,1,0:T(8,128)S(1)} %get-tuple-element.56), channel_id=1, source_target_pairs={{0,24},{2,26},{4,28},{6,30},{8,16},{10,18},{12,20},{14,22},{16,8},... | collective-permute-start | bytes 294920 | tf_op jit(solution)/shard_map/ppermute | solution.py:50
  345.0 16.1 %collective-permute-start.26 = (f32[8,192,128]{2,1,0:T(8,128)}, f32[8,192,128]{2,1,0:T(8,128)}, u32[]{:S(2)}, u32[]{:S(2)}) collective-permute-start(f32[8,192,128]{2,1,0:T(8,128)} %constant_dynamic-update-slice_fusion.7.refs_2_), channel_id=1, source_target_pairs={{0,2},{2,0},{4,6},{6,4},{8,10},{10,8},{12,14},{14,12},{16,18},{18,... | collective-permute-start | bytes 2359304 | tf_op jit(solution)/shard_map/ppermute | solution.py:50
  348.1 13.0 %collective-permute-start.28 = (f32[8,192,128]{2,1,0:T(8,128)}, f32[8,192,128]{2,1,0:T(8,128)}, u32[]{:S(2)}, u32[]{:S(2)}) collective-permute-start(f32[8,192,128]{2,1,0:T(8,128)} %constant_dynamic-update-slice_fusion.12.refs_4_), channel_id=1, source_target_pairs={{0,2},{2,0},{4,6},{6,4},{8,10},{10,8},{12,14},{14,12},{16,18},{18,... | collective-permute-start | bytes 2359304 | tf_op jit(solution)/shard_map/ppermute | solution.py:50
  348.7 12.3 %collective-permute-start.21 = (f32[4,192,128]{2,1,0:T(8,128)S(1)}, f32[4,192,128]{2,1,0:T(8,128)S(1)}, u32[]{:S(2)}, u32[]{:S(2)}) collective-permute-start(f32[4,192,128]{2,1,0:T(8,128)S(1)} %pad_maximum_fusion.1), channel_id=1, source_target_pairs={{0,4},{2,6},{4,0},{6,2},{8,12},{10,14},{12,8},{14,10},{16,20},{18,... | collective-permute-start | bytes 1179656 | tf_op jit(solution)/shard_map/ppermute | solution.py:50
  350.6 37.2 %all-to-all-start.6 = ((f32[32,4,2560]{2,1,0:T(4,128)}), f32[32,4,2560]{2,1,0:T(4,128)S(1)}, u32[]{:S(2)}, u32[]{:S(2)}) async-start(f32[32,4,2560]{2,1,0:T(4,128)} %bitcast.63), calls=%async_computation.6 | async-start | bytes 2621440 | tf_op jit(solution)/shard_map/all_to_all | solution.py:565
  361.0 14.5 %copy-start.11 = (f32[8,192,128]{2,1,0:T(8,128)}, f32[8,192,128]{2,1,0:T(8,128)S(1)}, u32[]{:S(2)}) copy-start(f32[8,192,128]{2,1,0:T(8,128)S(1)} %constant_dynamic-update-slice_fusion.2.refs_1_) | copy-start | bytes 2359300
  375.5 5.4 %collective-permute-start.29 = (f32[8,192,128]{2,1,0:T(8,128)S(1)}, f32[8,192,128]{2,1,0:T(8,128)S(1)}, u32[]{:S(2)}, u32[]{:S(2)}) collective-permute-start(f32[8,192,128]{2,1,0:T(8,128)S(1)} %constant_dynamic-update-slice_fusion.2.refs_1_), channel_id=1, source_target_pairs={{0,2},{2,0},{4,6},{6,4},{8,10},{10,8},{12,14},{14,12},{16,18},{18,... | collective-permute-start | bytes 2359304 | tf_op jit(solution)/shard_map/ppermute | solution.py:50
  389.0 6.8 %copy-start.1 = (f32[64,4,4,256]{3,2,1,0:T(4,128)S(1)}, f32[64,4,4,256]{3,2,1,0:T(4,128)}, u32[]{:S(2)}) copy-start(f32[64,4,4,256]{3,2,1,0:T(4,128)} %param.18) | copy-start | bytes 3145732
  (7 other events, 19.7 us)

commit v4 on v3

--- a/solution.py
+++ b/solution.py
@@ -58,12 +58,17 @@
     return a
 
 
-def scatter_sum(part, axis, size):
+def scatter_near(part, axis, size):
     bit = 1
     while bit < min(size, 4):
         half = part.shape[0] // 2
         part = part[:half] + swap(part[half:], axis, size, bit)
         bit *= 2
+    return part
+
+
+def scatter_far(part, axis, size):
+    bit = min(size, 4)
     moved = [
         swap(part[k], axis, size, bit_reversed(k, part.shape[0]) * bit)
         for k in range(1, part.shape[0])
@@ -263,15 +268,14 @@
             pr[:reach, at] = probs.astype(BF16)
         dk[:reach] += mm(ds[:reach], q_s[...])
         dv[:reach] += mm(pr[:reach], up_s[...])
-        dq = split2(mm(k_t[:, :reach], ds[:reach]))
+        dq = mm(k_t[:, :reach], ds[:reach]).astype(BF16)
         dk_b, dv_b = split2(dk[here]), split2(dv[here])
         lct = [(lct_h[part, b], lct_l[part, b]) for part in range(3)]
         both = jnp.zeros((slots * rank, block), F32)
         for h in range(groups):
             at, lanes = slice(h * block, (h + 1) * block), slice(h * head, (h + 1) * head)
-            dq_h = (dq[0][:, at], dq[1][:, at])
-            du[:, lanes] += mm3(lct[0], dq_h, NT)
-            both += mm3((u_q[0][:, lanes], u_q[1][:, lanes]), dq_h)
+            du[:, lanes] += mm(lct[0][0], dq[:, at], NT)
+            both += mm(u_q[0][:, lanes], dq[:, at])
         du[:, wide : wide + head] += mm3(lct[1], dk_b)
         du[:, wide + head :] += mm3(lct[2], dv_b)
         for part, full in enumerate((both, mm3(u_k, dk_b, NT), mm3(u_v, dv_b, NT))):
@@ -377,7 +381,7 @@
     )
 
 
-def down_grad_kernel(blocks, per_step, order_ref, first_ref, source_ref, *refs):
+def down_grad_kernel(blocks, per_step, order_ref, first_ref, owner_ref, source_ref, *refs):
     x_refs, g_refs = refs[:blocks], refs[blocks : 3 * blocks]
     out_ref, x_all, g_ref, sems = refs[3 * blocks :]
     half = g_refs[0].shape[0]
@@ -401,31 +405,42 @@
         for copy in copies:
             copy.wait()
 
-    for t in range(per_step):
-        tenant = step * per_step + t
-        out_ref[t] = jnp.zeros(out_ref.shape[1:], F32)
-
-        def add(e, carry):
-            item = order_ref[e]
+    out_ref[...] = jnp.zeros_like(out_ref)
+    start, stop = first_ref[step * per_step], first_ref[(step + 1) * per_step]
+    unroll = 4
+
+    def add(i, carry):
+        terms = []
+        for u in range(unroll):
+            e = start + i * unroll + u
+            item = order_ref[jnp.minimum(e, stop - 1)]
             place = item // blocks
             b = item - place * blocks
             x = x_all[b, source_ref[place]].astype(BF16)
             high, low = split2(g_ref[b, place])
-            out_ref[t] += mm(high, x) + mm(low, x)
-            return carry
-
-        lax.fori_loop(first_ref[tenant], first_ref[tenant + 1], add, 0)
-
-
-def down_grad(xs, g, order, first, source, tenants):
+            terms.append((e, item, mm(high, x) + mm(low, x)))
+        for e, item, term in terms:
+            t = owner_ref[item] - step * per_step
+
+            @pl.when(e < stop)
+            def _():
+                out_ref[t] += term
+
+        return carry
+
+    lax.fori_loop(0, (stop - start + unroll - 1) // unroll, add, 0)
+
+
+def down_grad(xs, g, owners, source, tenants):
     blocks = len(xs)
     n, rows, width = xs[1].shape
     rank = g[0].shape[1]
+    order, first = by_tenant(owners, tenants)
     per_step = 8
     return pl.pallas_call(
         functools.partial(down_grad_kernel, blocks, per_step),
         grid_spec=pltpu.PrefetchScalarGridSpec(
-            num_scalar_prefetch=3,
+            num_scalar_prefetch=4,
             grid=(tenants // per_step,),
             in_specs=[pl.BlockSpec(memory_space=pl.ANY)] * (3 * blocks),
             out_specs=pl.BlockSpec((per_step, rank, width), lambda i, *_: (i, 0, 0)),
@@ -437,9 +452,9 @@
         ),
         out_shape=jax.ShapeDtypeStruct((tenants, rank, width), F32),
         compiler_params=pltpu.CompilerParams(vmem_limit_bytes=VMEM_LIMIT),
-        cost_estimate=cost(15),
+        cost_estimate=cost(14),
         name="down_grad",
-    )(order, first, source, *xs, *g)
+    )(order, first, owners, source, *xs, *g)
 
 
 def down_grad_last_kernel(owner_ref, leader_ref, source_ref, *refs):
@@ -618,14 +633,16 @@
 
     weights = jnp.swapaxes(adapter_down_weight, 1, 2)
     part = down_partial(xs[:-1], weights, source, owners[:, :-1], block)
-    early = sum_over(scatter_sum(part, "dp", dp_count), "mp", mp_count)
+    near = scatter_near(part, "dp", dp_count)
+    early = sum_over(scatter_far(near, "dp", dp_count), "mp", mp_count)
     part = down_partial(xs[-1:], weights, source, owners[:, -1:], block)
-    late = sum_over(scatter_sum(part, "dp", dp_count), "mp", mp_count)
+    late_part = scatter_far(scatter_near(part, "dp", dp_count), "dp", dp_count)
+    late = sum_over(late_part, "mp", mp_count)
     lows = [early[b] for b in range(blocks - 1)] + [late[0]]
 
     panels = []
     for c in range(calls):
-        own = after(owns[c], xs[-1], early) if c == 0 else after(owns[c], panels[-1], late)
+        own = after(owns[c], xs[-1], near) if c == 0 else after(owns[c], panels[-1], late_part)
         panels.append(exchange(own).reshape(dp_count, slots, piece, heads * per))
 
     attend = functools.partial(
@@ -668,8 +685,7 @@
     dus.append(exchange(du))
 
     early = [half for pair in g_halves[1:] for half in pair]
-    order, first = by_tenant(owners[:, 1:].reshape(-1), tenants)
-    grad_down = down_grad(xs[1:], early, order, first, source, tenants)
+    grad_down = down_grad(xs[1:], early, owners[:, 1:].reshape(-1), source, tenants)
     fars[0] = after(fars[0], grad_down)
     g_halves[0] = (fars[0], swap(fars[0], "dp", dp_count, 1))
     grad_down = down_grad_last(xs[0], g_halves[0], grad_down, owners[:, 0], source)

time: 397 us -> 383 us (0.965)
  waiting for transfers between devices: 148 us -> 130 us
  starting transfers between devices: 94.1 us -> 109 us
  Pallas kernels: 104 us -> 95.7 us
    ppermute x30, waiting for transfers between devices: 92.5 us -> 69.6 us  [swap(): return lax.ppermute(a, axis, [(i, i ^ bit) for i in range(size)])]
    ppermute x30, starting transfers between devices: 41.1 us -> 54.5 us  [swap(): return lax.ppermute(a, axis, [(i, i ^ bit) for i in range(size)])]
    pallas_call x4, Pallas kernels: 48.1 us -> 42.1 us  [attention(): pl.pallas_call(functools.partial(attention_kernel, groups, slots, blocks,...]
    all_to_all x7, waiting for transfers between devices: 55.8 us -> 60.4 us  [exchange(): return lax.all_to_all(a, 'dp', split_axis=0, concat_axis=0, tiled=True)]
    unnamed x49 -> x51, local copies, waits for them, and re-layouts: 9.58 us -> 8.75 us
  transfers between devices with their start and end apart: 37 -> 37, of which waited for: 19 -> 15; matrix products, arithmetic and copies ran while one was open for 11% -> 11% of each run, Pallas kernels for 23% -> 22%
where the time goes in v4:
time: 383 us; the launch traced here: 382 us
  waiting for transfers between devices  130 us (34%)
  starting transfers between devices  109 us (28%)
  Pallas kernels  95.7 us (25%)
  local copies, waits for them, and re-layouts  37.6 us (10%)
  other arithmetic  8.76 us (2%)
    ppermute x30, waiting for transfers between devices, swap(): return lax.ppermute(a, axis, [(i, i ^ bit) for i in range(size)])  69.6 us
    all_to_all x7, waiting for transfers between devices, exchange(): return lax.all_to_all(a, 'dp', split_axis=0, concat_axis=0, tiled=True)  60.4 us
    ppermute x30, starting transfers between devices, swap(): return lax.ppermute(a, axis, [(i, i ^ bit) for i in range(size)])  54.5 us
    all_to_all x7, starting transfers between devices, exchange(): return lax.all_to_all(a, 'dp', split_axis=0, concat_axis=0, tiled=True)  54.2 us
    pallas_call x4, Pallas kernels, attention(): pl.pallas_call(functools.partial(attention_kernel, groups, slots, blocks,...  42.1 us
    pallas_call x2, Pallas kernels, down_partial(): pl.pallas_call(functools.partial(down_kernel, count, calls), grid_spec=pl...  15.7 us
    pallas_call x3, Pallas kernels, rows_wire(): pl.pallas_call(functools.partial(wire_kernel, per), grid_spec=pltpu.Prefe...  12.9 us
    pallas_call x1, Pallas kernels, down_grad(): pl.pallas_call(functools.partial(down_grad_kernel, blocks, per_step), gri...  12.2 us
  transfers between devices with their start and end apart: 37, of which 15 were waited for; matrix products, arithmetic and copies ran while one was open for 11% of the time, Pallas kernels for 22%

profile of v4, /device:TPU:1, one launch (start us, length us, event | category | flops | bytes accessed | tf_op | source)
XLA Modules:
  0.0 381.8 jit_solution(13335268909082285204)
XLA Ops:
  0.6 4.4 %rows_wire.3 = f32[16,136,256]{2,1,0:T(8,128)} custom-call(s32[3]{0:T(128)} %slot_ref.5, bf16[384,4096]{1,0:T(8,128)(2,1)} %x_ref.5), custom_call_target="tpu_custom_call" | custom-call | flops 2000000000 | bytes 7200000 | tf_op jit(solution)/shard_map/rows_wire/pallas_call | solution.py:133
  5.1 7.3 %all-to-all-start = ((f32[16,136,256]{2,1,0:T(8,128)}), f32[16,136,256]{2,1,0:T(8,128)S(1)}, u32[]{:S(2)}, u32[]{:S(2)}) async-start(f32[16,136,256]{2,1,0:T(8,128)} %rows_wire.3), calls=%async_computation | async-start | bytes 4456448 | tf_op jit(solution)/shard_map/all_to_all | solution.py:580
  12.4 4.2 %rows_wire.4 = f32[16,128,256]{2,1,0:T(8,128)} custom-call(s32[3]{0:T(128)} %slot_ref.5, bf16[384,4096]{1,0:T(8,128)(2,1)} %x_ref.5), custom_call_target="tpu_custom_call" | custom-call | flops 2000000000 | bytes 7200000 | tf_op jit(solution)/shard_map/rows_wire/pallas_call | solution.py:133
  16.6 39.5 %all-to-all-done.refs_0_.refs_2_ = f32[16,136,256]{2,1,0:T(8,128)S(1)} async-done(((f32[16,136,256]{2,1,0:T(8,128)}), f32[16,136,256]{2,1,0:T(8,128)S(1)}, u32[]{:S(2)}, u32[]{:S(2)}) %all-to-all-start) | async-done | bytes 2228256 | tf_op jit(solution)/shard_map/all_to_all | solution.py:580
  56.1 11.4 %all-to-all-start.1 = ((f32[16,128,256]{2,1,0:T(8,128)}), f32[16,128,256]{2,1,0:T(8,128)}, u32[]{:S(2)}, u32[]{:S(2)}) async-start(f32[16,128,256]{2,1,0:T(8,128)} %rows_wire.4), calls=%async_computation.1 | async-start | bytes 4194304 | tf_op jit(solution)/shard_map/all_to_all | solution.py:580
  67.7 5.2 %gather_fusion.2 = f32[32,4,4096]{2,1,0:T(4,128)} fusion(f32[64,4,4096]{2,1,0:T(4,128)} %param.17, s32[1024]{0:T(1024)S(1)} %pad_clamp_fusion), kind=kCustom, calls=%fused_computation.2 | custom fusion | bytes 4194432 | tf_op jit(solution)/shard_map/gather | solution.py:613
  72.9 3.0 reshape.166
  76.0 1.6 gather_fusion.3
  78.7 2.1 fusion.41
  80.8 3.4 reshape.167
  84.1 2.3 reshape.168
  87.1 4.3 %rows_wire.5 = f32[16,128,256]{2,1,0:T(8,128)} custom-call(s32[3]{0:T(128)} %slot_ref.5, bf16[384,4096]{1,0:T(8,128)(2,1)} %x_ref.5), custom_call_target="tpu_custom_call" | custom-call | flops 2000000000 | bytes 7200000 | tf_op jit(solution)/shard_map/rows_wire/pallas_call | solution.py:133
  91.4 17.7 %all-to-all-done.1.refs_1_.refs_3_.refs_0_ = f32[16,128,256]{2,1,0:T(8,128)} async-done(((f32[16,128,256]{2,1,0:T(8,128)}), f32[16,128,256]{2,1,0:T(8,128)}, u32[]{:S(2)}, u32[]{:S(2)}) %all-to-all-start.1) | async-done | bytes 2097184 | tf_op jit(solution)/shard_map/all_to_all | solution.py:580
  109.1 10.9 %all-to-all-start.2 = ((f32[16,128,256]{2,1,0:T(8,128)}), f32[16,128,256]{2,1,0:T(8,128)S(1)}, u32[]{:S(2)}, u32[]{:S(2)}) async-start(f32[16,128,256]{2,1,0:T(8,128)} %rows_wire.5), calls=%async_computation.2 | async-start | bytes 4194304 | tf_op jit(solution)/shard_map/all_to_all | solution.py:580
  123.5 10.0 %down_partial.2 = f32[16,2,192,128]{3,2,1,0:T(8,128)} custom-call(s32[16]{0:T(128)} %fusion.22.source_ref, s32[32]{0:T(128)} %reshape.164.tenant_ref, f32[16,136,256]{2,1,0:T(8,128)} %copy-done.4, f32[16,128,256]{2,1,0:T(8,128)} %all-to-all-done.1.refs_1_.refs_3_.refs_0_, f32[16,136,256]{2,1,0:T(8,128)} %copy-done.4, ...), custom_call_target="tpu_custom_call" | custom-call | flops 4000000000 | bytes 14400000 | tf_op jit(solution)/shard_map/down_partial/pallas_call | solution.py:172
  133.4 1.7 slice.112
  135.2 3.4 collective-permute-done
  140.8 25.0 %collective-permute-done.1 = f32[4,2,192,128]{3,2,1,0:T(8,128)S(1)} collective-permute-done((f32[4,2,192,128]{3,2,1,0:T(8,128)S(1)}, f32[4,2,192,128]{3,2,1,0:T(8,128)S(1)}, u32[]{:S(2)}, u32[]{:S(2)}) %collective-permute-start.1) | collective-permute-done | bytes 786464 | tf_op jit(solution)/shard_map/ppermute | solution.py:50
  166.0 8.0 %all-to-all-start.3 = ((f32[32,4,2560]{2,1,0:T(4,128)}), f32[32,4,2560]{2,1,0:T(4,128)}, u32[]{:S(2)}, u32[]{:S(2)}) async-start(f32[32,4,2560]{2,1,0:T(4,128)} %reshape.168), calls=%async_computation.3 | async-start | bytes 2621440 | tf_op jit(solution)/shard_map/all_to_all | solution.py:580
  173.9 5.8 %down_partial.3 = f32[16,1,192,128]{3,2,1,0:T(8,128)} custom-call(s32[16]{0:T(128)} %fusion.22.source_ref, s32[16]{0:T(128)} %get-tuple-element.49.tenant_ref, f32[16,128,256]{2,1,0:T(8,128)} %copy-done.3, f32[16,128,256]{2,1,0:T(8,128)} %copy-done.3, f32[16,128,256]{2,1,0:T(8,128)} %copy-done.3, f32[16,128,256]{2,1,0:T(8,128)} %copy-done.3, ...), custom_call_target="tpu_custom_call" | custom-call | flops 2000000000 | bytes 7200000 | tf_op jit(solution)/shard_map/down_partial/pallas_call | solution.py:172
  181.2 2.1 collective-permute-done.6
  185.0 3.1 collective-permute-start.4
  188.6 10.0 %collective-permute-done.7 = f32[4,1,192,128]{3,2,1,0:T(8,128)S(1)} collective-permute-done((f32[4,1,192,128]{3,2,1,0:T(8,128)S(1)}, f32[4,1,192,128]{3,2,1,0:T(8,128)S(1)}, u32[]{:S(2)}, u32[]{:S(2)}) %collective-permute-start.7) | collective-permute-done | bytes 393248 | tf_op jit(solution)/shard_map/ppermute | solution.py:50
  198.7 3.2 collective-permute-start.10
  203.6 16.8 %collective-permute-start.8 = (f32[1,192,128]{2,1,0:T(8,128)S(1)}, f32[1,192,128]{2,1,0:T(8,128)S(1)}, u32[]{:S(2)}, u32[]{:S(2)}) collective-permute-start(f32[1,192,128]{2,1,0:T(8,128)S(1)} %get-tuple-element.62), channel_id=1, source_target_pairs={{0,16},{2,18},{4,20},{6,22},{8,24},{10,26},{12,28},{14,30},{16,0},... | collective-permute-start | bytes 294920 | tf_op jit(solution)/shard_map/ppermute | solution.py:50
  220.4 4.9 %collective-permute-done.2 = f32[2,192,128]{2,1,0:T(8,128)S(1)} collective-permute-done((f32[2,192,128]{2,1,0:T(8,128)S(1)}, f32[2,192,128]{2,1,0:T(8,128)S(1)}, u32[]{:S(2)}, u32[]{:S(2)}) %collective-permute-start.2) | collective-permute-done | bytes 196640 | tf_op jit(solution)/shard_map/ppermute | solution.py:50
  226.7 3.9 %collective-permute-done.8 = f32[1,192,128]{2,1,0:T(8,128)S(1)} collective-permute-done((f32[1,192,128]{2,1,0:T(8,128)S(1)}, f32[1,192,128]{2,1,0:T(8,128)S(1)}, u32[]{:S(2)}, u32[]{:S(2)}) %collective-permute-start.8) | collective-permute-done | bytes 98336 | tf_op jit(solution)/shard_map/ppermute | solution.py:50
  230.7 4.6 %all-to-all-start.4 = ((f32[32,4,2560]{2,1,0:T(4,128)}), f32[32,4,2560]{2,1,0:T(4,128)S(1)}, u32[]{:S(2)}, u32[]{:S(2)}) async-start(f32[32,4,2560]{2,1,0:T(4,128)} %reshape.167), calls=%async_computation.4 | async-start | bytes 2621440 | tf_op jit(solution)/shard_map/all_to_all | solution.py:580
  239.5 2.2 collective-permute-done.11
  243.2 16.7 %attention_grads.4 = (f32[16,2,4,2560]{3,2,1,0:T(4,128)}, f32[3,192,128]{2,1,0:T(8,128)}) custom-call(bf16[384,4096]{1,0:T(8,128)(2,1)} %refs_0_.7, bf16[384,512]{1,0:T(8,128)(2,1)} %refs_1_.7, bf16[384,512]{1,0:T(8,128)(2,1)} %refs_2_.7, bf16[384,4096]{1,0:T(8,128)(2,1)} %refs_3_.7, f32[192,128]{1,0:T(8,128)} %get-tuple-element.66.refs_4_, ...), custom_call_target="tpu_custom_call" | custom-call | flops 20000000000 | bytes 72000000 | tf_op jit(solution)/shard_map/attention_grads/pallas_call | solution.py:329
  259.8 3.2 all-to-all-done.4
  264.1 7.7 %all-to-all-start.5 = ((f32[32,4,2560]{2,1,0:T(4,128)}), f32[32,4,2560]{2,1,0:T(4,128)S(1)}, u32[]{:S(2)}, u32[]{:S(2)}) async-start(f32[32,4,2560]{2,1,0:T(4,128)} %bitcast.68), calls=%async_computation.5 | async-start | bytes 2621440 | tf_op jit(solution)/shard_map/all_to_all | solution.py:580
  271.7 9.6 %attention_grads.5 = (f32[1,192,128]{2,1,0:T(8,128)}, f32[2,384,128]{2,1,0:T(8,128)}, f32[2,384,128]{2,1,0:T(8,128)}, f32[2,128,1280]{2,1,0:T(8,128)}) custom-call(bf16[384,4096]{1,0:T(8,128)(2,1)} %refs_0_.7, bf16[384,512]{1,0:T(8,128)(2,1)} %refs_1_.7, bf16[384,512]{1,0:T(8,128)(2,1)} %refs_2_.7, bf16[384,4096]{1,0:T(8,128)(2,1)} %refs_3_.7, ...), custom_call_target="tpu_custom_call" | custom-call | flops 10000000000 | bytes 36000000 | tf_op jit(solution)/shard_map/attention_grads/pallas_call | solution.py:329
  282.5 8.6 %attention_grads.6 = (f32[1,192,128]{2,1,0:T(8,128)}, f32[2,384,128]{2,1,0:T(8,128)}, f32[2,384,128]{2,1,0:T(8,128)}, f32[2,128,1280]{2,1,0:T(8,128)}) custom-call(bf16[384,4096]{1,0:T(8,128)(2,1)} %refs_0_.7, bf16[384,512]{1,0:T(8,128)(2,1)} %refs_1_.7, bf16[384,512]{1,0:T(8,128)(2,1)} %refs_2_.7, bf16[384,4096]{1,0:T(8,128)(2,1)} %refs_3_.7, ...), custom_call_target="tpu_custom_call" | custom-call | flops 6666666496 | bytes 24000000 | tf_op jit(solution)/shard_map/attention_grads/pallas_call | solution.py:329
  292.1 3.2 collective-permute-start.15
  297.2 2.0 collective-permute-start.22
  300.6 7.2 %attention_grads.7 = (f32[16,2,4,2560]{3,2,1,0:T(4,128)}, f32[1,192,128]{2,1,0:T(8,128)}) custom-call(bf16[384,4096]{1,0:T(8,128)(2,1)} %refs_0_.7, bf16[384,512]{1,0:T(8,128)(2,1)} %refs_1_.7, bf16[384,512]{1,0:T(8,128)(2,1)} %refs_2_.7, bf16[384,4096]{1,0:T(8,128)(2,1)} %refs_3_.7, f32[192,128]{1,0:T(8,128)} %get-tuple-element.66.refs_4_, ...), custom_call_target="tpu_custom_call" | custom-call | flops 3333333248 | bytes 11999999 | tf_op jit(solution)/shard_map/attention_grads/pallas_call | solution.py:329
  308.1 6.7 %collective-permute-done.13 = f32[1,192,128]{2,1,0:T(8,128)S(1)} collective-permute-done((f32[1,192,128]{2,1,0:T(8,128)S(1)}, f32[1,192,128]{2,1,0:T(8,128)S(1)}, u32[]{:S(2)}, u32[]{:S(2)}) %collective-permute-start.13) | collective-permute-done | bytes 98336 | tf_op jit(solution)/shard_map/ppermute | solution.py:50
  323.1 2.3 collective-permute-start.18
  325.7 2.0 collective-permute-start.20
  327.7 3.8 %collective-permute-done.25 = f32[4,192,128]{2,1,0:T(8,128)S(1)} collective-permute-done((f32[4,192,128]{2,1,0:T(8,128)S(1)}, f32[4,192,128]{2,1,0:T(8,128)S(1)}, u32[]{:S(2)}, u32[]{:S(2)}) %collective-permute-start.25) | collective-permute-done | bytes 393248 | tf_op jit(solution)/shard_map/ppermute | solution.py:50
  332.3 3.3 collective-permute-start.26
  339.1 4.4 %all-to-all-start.6 = ((f32[32,4,2560]{2,1,0:T(4,128)}), f32[32,4,2560]{2,1,0:T(4,128)S(1)}, u32[]{:S(2)}, u32[]{:S(2)}) async-start(f32[32,4,2560]{2,1,0:T(4,128)} %bitcast.64), calls=%async_computation.6 | async-start | bytes 2621440 | tf_op jit(solution)/shard_map/all_to_all | solution.py:580
  343.6 5.7 %collective-permute-done.21 = f32[4,192,128]{2,1,0:T(8,128)S(1)} collective-permute-done((f32[4,192,128]{2,1,0:T(8,128)S(1)}, f32[4,192,128]{2,1,0:T(8,128)S(1)}, u32[]{:S(2)}, u32[]{:S(2)}) %collective-permute-start.21) | collective-permute-done | bytes 393248 | tf_op jit(solution)/shard_map/ppermute | solution.py:50
  349.3 12.2 %down_grad.1.refs_3_ = f32[64,192,256]{2,1,0:T(8,128)} custom-call(s32[32]{0:T(128)} %select_reduce_fusion.1.order_ref, s32[65]{0:T(128)} %convert_reduce_fusion.2.first_ref, s32[32]{0:T(128)} %copy-done.18, s32[16]{0:T(128)} %fusion.22.source_ref, f32[16,128,256]{2,1,0:T(8,128)} %all-to-all-done.1.refs_1_.refs_3_.refs_0_, f32[16,128,256]{2,1,0:T(8,128)} %copy-done.3, ...), custom_call_target="tpu_custom_call" | custom-call | flops 14000000000 | bytes 50400000 | tf_op jit(solution)/shard_map/down_grad/pallas_call | solution.py:440
  361.6 3.0 collective-permute-start.29
  367.9 6.1 %down_grad_last.1 = f32[64,192,256]{2,1,0:T(8,128)} custom-call(s32[16]{0:T(128)} %copy-done.16, s32[16]{0:T(128)} %select_reduce_fusion.2.leader_ref, s32[16]{0:T(128)} %fusion.22.source_ref, f32[16,136,256]{2,1,0:T(8,128)} %copy-done.4, f32[8,192,128]{2,1,0:T(8,128)} %copy-done.11, f32[8,192,128]{2,1,0:T(8,128)} %copy-done.12, ...), custom_call_target="tpu_custom_call", output_to_operand_aliasing={{}: (6, {})} | custom-call | flops 6000000000 | bytes 21600000 | tf_op jit(solution)/shard_map/down_grad_last/pallas_call | solution.py:501
  375.1 6.8 %up_grad.1 = (f32[64,4,4096]{2,1,0:T(4,128)}, f32[64,4,4,256]{3,2,1,0:T(4,128)}) custom-call(s32[32]{0:T(128)} %select_reduce_fusion.order_ref, s32[65]{0:T(128)} %convert_reduce_fusion.first_ref, f32[32,4,2560]{2,1,0:T(4,128)} %copy-done.8, f32[32,4,2560]{2,1,0:T(4,128)} %copy-done.10), custom_call_target="tpu_custom_call" | custom-call | flops 6000000000 | bytes 21600000 | tf_op jit(solution)/shard_map/up_grad/pallas_call | solution.py:557
  (150 shorter events, 44.5 us)
Async XLA Ops:
  0.6 75.3 %copy-start = (f32[64,4,4,256]{3,2,1,0:T(4,128)S(1)}, f32[64,4,4,256]{3,2,1,0:T(4,128)}, u32[]{:S(2)}) copy-start(f32[64,4,4,256]{3,2,1,0:T(4,128)} %param.18) | copy-start | bytes 3145732
  5.1 51.1 %all-to-all-start = ((f32[16,136,256]{2,1,0:T(8,128)}), f32[16,136,256]{2,1,0:T(8,128)S(1)}, u32[]{:S(2)}, u32[]{:S(2)}) async-start(f32[16,136,256]{2,1,0:T(8,128)} %rows_wire.3), calls=%async_computation | async-start | bytes 4456448 | tf_op jit(solution)/shard_map/all_to_all | solution.py:580
  16.6 50.9 %copy-start.2 = (s32[16,2]{0,1:T(2,128)S(1)}, s32[16,2]{0,1:T(2,128)}, u32[]{:S(2)}) copy-start(s32[16,2]{0,1:T(2,128)} %param.21) | copy-start | bytes 388
  56.1 11.4 %copy-start.4 = (f32[16,136,256]{2,1,0:T(8,128)}, f32[16,136,256]{2,1,0:T(8,128)S(1)}, u32[]{:S(2)}) copy-start(f32[16,136,256]{2,1,0:T(8,128)S(1)} %all-to-all-done.refs_0_.refs_2_) | copy-start | bytes 6684676
  56.1 53.0 %all-to-all-start.1 = ((f32[16,128,256]{2,1,0:T(8,128)}), f32[16,128,256]{2,1,0:T(8,128)}, u32[]{:S(2)}, u32[]{:S(2)}) async-start(f32[16,128,256]{2,1,0:T(8,128)} %rows_wire.4), calls=%async_computation.1 | async-start | bytes 4194304 | tf_op jit(solution)/shard_map/all_to_all | solution.py:580
  109.1 56.8 %all-to-all-start.2 = ((f32[16,128,256]{2,1,0:T(8,128)}), f32[16,128,256]{2,1,0:T(8,128)S(1)}, u32[]{:S(2)}, u32[]{:S(2)}) async-start(f32[16,128,256]{2,1,0:T(8,128)} %rows_wire.5), calls=%async_computation.2 | async-start | bytes 4194304 | tf_op jit(solution)/shard_map/all_to_all | solution.py:580
  135.1 3.5 collective-permute-start
  138.8 27.0 %collective-permute-start.1 = (f32[4,2,192,128]{3,2,1,0:T(8,128)S(1)}, f32[4,2,192,128]{3,2,1,0:T(8,128)S(1)}, u32[]{:S(2)}, u32[]{:S(2)}) collective-permute-start(f32[4,2,192,128]{3,2,1,0:T(8,128)S(1)} %slice.114), channel_id=1, source_target_pairs={{0,4},{2,6},{4,0},{6,2},{8,12},{10,14},{12,8},{14,10},{16,20},{18,... | collective-permute-start | bytes 2359304 | tf_op jit(solution)/shard_map/ppermute | solution.py:50
  140.8 225.4 %copy-start.16 = (s32[16]{0:T(128)}, s32[16]{0:T(128)S(1)}, u32[]{:S(2)}) copy-start(s32[16]{0:T(128)S(1)} %get-tuple-element.50.owner_ref) | copy-start | bytes 196
  166.0 64.7 %all-to-all-start.3 = ((f32[32,4,2560]{2,1,0:T(4,128)}), f32[32,4,2560]{2,1,0:T(4,128)}, u32[]{:S(2)}, u32[]{:S(2)}) async-start(f32[32,4,2560]{2,1,0:T(4,128)} %reshape.168), calls=%async_computation.3 | async-start | bytes 2621440 | tf_op jit(solution)/shard_map/all_to_all | solution.py:580
  181.0 2.4 collective-permute-start.6
  183.5 15.1 %collective-permute-start.7 = (f32[4,1,192,128]{3,2,1,0:T(8,128)S(1)}, f32[4,1,192,128]{3,2,1,0:T(8,128)S(1)}, u32[]{:S(2)}, u32[]{:S(2)}) collective-permute-start(f32[4,1,192,128]{3,2,1,0:T(8,128)S(1)} %slice.126), channel_id=1, source_target_pairs={{0,4},{2,6},{4,0},{6,2},{8,12},{10,14},{12,8},{14,10},{16,20},{18,... | collective-permute-start | bytes 1179656 | tf_op jit(solution)/shard_map/ppermute | solution.py:50
  185.0 18.7 %collective-permute-start.4 = (f32[2,192,128]{2,1,0:T(8,128)S(1)}, f32[2,192,128]{2,1,0:T(8,128)S(1)}, u32[]{:S(2)}, u32[]{:S(2)}) collective-permute-start(f32[2,192,128]{2,1,0:T(8,128)S(1)} %get-tuple-element.60), channel_id=1, source_target_pairs={{0,24},{2,26},{4,28},{6,30},{8,16},{10,18},{12,20},{14,22},{16,8},... | collective-permute-start | bytes 589832 | tf_op jit(solution)/shard_map/ppermute | solution.py:50
  188.0 32.4 %collective-permute-start.3 = (f32[2,192,128]{2,1,0:T(8,128)S(1)}, f32[2,192,128]{2,1,0:T(8,128)S(1)}, u32[]{:S(2)}, u32[]{:S(2)}) collective-permute-start(f32[2,192,128]{2,1,0:T(8,128)S(1)} %get-tuple-element.61), channel_id=1, source_target_pairs={{0,8},{2,10},{4,12},{6,14},{8,0},{10,2},{12,4},{14,6},{16,24},{18,... | collective-permute-start | bytes 589832 | tf_op jit(solution)/shard_map/ppermute | solution.py:50
  188.0 37.3 %collective-permute-start.2 = (f32[2,192,128]{2,1,0:T(8,128)S(1)}, f32[2,192,128]{2,1,0:T(8,128)S(1)}, u32[]{:S(2)}, u32[]{:S(2)}) collective-permute-start(f32[2,192,128]{2,1,0:T(8,128)S(1)} %get-tuple-element.59), channel_id=1, source_target_pairs={{0,16},{2,18},{4,20},{6,22},{8,24},{10,26},{12,28},{14,30},{16,0},... | collective-permute-start | bytes 589832 | tf_op jit(solution)/shard_map/ppermute | solution.py:50
  198.7 36.5 %copy-start.17 = (s32[3]{0:T(128)S(1)}, s32[3]{0:T(128)}, u32[]{:S(2)}) copy-start(s32[3]{0:T(128)} %slot_ref.5) | copy-start | bytes 40
  198.7 36.6 %copy-start.15 = (s32[384]{0:T(512)S(1)}, s32[384]{0:T(512)}, u32[]{:S(2)}) copy-start(s32[384]{0:T(512)} %param.19) | copy-start | bytes 4612
  198.7 28.0 %collective-permute-start.10 = (f32[1,192,128]{2,1,0:T(8,128)S(1)}, f32[1,192,128]{2,1,0:T(8,128)S(1)}, u32[]{:S(2)}, u32[]{:S(2)}) collective-permute-start(f32[1,192,128]{2,1,0:T(8,128)S(1)} %get-tuple-element.63), channel_id=1, source_target_pairs={{0,24},{2,26},{4,28},{6,30},{8,16},{10,18},{12,20},{14,22},{16,8},... | collective-permute-start | bytes 294920 | tf_op jit(solution)/shard_map/ppermute | solution.py:50
  201.9 24.8 %collective-permute-start.9 = (f32[1,192,128]{2,1,0:T(8,128)S(1)}, f32[1,192,128]{2,1,0:T(8,128)S(1)}, u32[]{:S(2)}, u32[]{:S(2)}) collective-permute-start(f32[1,192,128]{2,1,0:T(8,128)S(1)} %get-tuple-element.64), channel_id=1, source_target_pairs={{0,8},{2,10},{4,12},{6,14},{8,0},{10,2},{12,4},{14,6},{16,24},{18,... | collective-permute-start | bytes 294920 | tf_op jit(solution)/shard_map/ppermute | solution.py:50
  203.6 27.0 %collective-permute-start.8 = (f32[1,192,128]{2,1,0:T(8,128)S(1)}, f32[1,192,128]{2,1,0:T(8,128)S(1)}, u32[]{:S(2)}, u32[]{:S(2)}) collective-permute-start(f32[1,192,128]{2,1,0:T(8,128)S(1)} %get-tuple-element.62), channel_id=1, source_target_pairs={{0,16},{2,18},{4,20},{6,22},{8,24},{10,26},{12,28},{14,30},{16,0},... | collective-permute-start | bytes 294920 | tf_op jit(solution)/shard_map/ppermute | solution.py:50
  225.4 12.1 %collective-permute-start.5 = (f32[2,192,128]{2,1,0:T(8,128)S(1)}, f32[2,192,128]{2,1,0:T(8,128)S(1)}, u32[]{:S(2)}, u32[]{:S(2)}) collective-permute-start(f32[2,192,128]{2,1,0:T(8,128)S(1)} %fusion.2), channel_id=1, source_target_pairs={{0,1},{1,0},{2,3},{3,2},{4,5},{5,4},{6,7},{7,6},{8,9},{9,8},{10,11... | collective-permute-start | bytes 589832 | tf_op jit(solution)/shard_map/ppermute | solution.py:50
  230.7 32.3 %all-to-all-start.4 = ((f32[32,4,2560]{2,1,0:T(4,128)}), f32[32,4,2560]{2,1,0:T(4,128)S(1)}, u32[]{:S(2)}, u32[]{:S(2)}) async-start(f32[32,4,2560]{2,1,0:T(4,128)} %reshape.167), calls=%async_computation.4 | async-start | bytes 2621440 | tf_op jit(solution)/shard_map/all_to_all | solution.py:580
  237.3 99.2 %copy-start.18 = (s32[32]{0:T(128)}, s32[32]{0:T(128)S(1)}, u32[]{:S(2)}) copy-start(s32[32]{0:T(128)S(1)} %lt.135.owner_ref) | copy-start | bytes 388
  237.5 4.2 %collective-permute-start.11 = (f32[1,192,128]{2,1,0:T(8,128)S(1)}, f32[1,192,128]{2,1,0:T(8,128)S(1)}, u32[]{:S(2)}, u32[]{:S(2)}) collective-permute-start(f32[1,192,128]{2,1,0:T(8,128)S(1)} %fusion.5), channel_id=1, source_target_pairs={{0,1},{1,0},{2,3},{3,2},{4,5},{5,4},{6,7},{7,6},{8,9},{9,8},{10,11... | collective-permute-start | bytes 294920 | tf_op jit(solution)/shard_map/ppermute | solution.py:50
  264.1 52.1 %all-to-all-start.5 = ((f32[32,4,2560]{2,1,0:T(4,128)}), f32[32,4,2560]{2,1,0:T(4,128)S(1)}, u32[]{:S(2)}, u32[]{:S(2)}) async-start(f32[32,4,2560]{2,1,0:T(4,128)} %bitcast.68), calls=%async_computation.5 | async-start | bytes 2621440 | tf_op jit(solution)/shard_map/all_to_all | solution.py:580
  281.3 10.2 %collective-permute-start.12 = (f32[1,192,128]{2,1,0:T(8,128)}, f32[1,192,128]{2,1,0:T(8,128)S(1)}, u32[]{:S(2)}, u32[]{:S(2)}) collective-permute-start(f32[1,192,128]{2,1,0:T(8,128)} %get-tuple-element.37), channel_id=1, source_target_pairs={{0,1},{1,0},{2,3},{3,2},{4,5},{5,4},{6,7},{7,6},{8,9},{9,8},{10,11... | collective-permute-start | bytes 294920 | tf_op jit(solution)/shard_map/ppermute | solution.py:50
  282.5 8.9 %copy-start.14 = (f32[1,192,128]{2,1,0:T(8,128)S(1)}, f32[1,192,128]{2,1,0:T(8,128)}, u32[]{:S(2)}) copy-start(f32[1,192,128]{2,1,0:T(8,128)} %get-tuple-element.37) | copy-start | bytes 294916
  291.1 4.5 %collective-permute-start.16 = (f32[1,192,128]{2,1,0:T(8,128)}, f32[1,192,128]{2,1,0:T(8,128)S(1)}, u32[]{:S(2)}, u32[]{:S(2)}) collective-permute-start(f32[1,192,128]{2,1,0:T(8,128)} %get-tuple-element.43), channel_id=1, source_target_pairs={{0,1},{1,0},{2,3},{3,2},{4,5},{5,4},{6,7},{7,6},{8,9},{9,8},{10,11... | collective-permute-start | bytes 294920 | tf_op jit(solution)/shard_map/ppermute | solution.py:50
  292.1 15.8 %collective-permute-start.15 = (f32[1,192,128]{2,1,0:T(8,128)S(1)}, f32[1,192,128]{2,1,0:T(8,128)S(1)}, u32[]{:S(2)}, u32[]{:S(2)}) collective-permute-start(f32[1,192,128]{2,1,0:T(8,128)S(1)} %get-tuple-element.52), channel_id=1, source_target_pairs={{0,24},{2,26},{4,28},{6,30},{8,16},{10,18},{12,20},{14,22},{16,8},... | collective-permute-start | bytes 294920 | tf_op jit(solution)/shard_map/ppermute | solution.py:50
  295.3 12.8 %collective-permute-start.14 = (f32[1,192,128]{2,1,0:T(8,128)S(1)}, f32[1,192,128]{2,1,0:T(8,128)S(1)}, u32[]{:S(2)}, u32[]{:S(2)}) collective-permute-start(f32[1,192,128]{2,1,0:T(8,128)S(1)} %get-tuple-element.52), channel_id=1, source_target_pairs={{0,8},{2,10},{4,12},{6,14},{8,0},{10,2},{12,4},{14,6},{16,24},{18,... | collective-permute-start | bytes 294920 | tf_op jit(solution)/shard_map/ppermute | solution.py:50
  295.3 19.5 %collective-permute-start.13 = (f32[1,192,128]{2,1,0:T(8,128)S(1)}, f32[1,192,128]{2,1,0:T(8,128)S(1)}, u32[]{:S(2)}, u32[]{:S(2)}) collective-permute-start(f32[1,192,128]{2,1,0:T(8,128)S(1)} %get-tuple-element.52), channel_id=1, source_target_pairs={{0,16},{2,18},{4,20},{6,22},{8,24},{10,26},{12,28},{14,30},{16,0},... | collective-permute-start | bytes 294920 | tf_op jit(solution)/shard_map/ppermute | solution.py:50
  297.2 20.7 %collective-permute-start.22 = (f32[1,192,128]{2,1,0:T(8,128)S(1)}, f32[1,192,128]{2,1,0:T(8,128)S(1)}, u32[]{:S(2)}, u32[]{:S(2)}) collective-permute-start(f32[1,192,128]{2,1,0:T(8,128)S(1)} %get-tuple-element.54), channel_id=1, source_target_pairs={{0,16},{2,18},{4,20},{6,22},{8,24},{10,26},{12,28},{14,30},{16,0},... | collective-permute-start | bytes 294920 | tf_op jit(solution)/shard_map/ppermute | solution.py:50
  299.2 18.8 %collective-permute-start.23 = (f32[1,192,128]{2,1,0:T(8,128)S(1)}, f32[1,192,128]{2,1,0:T(8,128)S(1)}, u32[]{:S(2)}, u32[]{:S(2)}) collective-permute-start(f32[1,192,128]{2,1,0:T(8,128)S(1)} %get-tuple-element.54), channel_id=1, source_target_pairs={{0,8},{2,10},{4,12},{6,14},{8,0},{10,2},{12,4},{14,6},{16,24},{18,... | collective-permute-start | bytes 294920 | tf_op jit(solution)/shard_map/ppermute | solution.py:50
  307.9 15.3 %copy-start.13 = (f32[1,192,128]{2,1,0:T(8,128)S(1)}, f32[1,192,128]{2,1,0:T(8,128)}, u32[]{:S(2)}) copy-start(f32[1,192,128]{2,1,0:T(8,128)} %get-tuple-element.44) | copy-start | bytes 294916
  307.9 10.1 %collective-permute-start.24 = (f32[1,192,128]{2,1,0:T(8,128)S(1)}, f32[1,192,128]{2,1,0:T(8,128)S(1)}, u32[]{:S(2)}, u32[]{:S(2)}) collective-permute-start(f32[1,192,128]{2,1,0:T(8,128)S(1)} %get-tuple-element.54), channel_id=1, source_target_pairs={{0,24},{2,26},{4,28},{6,30},{8,16},{10,18},{12,20},{14,22},{16,8},... | collective-permute-start | bytes 294920 | tf_op jit(solution)/shard_map/ppermute | solution.py:50
  314.8 20.8 %collective-permute-start.27 = (f32[4,192,128]{2,1,0:T(8,128)S(1)}, f32[4,192,128]{2,1,0:T(8,128)S(1)}, u32[]{:S(2)}, u32[]{:S(2)}) collective-permute-start(f32[4,192,128]{2,1,0:T(8,128)S(1)} %pad_maximum_fusion), channel_id=1, source_target_pairs={{0,4},{2,6},{4,0},{6,2},{8,12},{10,14},{12,8},{14,10},{16,20},{18,... | collective-permute-start | bytes 1179656 | tf_op jit(solution)/shard_map/ppermute | solution.py:50
  316.1 21.0 %copy-start.8 = (f32[32,4,2560]{2,1,0:T(4,128)}, f32[32,4,2560]{2,1,0:T(4,128)S(1)}, u32[]{:S(2)}) copy-start(f32[32,4,2560]{2,1,0:T(4,128)S(1)} %all-to-all-done.5.refs_0_) | copy-start | bytes 3932164
  316.1 7.0 %collective-permute-start.17 = (f32[1,192,128]{2,1,0:T(8,128)}, f32[1,192,128]{2,1,0:T(8,128)S(1)}, u32[]{:S(2)}, u32[]{:S(2)}) collective-permute-start(f32[1,192,128]{2,1,0:T(8,128)} %get-tuple-element.44), channel_id=1, source_target_pairs={{0,1},{1,0},{2,3},{3,2},{4,5},{5,4},{6,7},{7,6},{8,9},{9,8},{10,11... | collective-permute-start | bytes 294920 | tf_op jit(solution)/shard_map/ppermute | solution.py:50
  318.0 13.5 %collective-permute-start.25 = (f32[4,192,128]{2,1,0:T(8,128)S(1)}, f32[4,192,128]{2,1,0:T(8,128)S(1)}, u32[]{:S(2)}, u32[]{:S(2)}) collective-permute-start(f32[4,192,128]{2,1,0:T(8,128)S(1)} %pad_maximum_fusion.2), channel_id=1, source_target_pairs={{0,4},{2,6},{4,0},{6,2},{8,12},{10,14},{12,8},{14,10},{16,20},{18,... | collective-permute-start | bytes 1179656 | tf_op jit(solution)/shard_map/ppermute | solution.py:50
  323.1 13.9 %collective-permute-start.18 = (f32[1,192,128]{2,1,0:T(8,128)S(1)}, f32[1,192,128]{2,1,0:T(8,128)S(1)}, u32[]{:S(2)}, u32[]{:S(2)}) collective-permute-start(f32[1,192,128]{2,1,0:T(8,128)S(1)} %get-tuple-element.56), channel_id=1, source_target_pairs={{0,16},{2,18},{4,20},{6,22},{8,24},{10,26},{12,28},{14,30},{16,0},... | collective-permute-start | bytes 294920 | tf_op jit(solution)/shard_map/ppermute | solution.py:50
  325.5 11.6 %collective-permute-start.19 = (f32[1,192,128]{2,1,0:T(8,128)S(1)}, f32[1,192,128]{2,1,0:T(8,128)S(1)}, u32[]{:S(2)}, u32[]{:S(2)}) collective-permute-start(f32[1,192,128]{2,1,0:T(8,128)S(1)} %get-tuple-element.56), channel_id=1, source_target_pairs={{0,8},{2,10},{4,12},{6,14},{8,0},{10,2},{12,4},{14,6},{16,24},{18,... | collective-permute-start | bytes 294920 | tf_op jit(solution)/shard_map/ppermute | solution.py:50
  325.7 11.4 %collective-permute-start.20 = (f32[1,192,128]{2,1,0:T(8,128)S(1)}, f32[1,192,128]{2,1,0:T(8,128)S(1)}, u32[]{:S(2)}, u32[]{:S(2)}) collective-permute-start(f32[1,192,128]{2,1,0:T(8,128)S(1)} %get-tuple-element.56), channel_id=1, source_target_pairs={{0,24},{2,26},{4,28},{6,30},{8,16},{10,18},{12,20},{14,22},{16,8},... | collective-permute-start | bytes 294920 | tf_op jit(solution)/shard_map/ppermute | solution.py:50
  332.3 17.0 %collective-permute-start.26 = (f32[8,192,128]{2,1,0:T(8,128)}, f32[8,192,128]{2,1,0:T(8,128)}, u32[]{:S(2)}, u32[]{:S(2)}) collective-permute-start(f32[8,192,128]{2,1,0:T(8,128)} %constant_dynamic-update-slice_fusion.7.refs_2_), channel_id=1, source_target_pairs={{0,2},{2,0},{4,6},{6,4},{8,10},{10,8},{12,14},{14,12},{16,18},{18,... | collective-permute-start | bytes 2359304 | tf_op jit(solution)/shard_map/ppermute | solution.py:50
  336.5 12.9 %collective-permute-start.28 = (f32[8,192,128]{2,1,0:T(8,128)}, f32[8,192,128]{2,1,0:T(8,128)}, u32[]{:S(2)}, u32[]{:S(2)}) collective-permute-start(f32[8,192,128]{2,1,0:T(8,128)} %constant_dynamic-update-slice_fusion.12.refs_4_), channel_id=1, source_target_pairs={{0,2},{2,0},{4,6},{6,4},{8,10},{10,8},{12,14},{14,12},{16,18},{18,... | collective-permute-start | bytes 2359304 | tf_op jit(solution)/shard_map/ppermute | solution.py:50
  337.1 12.1 %collective-permute-start.21 = (f32[4,192,128]{2,1,0:T(8,128)S(1)}, f32[4,192,128]{2,1,0:T(8,128)S(1)}, u32[]{:S(2)}, u32[]{:S(2)}) collective-permute-start(f32[4,192,128]{2,1,0:T(8,128)S(1)} %pad_maximum_fusion.1), channel_id=1, source_target_pairs={{0,4},{2,6},{4,0},{6,2},{8,12},{10,14},{12,8},{14,10},{16,20},{18,... | collective-permute-start | bytes 1179656 | tf_op jit(solution)/shard_map/ppermute | solution.py:50
  339.1 34.9 %all-to-all-start.6 = ((f32[32,4,2560]{2,1,0:T(4,128)}), f32[32,4,2560]{2,1,0:T(4,128)S(1)}, u32[]{:S(2)}, u32[]{:S(2)}) async-start(f32[32,4,2560]{2,1,0:T(4,128)} %bitcast.64), calls=%async_computation.6 | async-start | bytes 2621440 | tf_op jit(solution)/shard_map/all_to_all | solution.py:580
  349.3 12.2 %copy-start.11 = (f32[8,192,128]{2,1,0:T(8,128)}, f32[8,192,128]{2,1,0:T(8,128)S(1)}, u32[]{:S(2)}) copy-start(f32[8,192,128]{2,1,0:T(8,128)S(1)} %constant_dynamic-update-slice_fusion.2.refs_1_) | copy-start | bytes 2359300
  361.6 5.4 %collective-permute-start.29 = (f32[8,192,128]{2,1,0:T(8,128)S(1)}, f32[8,192,128]{2,1,0:T(8,128)S(1)}, u32[]{:S(2)}, u32[]{:S(2)}) collective-permute-start(f32[8,192,128]{2,1,0:T(8,128)S(1)} %constant_dynamic-update-slice_fusion.2.refs_1_), channel_id=1, source_target_pairs={{0,2},{2,0},{4,6},{6,4},{8,10},{10,8},{12,14},{14,12},{16,18},{18,... | collective-permute-start | bytes 2359304 | tf_op jit(solution)/shard_map/ppermute | solution.py:50
  (8 other events, 27.6 us)

commit v5 on v4

--- a/solution.py
+++ b/solution.py
@@ -125,17 +125,16 @@
         out_ref[:, rows:] = jnp.broadcast_to(tile[None], (n, 8, width))
 
 
-def rows_wire(x, block_slots, n, b):
-    blocks = block_slots.shape[0]
-    rows, width = x.shape[0] // blocks, x.shape[1] // n
+def rows_wire(x, block_slots, n, start, rows):
+    width = x.shape[1] // n
     per = min(n, max(128 // width, 1) * 4)
-    tall = rows + (8 if b == 0 else 0)
+    tall = rows + (8 if start == 0 else 0)
     return pl.pallas_call(
         functools.partial(wire_kernel, per),
         grid_spec=pltpu.PrefetchScalarGridSpec(
             num_scalar_prefetch=1,
             grid=(n // per,),
-            in_specs=[pl.BlockSpec((rows, per * width), lambda i, s: (b, i))],
+            in_specs=[pl.BlockSpec((rows, per * width), lambda i, s: (start // rows, i))],
             out_specs=pl.BlockSpec((per, tall, width), lambda i, s: (i, 0, 0)),
         ),
         out_shape=jax.ShapeDtypeStruct((n, tall, width), F32),
@@ -155,14 +154,14 @@
 
 
 def down_partial(xs, weights, source, tenant, rows):
-    n, _, width = xs[0].shape
+    n, _, width = xs[0][0].shape
     rank = weights.shape[1]
     calls = len(xs)
     count = 4 // calls
     every = [(c, b) for c in range(count) for b in range(calls)]
 
     def x_spec(c, b):
-        return pl.BlockSpec((1, rows, width), lambda p, s, t: (s[p * count + c], 0, 0))
+        return pl.BlockSpec((1, rows, width), lambda p, s, t: (s[p * count + c], xs[b][1] // rows, 0))
 
     def w_spec(c, b):
         return pl.BlockSpec(
@@ -181,7 +180,7 @@
         cost_estimate=cost(DOWN_MICROS * calls),
         compiler_params=pltpu.CompilerParams(vmem_limit_bytes=VMEM_LIMIT),
         name="down_partial",
-    )(source, tenant.reshape(-1), *[xs[b] for _, b in every], *[weights] * len(every))
+    )(source, tenant.reshape(-1), *[xs[b][0] for _, b in every], *[weights] * len(every))
 
 
 def attention_kernel(groups, slots, blocks, todo, *refs):
@@ -381,7 +380,8 @@
     )
 
 
-def down_grad_kernel(blocks, per_step, order_ref, first_ref, owner_ref, source_ref, *refs):
+def down_grad_kernel(starts, per_step, order_ref, first_ref, owner_ref, source_ref, *refs):
+    blocks = len(starts)
     x_refs, g_refs = refs[:blocks], refs[blocks : 3 * blocks]
     out_ref, x_all, g_ref, sems = refs[3 * blocks :]
     half = g_refs[0].shape[0]
@@ -391,7 +391,7 @@
     def _():
         copies = [
             pltpu.make_async_copy(
-                x_refs[b].at[:, pl.ds(0, x_all.shape[2])], x_all.at[b], sems.at[b]
+                x_refs[b].at[:, pl.ds(starts[b], x_all.shape[2])], x_all.at[b], sems.at[b]
             )
             for b in range(blocks)
         ] + [
@@ -433,12 +433,13 @@
 
 def down_grad(xs, g, owners, source, tenants):
     blocks = len(xs)
-    n, rows, width = xs[1].shape
+    n, _, width = xs[0][0].shape
+    rows = g[0].shape[2]
     rank = g[0].shape[1]
     order, first = by_tenant(owners, tenants)
     per_step = 8
     return pl.pallas_call(
-        functools.partial(down_grad_kernel, blocks, per_step),
+        functools.partial(down_grad_kernel, [start for _, start in xs], per_step),
         grid_spec=pltpu.PrefetchScalarGridSpec(
             num_scalar_prefetch=4,
             grid=(tenants // per_step,),
@@ -454,7 +455,7 @@
         compiler_params=pltpu.CompilerParams(vmem_limit_bytes=VMEM_LIMIT),
         cost_estimate=cost(14),
         name="down_grad",
-    )(order, first, owners, source, *xs, *g)
+    )(order, first, owners, source, *[x for x, _ in xs], *g)
 
 
 def down_grad_last_kernel(owner_ref, leader_ref, source_ref, *refs):
@@ -606,8 +607,10 @@
     wide = adapter_up_query.shape[2] // kv_heads
     me = lax.axis_index("dp").astype(jnp.int32)
 
+    early_rows = (blocks - 1) * block
     wires = [
-        rows_wire(normed_input_rows, block_tenant_slot, dp_count, b) for b in range(blocks)
+        rows_wire(normed_input_rows, block_tenant_slot, dp_count, start, size)
+        for start, size in ((0, early_rows), (early_rows, block))
     ]
     wanted = shard_tenant_table.reshape(-1)
     up_query = adapter_up_query[wanted].reshape(-1, piece, kv_heads, wide)
@@ -621,14 +624,14 @@
         for c in range(calls)
     ]
 
-    xs = [exchange(wires[0])]
-    for b in range(1, blocks):
-        xs.append(exchange(after(wires[b], xs[-1], *(owns if b == blocks - 1 else ()))))
+    moved = exchange(wires[0])
+    x_last = exchange(after(wires[1], moved, *owns))
+    xs = [(moved, b * block) for b in range(blocks - 1)] + [(x_last, 0)]
 
     source = me ^ bit_reverse(
         jnp.arange(dp_count, dtype=jnp.int32), dp_count.bit_length() - 1
     )
-    slots_all = xs[0][:, block, :blocks].astype(jnp.int32)[source]
+    slots_all = moved[:, early_rows, :blocks].astype(jnp.int32)[source]
     owners = shard_tenant_table[source[:, None], slots_all]
 
     weights = jnp.swapaxes(adapter_down_weight, 1, 2)
@@ -642,7 +645,7 @@
 
     panels = []
     for c in range(calls):
-        own = after(owns[c], xs[-1], near) if c == 0 else after(owns[c], panels[-1], late_part)
+        own = after(owns[c], x_last, near) if c == 0 else after(owns[c], panels[-1], late_part)
         panels.append(exchange(own).reshape(dp_count, slots, piece, heads * per))
 
     attend = functools.partial(
@@ -688,7 +691,7 @@
     grad_down = down_grad(xs[1:], early, owners[:, 1:].reshape(-1), source, tenants)
     fars[0] = after(fars[0], grad_down)
     g_halves[0] = (fars[0], swap(fars[0], "dp", dp_count, 1))
-    grad_down = down_grad_last(xs[0], g_halves[0], grad_down, owners[:, 0], source)
+    grad_down = down_grad_last(moved, g_halves[0], grad_down, owners[:, 0], source)
     order, first = by_tenant(wanted, tenants)
     grad_upq, grad_upkv = up_grad(dus, order, first, tenants, kv_heads, head)
     return (

time: 383 us -> 377 us (0.984)
    pallas_call x3 -> x2, Pallas kernels: 12.9 us -> 9.28 us  [rows_wire(): pl.pallas_call(functools.partial(wire_kernel, per), grid_spec=pltpu.Prefe...]
    all_to_all x7 -> x6, starting transfers between devices: 54.2 us -> 51.8 us  [exchange(): return lax.all_to_all(a, 'dp', split_axis=0, concat_axis=0, tiled=True)]
    all_to_all x7 -> x6, waiting for transfers between devices: 60.4 us -> 59.7 us  [exchange(): return lax.all_to_all(a, 'dp', split_axis=0, concat_axis=0, tiled=True)]
    unnamed x51 -> x49, local copies, waits for them, and re-layouts: 8.75 us -> 8.8 us
  transfers between devices with their start and end apart: 37 -> 36, of which waited for: 15 -> 14; matrix products, arithmetic and copies ran while one was open for 11% -> 11% of each run, Pallas kernels for 22% -> 22%
where the time goes in v5:
time: 377 us; the launch traced here: 376 us
  waiting for transfers between devices  127 us (34%)
  starting transfers between devices  109 us (29%)
  Pallas kernels  92.7 us (25%)
  local copies, waits for them, and re-layouts  37.7 us (10%)
  other arithmetic  8.76 us (2%)
    ppermute x30, waiting for transfers between devices, swap(): return lax.ppermute(a, axis, [(i, i ^ bit) for i in range(size)])  67.6 us
    all_to_all x6, waiting for transfers between devices, exchange(): return lax.all_to_all(a, 'dp', split_axis=0, concat_axis=0, tiled=True)  59.7 us
    ppermute x30, starting transfers between devices, swap(): return lax.ppermute(a, axis, [(i, i ^ bit) for i in range(size)])  56.7 us
    all_to_all x6, starting transfers between devices, exchange(): return lax.all_to_all(a, 'dp', split_axis=0, concat_axis=0, tiled=True)  51.8 us
    pallas_call x4, Pallas kernels, attention(): pl.pallas_call(functools.partial(attention_kernel, groups, slots, blocks,...  42 us
    pallas_call x2, Pallas kernels, down_partial(): pl.pallas_call(functools.partial(down_kernel, count, calls), grid_spec=pl...  15.4 us
    pallas_call x1, Pallas kernels, down_grad(): pl.pallas_call(functools.partial(down_grad_kernel, [start for _, start in...  12.9 us
    pallas_call x2, Pallas kernels, rows_wire(): pl.pallas_call(functools.partial(wire_kernel, per), grid_spec=pltpu.Prefe...  9.28 us
  transfers between devices with their start and end apart: 36, of which 14 were waited for; matrix products, arithmetic and copies ran while one was open for 11% of the time, Pallas kernels for 22%

profile of v5, /device:TPU:1, one launch (start us, length us, event | category | flops | bytes accessed | tf_op | source)
XLA Modules:
  0.0 376.0 jit_solution(18198725260570553823)
XLA Ops:
  0.6 5.0 %rows_wire.2 = f32[16,264,256]{2,1,0:T(8,128)} custom-call(s32[3]{0:T(128)} %slot_ref.3, bf16[384,4096]{1,0:T(8,128)(2,1)} %x_ref.3), custom_call_target="tpu_custom_call" | custom-call | flops 2000000000 | bytes 7200000 | tf_op jit(solution)/shard_map/rows_wire/pallas_call | solution.py:132
  5.7 7.5 %all-to-all-start = ((f32[16,264,256]{2,1,0:T(8,128)}), f32[16,264,256]{2,1,0:T(8,128)}, u32[]{:S(2)}, u32[]{:S(2)}) async-start(f32[16,264,256]{2,1,0:T(8,128)} %rows_wire.2), calls=%async_computation | async-start | bytes 8650752 | tf_op jit(solution)/shard_map/all_to_all | solution.py:581
  13.3 5.2 %gather_fusion.2 = f32[32,4,4096]{2,1,0:T(4,128)} fusion(f32[64,4,4096]{2,1,0:T(4,128)} %param.17, s32[1024]{0:T(1024)S(1)} %pad_clamp_fusion), kind=kCustom, calls=%fused_computation.2 | custom fusion | bytes 4194432 | tf_op jit(solution)/shard_map/gather | solution.py:616
  18.5 3.0 reshape.166
  21.6 1.6 gather_fusion.3
  24.3 2.1 fusion.41
  26.4 3.4 reshape.167
  29.7 2.3 reshape.168
  32.6 4.3 %rows_wire.3 = f32[16,128,256]{2,1,0:T(8,128)} custom-call(s32[3]{0:T(128)} %slot_ref.3, bf16[384,4096]{1,0:T(8,128)(2,1)} %x_ref.3), custom_call_target="tpu_custom_call" | custom-call | flops 2000000000 | bytes 7200000 | tf_op jit(solution)/shard_map/rows_wire/pallas_call | solution.py:132
  36.9 56.6 %all-to-all-done.refs_0_.refs_1_.refs_2_.refs_3_ = f32[16,264,256]{2,1,0:T(8,128)} async-done(((f32[16,264,256]{2,1,0:T(8,128)}), f32[16,264,256]{2,1,0:T(8,128)}, u32[]{:S(2)}, u32[]{:S(2)}) %all-to-all-start) | async-done | bytes 4325408 | tf_op jit(solution)/shard_map/all_to_all | solution.py:581
  93.5 19.8 %all-to-all-start.1 = ((f32[16,128,256]{2,1,0:T(8,128)}), f32[16,128,256]{2,1,0:T(8,128)S(1)}, u32[]{:S(2)}, u32[]{:S(2)}) async-start(f32[16,128,256]{2,1,0:T(8,128)} %rows_wire.3), calls=%async_computation.1 | async-start | bytes 4194304 | tf_op jit(solution)/shard_map/all_to_all | solution.py:581
  116.8 9.7 %down_partial.2 = f32[16,2,192,128]{3,2,1,0:T(8,128)} custom-call(s32[16]{0:T(128)} %fusion.22.source_ref, s32[32]{0:T(128)} %reshape.164.tenant_ref, f32[16,264,256]{2,1,0:T(8,128)} %all-to-all-done.refs_0_.refs_1_.refs_2_.refs_3_, f32[16,264,256]{2,1,0:T(8,128)} %all-to-all-done.refs_0_.refs_1_.refs_2_.refs_3_, ...), custom_call_target="tpu_custom_call" | custom-call | flops 4000000000 | bytes 14400000 | tf_op jit(solution)/shard_map/down_partial/pallas_call | solution.py:171
  126.5 1.7 slice.112
  128.3 3.3 collective-permute-done
  131.9 1.6 collective-permute-start.1
  134.2 25.0 %collective-permute-done.1 = f32[4,2,192,128]{3,2,1,0:T(8,128)S(1)} collective-permute-done((f32[4,2,192,128]{3,2,1,0:T(8,128)S(1)}, f32[4,2,192,128]{3,2,1,0:T(8,128)S(1)}, u32[]{:S(2)}, u32[]{:S(2)}) %collective-permute-start.1) | collective-permute-done | bytes 786464 | tf_op jit(solution)/shard_map/ppermute | solution.py:50
  159.3 7.9 %all-to-all-start.2 = ((f32[32,4,2560]{2,1,0:T(4,128)}), f32[32,4,2560]{2,1,0:T(4,128)}, u32[]{:S(2)}, u32[]{:S(2)}) async-start(f32[32,4,2560]{2,1,0:T(4,128)} %reshape.168), calls=%async_computation.2 | async-start | bytes 2621440 | tf_op jit(solution)/shard_map/all_to_all | solution.py:581
  167.2 5.7 %down_partial.3 = f32[16,1,192,128]{3,2,1,0:T(8,128)} custom-call(s32[16]{0:T(128)} %fusion.22.source_ref, s32[16]{0:T(128)} %get-tuple-element.47.tenant_ref, f32[16,128,256]{2,1,0:T(8,128)} %copy-done.3, f32[16,128,256]{2,1,0:T(8,128)} %copy-done.3, f32[16,128,256]{2,1,0:T(8,128)} %copy-done.3, f32[16,128,256]{2,1,0:T(8,128)} %copy-done.3, ...), custom_call_target="tpu_custom_call" | custom-call | flops 2000000000 | bytes 7200000 | tf_op jit(solution)/shard_map/down_partial/pallas_call | solution.py:171
  174.5 2.1 collective-permute-done.6
  176.7 1.5 collective-permute-start.7
  178.3 3.1 collective-permute-start.4
  181.9 10.0 %collective-permute-done.7 = f32[4,1,192,128]{3,2,1,0:T(8,128)S(1)} collective-permute-done((f32[4,1,192,128]{3,2,1,0:T(8,128)S(1)}, f32[4,1,192,128]{3,2,1,0:T(8,128)S(1)}, u32[]{:S(2)}, u32[]{:S(2)}) %collective-permute-start.7) | collective-permute-done | bytes 393248 | tf_op jit(solution)/shard_map/ppermute | solution.py:50
  192.0 3.2 collective-permute-start.10
  196.9 16.8 %collective-permute-start.8 = (f32[1,192,128]{2,1,0:T(8,128)S(1)}, f32[1,192,128]{2,1,0:T(8,128)S(1)}, u32[]{:S(2)}, u32[]{:S(2)}) collective-permute-start(f32[1,192,128]{2,1,0:T(8,128)S(1)} %get-tuple-element.60), channel_id=1, source_target_pairs={{0,16},{2,18},{4,20},{6,22},{8,24},{10,26},{12,28},{14,30},{16,0},... | collective-permute-start | bytes 294920 | tf_op jit(solution)/shard_map/ppermute | solution.py:50
  213.7 4.9 %collective-permute-done.2 = f32[2,192,128]{2,1,0:T(8,128)S(1)} collective-permute-done((f32[2,192,128]{2,1,0:T(8,128)S(1)}, f32[2,192,128]{2,1,0:T(8,128)S(1)}, u32[]{:S(2)}, u32[]{:S(2)}) %collective-permute-start.2) | collective-permute-done | bytes 196640 | tf_op jit(solution)/shard_map/ppermute | solution.py:50
  220.0 3.9 %collective-permute-done.8 = f32[1,192,128]{2,1,0:T(8,128)S(1)} collective-permute-done((f32[1,192,128]{2,1,0:T(8,128)S(1)}, f32[1,192,128]{2,1,0:T(8,128)S(1)}, u32[]{:S(2)}, u32[]{:S(2)}) %collective-permute-start.8) | collective-permute-done | bytes 98336 | tf_op jit(solution)/shard_map/ppermute | solution.py:50
  223.9 4.6 %all-to-all-start.3 = ((f32[32,4,2560]{2,1,0:T(4,128)}), f32[32,4,2560]{2,1,0:T(4,128)S(1)}, u32[]{:S(2)}, u32[]{:S(2)}) async-start(f32[32,4,2560]{2,1,0:T(4,128)} %reshape.167), calls=%async_computation.3 | async-start | bytes 2621440 | tf_op jit(solution)/shard_map/all_to_all | solution.py:581
  232.9 2.2 collective-permute-done.11
  236.5 16.7 %attention_grads.4 = (f32[16,2,4,2560]{3,2,1,0:T(4,128)}, f32[3,192,128]{2,1,0:T(8,128)}) custom-call(bf16[384,4096]{1,0:T(8,128)(2,1)} %refs_0_.7, bf16[384,512]{1,0:T(8,128)(2,1)} %refs_1_.7, bf16[384,512]{1,0:T(8,128)(2,1)} %refs_2_.7, bf16[384,4096]{1,0:T(8,128)(2,1)} %refs_3_.7, f32[192,128]{1,0:T(8,128)} %get-tuple-element.64.refs_4_, ...), custom_call_target="tpu_custom_call" | custom-call | flops 20000000000 | bytes 72000000 | tf_op jit(solution)/shard_map/attention_grads/pallas_call | solution.py:328
  253.2 3.1 all-to-all-done.3
  257.3 7.7 %all-to-all-start.4 = ((f32[32,4,2560]{2,1,0:T(4,128)}), f32[32,4,2560]{2,1,0:T(4,128)S(1)}, u32[]{:S(2)}, u32[]{:S(2)}) async-start(f32[32,4,2560]{2,1,0:T(4,128)} %bitcast.68), calls=%async_computation.4 | async-start | bytes 2621440 | tf_op jit(solution)/shard_map/all_to_all | solution.py:581
  265.0 9.6 %attention_grads.5 = (f32[1,192,128]{2,1,0:T(8,128)}, f32[2,384,128]{2,1,0:T(8,128)}, f32[2,384,128]{2,1,0:T(8,128)}, f32[2,128,1280]{2,1,0:T(8,128)}) custom-call(bf16[384,4096]{1,0:T(8,128)(2,1)} %refs_0_.7, bf16[384,512]{1,0:T(8,128)(2,1)} %refs_1_.7, bf16[384,512]{1,0:T(8,128)(2,1)} %refs_2_.7, bf16[384,4096]{1,0:T(8,128)(2,1)} %refs_3_.7, ...), custom_call_target="tpu_custom_call" | custom-call | flops 10000000000 | bytes 36000000 | tf_op jit(solution)/shard_map/attention_grads/pallas_call | solution.py:328
  275.8 8.6 %attention_grads.6 = (f32[1,192,128]{2,1,0:T(8,128)}, f32[2,384,128]{2,1,0:T(8,128)}, f32[2,384,128]{2,1,0:T(8,128)}, f32[2,128,1280]{2,1,0:T(8,128)}) custom-call(bf16[384,4096]{1,0:T(8,128)(2,1)} %refs_0_.7, bf16[384,512]{1,0:T(8,128)(2,1)} %refs_1_.7, bf16[384,512]{1,0:T(8,128)(2,1)} %refs_2_.7, bf16[384,4096]{1,0:T(8,128)(2,1)} %refs_3_.7, ...), custom_call_target="tpu_custom_call" | custom-call | flops 6666666496 | bytes 24000000 | tf_op jit(solution)/shard_map/attention_grads/pallas_call | solution.py:328
  285.3 3.2 collective-permute-start.15
  288.9 1.6 constant_dynamic-update-slice_fusion.11
  290.5 2.0 collective-permute-start.22
  293.9 7.2 %attention_grads.7 = (f32[16,2,4,2560]{3,2,1,0:T(4,128)}, f32[1,192,128]{2,1,0:T(8,128)}) custom-call(bf16[384,4096]{1,0:T(8,128)(2,1)} %refs_0_.7, bf16[384,512]{1,0:T(8,128)(2,1)} %refs_1_.7, bf16[384,512]{1,0:T(8,128)(2,1)} %refs_2_.7, bf16[384,4096]{1,0:T(8,128)(2,1)} %refs_3_.7, f32[192,128]{1,0:T(8,128)} %get-tuple-element.64.refs_4_, ...), custom_call_target="tpu_custom_call" | custom-call | flops 3333333248 | bytes 11999999 | tf_op jit(solution)/shard_map/attention_grads/pallas_call | solution.py:328
  301.3 6.8 %collective-permute-done.13 = f32[1,192,128]{2,1,0:T(8,128)S(1)} collective-permute-done((f32[1,192,128]{2,1,0:T(8,128)S(1)}, f32[1,192,128]{2,1,0:T(8,128)S(1)}, u32[]{:S(2)}, u32[]{:S(2)}) %collective-permute-start.13) | collective-permute-done | bytes 98336 | tf_op jit(solution)/shard_map/ppermute | solution.py:50
  316.5 2.3 collective-permute-start.18
  319.0 2.0 collective-permute-start.20
  321.0 3.8 %collective-permute-done.25 = f32[4,192,128]{2,1,0:T(8,128)S(1)} collective-permute-done((f32[4,192,128]{2,1,0:T(8,128)S(1)}, f32[4,192,128]{2,1,0:T(8,128)S(1)}, u32[]{:S(2)}, u32[]{:S(2)}) %collective-permute-start.25) | collective-permute-done | bytes 393248 | tf_op jit(solution)/shard_map/ppermute | solution.py:50
  325.6 3.3 collective-permute-start.26
  332.4 4.4 %all-to-all-start.5 = ((f32[32,4,2560]{2,1,0:T(4,128)}), f32[32,4,2560]{2,1,0:T(4,128)S(1)}, u32[]{:S(2)}, u32[]{:S(2)}) async-start(f32[32,4,2560]{2,1,0:T(4,128)} %bitcast.64), calls=%async_computation.5 | async-start | bytes 2621440 | tf_op jit(solution)/shard_map/all_to_all | solution.py:581
  336.9 3.8 collective-permute-done.21
  340.7 12.9 %down_grad.1.refs_3_ = f32[64,192,256]{2,1,0:T(8,128)} custom-call(s32[32]{0:T(128)} %select_reduce_fusion.1.order_ref, s32[65]{0:T(128)} %convert_reduce_fusion.2.first_ref, s32[32]{0:T(128)} %copy-done.17, s32[16]{0:T(128)} %fusion.22.source_ref, f32[16,264,256]{2,1,0:T(8,128)} %all-to-all-done.refs_0_.refs_1_.refs_2_.refs_3_, f32[16,128,256]{2,1,0:T(8,128)} %copy-done.3, ...), custom_call_target="tpu_custom_call" | custom-call | flops 14000000000 | bytes 50400000 | tf_op jit(solution)/shard_map/down_grad/pallas_call | solution.py:441
  353.7 4.8 %collective-permute-start.29 = (f32[8,192,128]{2,1,0:T(8,128)S(1)}, f32[8,192,128]{2,1,0:T(8,128)S(1)}, u32[]{:S(2)}, u32[]{:S(2)}) collective-permute-start(f32[8,192,128]{2,1,0:T(8,128)S(1)} %constant_dynamic-update-slice_fusion.2.refs_1_), channel_id=1, source_target_pairs={{0,2},{2,0},{4,6},{6,4},{8,10},{10,8},{12,14},{14,12},{16,18},{18,... | collective-permute-start | bytes 2359304 | tf_op jit(solution)/shard_map/ppermute | solution.py:50
  361.8 6.3 %down_grad_last.1 = f32[64,192,256]{2,1,0:T(8,128)} custom-call(s32[16]{0:T(128)} %copy-done.15, s32[16]{0:T(128)} %select_reduce_fusion.2.leader_ref, s32[16]{0:T(128)} %fusion.22.source_ref, f32[16,264,256]{2,1,0:T(8,128)} %all-to-all-done.refs_0_.refs_1_.refs_2_.refs_3_, f32[8,192,128]{2,1,0:T(8,128)} %copy-done.10, ...), custom_call_target="tpu_custom_call", output_to_operand_aliasing={{}: (6, {})} | custom-call | flops 6000000000 | bytes 21600000 | tf_op jit(solution)/shard_map/down_grad_last/pallas_call | solution.py:502
  369.2 6.8 %up_grad.1 = (f32[64,4,4096]{2,1,0:T(4,128)}, f32[64,4,4,256]{3,2,1,0:T(4,128)}) custom-call(s32[32]{0:T(128)} %select_reduce_fusion.order_ref, s32[65]{0:T(128)} %convert_reduce_fusion.first_ref, f32[32,4,2560]{2,1,0:T(4,128)} %copy-done.7, f32[32,4,2560]{2,1,0:T(4,128)} %copy-done.9), custom_call_target="tpu_custom_call" | custom-call | flops 6000000000 | bytes 21600000 | tf_op jit(solution)/shard_map/up_grad/pallas_call | solution.py:558
  (145 shorter events, 40.4 us)
Async XLA Ops:
  0.6 20.9 %copy-start = (f32[64,4,4,256]{3,2,1,0:T(4,128)S(1)}, f32[64,4,4,256]{3,2,1,0:T(4,128)}, u32[]{:S(2)}) copy-start(f32[64,4,4,256]{3,2,1,0:T(4,128)} %param.18) | copy-start | bytes 3145732
  5.7 7.5 %copy-start.2 = (s32[16,2]{0,1:T(2,128)S(1)}, s32[16,2]{0,1:T(2,128)}, u32[]{:S(2)}) copy-start(s32[16,2]{0,1:T(2,128)} %param.21) | copy-start | bytes 388
  5.7 87.8 %all-to-all-start = ((f32[16,264,256]{2,1,0:T(8,128)}), f32[16,264,256]{2,1,0:T(8,128)}, u32[]{:S(2)}, u32[]{:S(2)}) async-start(f32[16,264,256]{2,1,0:T(8,128)} %rows_wire.2), calls=%async_computation | async-start | bytes 8650752 | tf_op jit(solution)/shard_map/all_to_all | solution.py:581
  93.5 65.8 %all-to-all-start.1 = ((f32[16,128,256]{2,1,0:T(8,128)}), f32[16,128,256]{2,1,0:T(8,128)S(1)}, u32[]{:S(2)}, u32[]{:S(2)}) async-start(f32[16,128,256]{2,1,0:T(8,128)} %rows_wire.3), calls=%async_computation.1 | async-start | bytes 4194304 | tf_op jit(solution)/shard_map/all_to_all | solution.py:581
  128.2 3.5 collective-permute-start
  131.9 27.3 %collective-permute-start.1 = (f32[4,2,192,128]{3,2,1,0:T(8,128)S(1)}, f32[4,2,192,128]{3,2,1,0:T(8,128)S(1)}, u32[]{:S(2)}, u32[]{:S(2)}) collective-permute-start(f32[4,2,192,128]{3,2,1,0:T(8,128)S(1)} %slice.114), channel_id=1, source_target_pairs={{0,4},{2,6},{4,0},{6,2},{8,12},{10,14},{12,8},{14,10},{16,20},{18,... | collective-permute-start | bytes 2359304 | tf_op jit(solution)/shard_map/ppermute | solution.py:50
  134.2 226.0 %copy-start.15 = (s32[16]{0:T(128)}, s32[16]{0:T(128)S(1)}, u32[]{:S(2)}) copy-start(s32[16]{0:T(128)S(1)} %get-tuple-element.48.owner_ref) | copy-start | bytes 196
  159.3 7.9 %copy-start.3 = (f32[16,128,256]{2,1,0:T(8,128)}, f32[16,128,256]{2,1,0:T(8,128)S(1)}, u32[]{:S(2)}) copy-start(f32[16,128,256]{2,1,0:T(8,128)S(1)} %all-to-all-done.1.refs_0_.refs_1_.refs_2_.refs_3_) | copy-start | bytes 6291460
  159.3 64.6 %all-to-all-start.2 = ((f32[32,4,2560]{2,1,0:T(4,128)}), f32[32,4,2560]{2,1,0:T(4,128)}, u32[]{:S(2)}, u32[]{:S(2)}) async-start(f32[32,4,2560]{2,1,0:T(4,128)} %reshape.168), calls=%async_computation.2 | async-start | bytes 2621440 | tf_op jit(solution)/shard_map/all_to_all | solution.py:581
  174.2 2.4 collective-permute-start.6
  176.7 15.2 %collective-permute-start.7 = (f32[4,1,192,128]{3,2,1,0:T(8,128)S(1)}, f32[4,1,192,128]{3,2,1,0:T(8,128)S(1)}, u32[]{:S(2)}, u32[]{:S(2)}) collective-permute-start(f32[4,1,192,128]{3,2,1,0:T(8,128)S(1)} %slice.126), channel_id=1, source_target_pairs={{0,4},{2,6},{4,0},{6,2},{8,12},{10,14},{12,8},{14,10},{16,20},{18,... | collective-permute-start | bytes 1179656 | tf_op jit(solution)/shard_map/ppermute | solution.py:50
  178.3 18.6 %collective-permute-start.4 = (f32[2,192,128]{2,1,0:T(8,128)S(1)}, f32[2,192,128]{2,1,0:T(8,128)S(1)}, u32[]{:S(2)}, u32[]{:S(2)}) collective-permute-start(f32[2,192,128]{2,1,0:T(8,128)S(1)} %get-tuple-element.58), channel_id=1, source_target_pairs={{0,24},{2,26},{4,28},{6,30},{8,16},{10,18},{12,20},{14,22},{16,8},... | collective-permute-start | bytes 589832 | tf_op jit(solution)/shard_map/ppermute | solution.py:50
  181.3 32.4 %collective-permute-start.3 = (f32[2,192,128]{2,1,0:T(8,128)S(1)}, f32[2,192,128]{2,1,0:T(8,128)S(1)}, u32[]{:S(2)}, u32[]{:S(2)}) collective-permute-start(f32[2,192,128]{2,1,0:T(8,128)S(1)} %get-tuple-element.59), channel_id=1, source_target_pairs={{0,8},{2,10},{4,12},{6,14},{8,0},{10,2},{12,4},{14,6},{16,24},{18,... | collective-permute-start | bytes 589832 | tf_op jit(solution)/shard_map/ppermute | solution.py:50
  181.3 37.3 %collective-permute-start.2 = (f32[2,192,128]{2,1,0:T(8,128)S(1)}, f32[2,192,128]{2,1,0:T(8,128)S(1)}, u32[]{:S(2)}, u32[]{:S(2)}) collective-permute-start(f32[2,192,128]{2,1,0:T(8,128)S(1)} %get-tuple-element.57), channel_id=1, source_target_pairs={{0,16},{2,18},{4,20},{6,22},{8,24},{10,26},{12,28},{14,30},{16,0},... | collective-permute-start | bytes 589832 | tf_op jit(solution)/shard_map/ppermute | solution.py:50
  192.0 36.5 %copy-start.16 = (s32[3]{0:T(128)S(1)}, s32[3]{0:T(128)}, u32[]{:S(2)}) copy-start(s32[3]{0:T(128)} %slot_ref.3) | copy-start | bytes 40
  192.0 36.6 %copy-start.14 = (s32[384]{0:T(512)S(1)}, s32[384]{0:T(512)}, u32[]{:S(2)}) copy-start(s32[384]{0:T(512)} %param.19) | copy-start | bytes 4612
  192.0 28.0 %collective-permute-start.10 = (f32[1,192,128]{2,1,0:T(8,128)S(1)}, f32[1,192,128]{2,1,0:T(8,128)S(1)}, u32[]{:S(2)}, u32[]{:S(2)}) collective-permute-start(f32[1,192,128]{2,1,0:T(8,128)S(1)} %get-tuple-element.61), channel_id=1, source_target_pairs={{0,24},{2,26},{4,28},{6,30},{8,16},{10,18},{12,20},{14,22},{16,8},... | collective-permute-start | bytes 294920 | tf_op jit(solution)/shard_map/ppermute | solution.py:50
  195.2 24.8 %collective-permute-start.9 = (f32[1,192,128]{2,1,0:T(8,128)S(1)}, f32[1,192,128]{2,1,0:T(8,128)S(1)}, u32[]{:S(2)}, u32[]{:S(2)}) collective-permute-start(f32[1,192,128]{2,1,0:T(8,128)S(1)} %get-tuple-element.62), channel_id=1, source_target_pairs={{0,8},{2,10},{4,12},{6,14},{8,0},{10,2},{12,4},{14,6},{16,24},{18,... | collective-permute-start | bytes 294920 | tf_op jit(solution)/shard_map/ppermute | solution.py:50
  196.9 27.0 %collective-permute-start.8 = (f32[1,192,128]{2,1,0:T(8,128)S(1)}, f32[1,192,128]{2,1,0:T(8,128)S(1)}, u32[]{:S(2)}, u32[]{:S(2)}) collective-permute-start(f32[1,192,128]{2,1,0:T(8,128)S(1)} %get-tuple-element.60), channel_id=1, source_target_pairs={{0,16},{2,18},{4,20},{6,22},{8,24},{10,26},{12,28},{14,30},{16,0},... | collective-permute-start | bytes 294920 | tf_op jit(solution)/shard_map/ppermute | solution.py:50
  218.7 12.2 %collective-permute-start.5 = (f32[2,192,128]{2,1,0:T(8,128)S(1)}, f32[2,192,128]{2,1,0:T(8,128)S(1)}, u32[]{:S(2)}, u32[]{:S(2)}) collective-permute-start(f32[2,192,128]{2,1,0:T(8,128)S(1)} %fusion.2), channel_id=1, source_target_pairs={{0,1},{1,0},{2,3},{3,2},{4,5},{5,4},{6,7},{7,6},{8,9},{9,8},{10,11... | collective-permute-start | bytes 589832 | tf_op jit(solution)/shard_map/ppermute | solution.py:50
  223.9 32.3 %all-to-all-start.3 = ((f32[32,4,2560]{2,1,0:T(4,128)}), f32[32,4,2560]{2,1,0:T(4,128)S(1)}, u32[]{:S(2)}, u32[]{:S(2)}) async-start(f32[32,4,2560]{2,1,0:T(4,128)} %reshape.167), calls=%async_computation.3 | async-start | bytes 2621440 | tf_op jit(solution)/shard_map/all_to_all | solution.py:581
  230.7 99.1 %copy-start.17 = (s32[32]{0:T(128)}, s32[32]{0:T(128)S(1)}, u32[]{:S(2)}) copy-start(s32[32]{0:T(128)S(1)} %lt.135.owner_ref) | copy-start | bytes 388
  230.9 4.2 %collective-permute-start.11 = (f32[1,192,128]{2,1,0:T(8,128)S(1)}, f32[1,192,128]{2,1,0:T(8,128)S(1)}, u32[]{:S(2)}, u32[]{:S(2)}) collective-permute-start(f32[1,192,128]{2,1,0:T(8,128)S(1)} %fusion.5), channel_id=1, source_target_pairs={{0,1},{1,0},{2,3},{3,2},{4,5},{5,4},{6,7},{7,6},{8,9},{9,8},{10,11... | collective-permute-start | bytes 294920 | tf_op jit(solution)/shard_map/ppermute | solution.py:50
  257.3 52.1 %all-to-all-start.4 = ((f32[32,4,2560]{2,1,0:T(4,128)}), f32[32,4,2560]{2,1,0:T(4,128)S(1)}, u32[]{:S(2)}, u32[]{:S(2)}) async-start(f32[32,4,2560]{2,1,0:T(4,128)} %bitcast.68), calls=%async_computation.4 | async-start | bytes 2621440 | tf_op jit(solution)/shard_map/all_to_all | solution.py:581
  274.6 10.1 %collective-permute-start.12 = (f32[1,192,128]{2,1,0:T(8,128)}, f32[1,192,128]{2,1,0:T(8,128)S(1)}, u32[]{:S(2)}, u32[]{:S(2)}) collective-permute-start(f32[1,192,128]{2,1,0:T(8,128)} %get-tuple-element.35), channel_id=1, source_target_pairs={{0,1},{1,0},{2,3},{3,2},{4,5},{5,4},{6,7},{7,6},{8,9},{9,8},{10,11... | collective-permute-start | bytes 294920 | tf_op jit(solution)/shard_map/ppermute | solution.py:50
  275.8 8.9 %copy-start.13 = (f32[1,192,128]{2,1,0:T(8,128)S(1)}, f32[1,192,128]{2,1,0:T(8,128)}, u32[]{:S(2)}) copy-start(f32[1,192,128]{2,1,0:T(8,128)} %get-tuple-element.35) | copy-start | bytes 294916
  284.4 4.5 %collective-permute-start.16 = (f32[1,192,128]{2,1,0:T(8,128)}, f32[1,192,128]{2,1,0:T(8,128)S(1)}, u32[]{:S(2)}, u32[]{:S(2)}) collective-permute-start(f32[1,192,128]{2,1,0:T(8,128)} %get-tuple-element.41), channel_id=1, source_target_pairs={{0,1},{1,0},{2,3},{3,2},{4,5},{5,4},{6,7},{7,6},{8,9},{9,8},{10,11... | collective-permute-start | bytes 294920 | tf_op jit(solution)/shard_map/ppermute | solution.py:50
  285.3 15.8 %collective-permute-start.15 = (f32[1,192,128]{2,1,0:T(8,128)S(1)}, f32[1,192,128]{2,1,0:T(8,128)S(1)}, u32[]{:S(2)}, u32[]{:S(2)}) collective-permute-start(f32[1,192,128]{2,1,0:T(8,128)S(1)} %get-tuple-element.50), channel_id=1, source_target_pairs={{0,24},{2,26},{4,28},{6,30},{8,16},{10,18},{12,20},{14,22},{16,8},... | collective-permute-start | bytes 294920 | tf_op jit(solution)/shard_map/ppermute | solution.py:50
  288.5 12.8 %collective-permute-start.14 = (f32[1,192,128]{2,1,0:T(8,128)S(1)}, f32[1,192,128]{2,1,0:T(8,128)S(1)}, u32[]{:S(2)}, u32[]{:S(2)}) collective-permute-start(f32[1,192,128]{2,1,0:T(8,128)S(1)} %get-tuple-element.50), channel_id=1, source_target_pairs={{0,8},{2,10},{4,12},{6,14},{8,0},{10,2},{12,4},{14,6},{16,24},{18,... | collective-permute-start | bytes 294920 | tf_op jit(solution)/shard_map/ppermute | solution.py:50
  288.5 19.5 %collective-permute-start.13 = (f32[1,192,128]{2,1,0:T(8,128)S(1)}, f32[1,192,128]{2,1,0:T(8,128)S(1)}, u32[]{:S(2)}, u32[]{:S(2)}) collective-permute-start(f32[1,192,128]{2,1,0:T(8,128)S(1)} %get-tuple-element.50), channel_id=1, source_target_pairs={{0,16},{2,18},{4,20},{6,22},{8,24},{10,26},{12,28},{14,30},{16,0},... | collective-permute-start | bytes 294920 | tf_op jit(solution)/shard_map/ppermute | solution.py:50
  290.5 20.8 %collective-permute-start.22 = (f32[1,192,128]{2,1,0:T(8,128)S(1)}, f32[1,192,128]{2,1,0:T(8,128)S(1)}, u32[]{:S(2)}, u32[]{:S(2)}) collective-permute-start(f32[1,192,128]{2,1,0:T(8,128)S(1)} %get-tuple-element.52), channel_id=1, source_target_pairs={{0,16},{2,18},{4,20},{6,22},{8,24},{10,26},{12,28},{14,30},{16,0},... | collective-permute-start | bytes 294920 | tf_op jit(solution)/shard_map/ppermute | solution.py:50
  292.5 18.8 %collective-permute-start.23 = (f32[1,192,128]{2,1,0:T(8,128)S(1)}, f32[1,192,128]{2,1,0:T(8,128)S(1)}, u32[]{:S(2)}, u32[]{:S(2)}) collective-permute-start(f32[1,192,128]{2,1,0:T(8,128)S(1)} %get-tuple-element.52), channel_id=1, source_target_pairs={{0,8},{2,10},{4,12},{6,14},{8,0},{10,2},{12,4},{14,6},{16,24},{18,... | collective-permute-start | bytes 294920 | tf_op jit(solution)/shard_map/ppermute | solution.py:50
  301.1 15.3 %copy-start.12 = (f32[1,192,128]{2,1,0:T(8,128)S(1)}, f32[1,192,128]{2,1,0:T(8,128)}, u32[]{:S(2)}) copy-start(f32[1,192,128]{2,1,0:T(8,128)} %get-tuple-element.42) | copy-start | bytes 294916
  301.1 10.1 %collective-permute-start.24 = (f32[1,192,128]{2,1,0:T(8,128)S(1)}, f32[1,192,128]{2,1,0:T(8,128)S(1)}, u32[]{:S(2)}, u32[]{:S(2)}) collective-permute-start(f32[1,192,128]{2,1,0:T(8,128)S(1)} %get-tuple-element.52), channel_id=1, source_target_pairs={{0,24},{2,26},{4,28},{6,30},{8,16},{10,18},{12,20},{14,22},{16,8},... | collective-permute-start | bytes 294920 | tf_op jit(solution)/shard_map/ppermute | solution.py:50
  308.1 20.8 %collective-permute-start.27 = (f32[4,192,128]{2,1,0:T(8,128)S(1)}, f32[4,192,128]{2,1,0:T(8,128)S(1)}, u32[]{:S(2)}, u32[]{:S(2)}) collective-permute-start(f32[4,192,128]{2,1,0:T(8,128)S(1)} %pad_maximum_fusion), channel_id=1, source_target_pairs={{0,4},{2,6},{4,0},{6,2},{8,12},{10,14},{12,8},{14,10},{16,20},{18,... | collective-permute-start | bytes 1179656 | tf_op jit(solution)/shard_map/ppermute | solution.py:50
  309.4 21.0 %copy-start.7 = (f32[32,4,2560]{2,1,0:T(4,128)}, f32[32,4,2560]{2,1,0:T(4,128)S(1)}, u32[]{:S(2)}) copy-start(f32[32,4,2560]{2,1,0:T(4,128)S(1)} %all-to-all-done.4.refs_0_) | copy-start | bytes 3932164
  309.4 7.1 %collective-permute-start.17 = (f32[1,192,128]{2,1,0:T(8,128)}, f32[1,192,128]{2,1,0:T(8,128)S(1)}, u32[]{:S(2)}, u32[]{:S(2)}) collective-permute-start(f32[1,192,128]{2,1,0:T(8,128)} %get-tuple-element.42), channel_id=1, source_target_pairs={{0,1},{1,0},{2,3},{3,2},{4,5},{5,4},{6,7},{7,6},{8,9},{9,8},{10,11... | collective-permute-start | bytes 294920 | tf_op jit(solution)/shard_map/ppermute | solution.py:50
  311.3 13.5 %collective-permute-start.25 = (f32[4,192,128]{2,1,0:T(8,128)S(1)}, f32[4,192,128]{2,1,0:T(8,128)S(1)}, u32[]{:S(2)}, u32[]{:S(2)}) collective-permute-start(f32[4,192,128]{2,1,0:T(8,128)S(1)} %pad_maximum_fusion.2), channel_id=1, source_target_pairs={{0,4},{2,6},{4,0},{6,2},{8,12},{10,14},{12,8},{14,10},{16,20},{18,... | collective-permute-start | bytes 1179656 | tf_op jit(solution)/shard_map/ppermute | solution.py:50
  316.5 13.9 %collective-permute-start.18 = (f32[1,192,128]{2,1,0:T(8,128)S(1)}, f32[1,192,128]{2,1,0:T(8,128)S(1)}, u32[]{:S(2)}, u32[]{:S(2)}) collective-permute-start(f32[1,192,128]{2,1,0:T(8,128)S(1)} %get-tuple-element.54), channel_id=1, source_target_pairs={{0,16},{2,18},{4,20},{6,22},{8,24},{10,26},{12,28},{14,30},{16,0},... | collective-permute-start | bytes 294920 | tf_op jit(solution)/shard_map/ppermute | solution.py:50
  318.8 11.6 %collective-permute-start.19 = (f32[1,192,128]{2,1,0:T(8,128)S(1)}, f32[1,192,128]{2,1,0:T(8,128)S(1)}, u32[]{:S(2)}, u32[]{:S(2)}) collective-permute-start(f32[1,192,128]{2,1,0:T(8,128)S(1)} %get-tuple-element.54), channel_id=1, source_target_pairs={{0,8},{2,10},{4,12},{6,14},{8,0},{10,2},{12,4},{14,6},{16,24},{18,... | collective-permute-start | bytes 294920 | tf_op jit(solution)/shard_map/ppermute | solution.py:50
  319.0 11.4 %collective-permute-start.20 = (f32[1,192,128]{2,1,0:T(8,128)S(1)}, f32[1,192,128]{2,1,0:T(8,128)S(1)}, u32[]{:S(2)}, u32[]{:S(2)}) collective-permute-start(f32[1,192,128]{2,1,0:T(8,128)S(1)} %get-tuple-element.54), channel_id=1, source_target_pairs={{0,24},{2,26},{4,28},{6,30},{8,16},{10,18},{12,20},{14,22},{16,8},... | collective-permute-start | bytes 294920 | tf_op jit(solution)/shard_map/ppermute | solution.py:50
  325.6 15.1 %collective-permute-start.26 = (f32[8,192,128]{2,1,0:T(8,128)}, f32[8,192,128]{2,1,0:T(8,128)}, u32[]{:S(2)}, u32[]{:S(2)}) collective-permute-start(f32[8,192,128]{2,1,0:T(8,128)} %constant_dynamic-update-slice_fusion.7.refs_2_), channel_id=1, source_target_pairs={{0,2},{2,0},{4,6},{6,4},{8,10},{10,8},{12,14},{14,12},{16,18},{18,... | collective-permute-start | bytes 2359304 | tf_op jit(solution)/shard_map/ppermute | solution.py:50
  329.7 11.0 %collective-permute-start.28 = (f32[8,192,128]{2,1,0:T(8,128)}, f32[8,192,128]{2,1,0:T(8,128)}, u32[]{:S(2)}, u32[]{:S(2)}) collective-permute-start(f32[8,192,128]{2,1,0:T(8,128)} %constant_dynamic-update-slice_fusion.12.refs_4_), channel_id=1, source_target_pairs={{0,2},{2,0},{4,6},{6,4},{8,10},{10,8},{12,14},{14,12},{16,18},{18,... | collective-permute-start | bytes 2359304 | tf_op jit(solution)/shard_map/ppermute | solution.py:50
  330.4 10.2 %collective-permute-start.21 = (f32[4,192,128]{2,1,0:T(8,128)S(1)}, f32[4,192,128]{2,1,0:T(8,128)S(1)}, u32[]{:S(2)}, u32[]{:S(2)}) collective-permute-start(f32[4,192,128]{2,1,0:T(8,128)S(1)} %pad_maximum_fusion.1), channel_id=1, source_target_pairs={{0,4},{2,6},{4,0},{6,2},{8,12},{10,14},{12,8},{14,10},{16,20},{18,... | collective-permute-start | bytes 1179656 | tf_op jit(solution)/shard_map/ppermute | solution.py:50
  332.4 35.7 %all-to-all-start.5 = ((f32[32,4,2560]{2,1,0:T(4,128)}), f32[32,4,2560]{2,1,0:T(4,128)S(1)}, u32[]{:S(2)}, u32[]{:S(2)}) async-start(f32[32,4,2560]{2,1,0:T(4,128)} %bitcast.64), calls=%async_computation.5 | async-start | bytes 2621440 | tf_op jit(solution)/shard_map/all_to_all | solution.py:581
  340.7 13.0 %copy-start.10 = (f32[8,192,128]{2,1,0:T(8,128)}, f32[8,192,128]{2,1,0:T(8,128)S(1)}, u32[]{:S(2)}) copy-start(f32[8,192,128]{2,1,0:T(8,128)S(1)} %constant_dynamic-update-slice_fusion.2.refs_1_) | copy-start | bytes 2359300
  353.7 7.2 %collective-permute-start.29 = (f32[8,192,128]{2,1,0:T(8,128)S(1)}, f32[8,192,128]{2,1,0:T(8,128)S(1)}, u32[]{:S(2)}, u32[]{:S(2)}) collective-permute-start(f32[8,192,128]{2,1,0:T(8,128)S(1)} %constant_dynamic-update-slice_fusion.2.refs_1_), channel_id=1, source_target_pairs={{0,2},{2,0},{4,6},{6,4},{8,10},{10,8},{12,14},{14,12},{16,18},{18,... | collective-permute-start | bytes 2359304 | tf_op jit(solution)/shard_map/ppermute | solution.py:50
  369.2 6.8 %copy-start.1 = (f32[64,4,4,256]{3,2,1,0:T(4,128)S(1)}, f32[64,4,4,256]{3,2,1,0:T(4,128)}, u32[]{:S(2)}) copy-start(f32[64,4,4,256]{3,2,1,0:T(4,128)} %param.18) | copy-start | bytes 3145732
  (6 other events, 12.9 us)
